TPU v7x, 32 devices: a whole 2x2x4 slice. The times are simulated.
32 devices in a mesh: groups: 2 (over x), gx: 16 (over z, y, core).
Axes of the slice: x: 2, y: 2, z: 4, core: 2. Of those that a mesh axis runs over, the one named last changes fastest.
Arguments:
- tokens: bfloat16 [1024, 16384], P('groups', 'gx'), parts along dimension 0, as said below
- gain: float32 [16384], P('gx'), may hold values from 0.1 to 1.9
- gate_weight: bfloat16 [16384, 1664], P(None, 'gx'), may hold values from -0.046875 to 0.046875
- up_weight: bfloat16 [16384, 1664], P(None, 'gx'), may hold values from -0.046875 to 0.046875
- down_weight: bfloat16 [1664, 16384], P('gx'), may hold values from -0.21875 to 0.21875
Outputs:
- mixed: bfloat16 [1024, 16384], P('groups', 'gx'), parts along dimension 0
There are 2 independent parts, one for each index of `groups`. A program takes and returns all parts, laid end to end along the dimension named above; an argument that names none is the same for every part. Nothing has to cross between parts.
Inputs may be any that keep to these rules, and one draw needn't show every extreme that they name: `tokens`: activations of one span.
All inputs are finite; a program needn't handle non-finite values.
Results may differ from a plain program's by a relative error of at most 0.02.
Values may be sent and summed in bfloat16 or wider, within the bound.
No kernel may reach another device: no remote copies, remote signals or barrier semaphores. Data moves between devices by JAX's collectives and lax.ppermute only.
A program may use at most 128 MiB of HBM per device.

v0:
```python
import jax
import jax.numpy as jnp
from jax import lax
from jax.sharding import PartitionSpec as P

D = 16384


def body(tokens, gain, gate_weight, up_weight, down_weight):
    values = tokens.astype(jnp.float32)
    total = lax.psum(jnp.sum(values * values, axis=1), "gx")
    scaled = (values * gain[None, :]).astype(jnp.bfloat16)
    piece = lax.all_gather(scaled, "gx", axis=1, tiled=True)
    gate_sum = jnp.dot(piece, gate_weight, preferred_element_type=jnp.float32)
    up_sum = jnp.dot(piece, up_weight, preferred_element_type=jnp.float32)
    inverse = lax.rsqrt(total / D + 1e-05)[:, None]
    hidden = (jax.nn.silu(gate_sum * inverse) * (up_sum * inverse)).astype(jnp.bfloat16)
    columns = lax.all_to_all(down_weight, "gx", split_axis=1, concat_axis=0, tiled=True)
    mixed = jnp.dot(
        lax.all_gather(hidden, "gx", axis=1, tiled=True),
        columns,
        preferred_element_type=jnp.float32,
    )
    return mixed.astype(jnp.bfloat16)


def solution(mesh):
    in_specs = (P("groups", "gx"), P("gx"), P(None, "gx"), P(None, "gx"), P("gx", None))
    out_specs = P("groups", "gx")
    return jax.shard_map(body, mesh=mesh, in_specs=in_specs, out_specs=out_specs, check_vma=False)
```

profile of v0, /device:TPU:1, one launch (start us, length us, event | category | flops | bytes accessed | tf_op | source)
XLA Modules:
  0.0 271.0 jit_solution(9703563730943213642)
XLA Ops:
  6.5 0.0 copy-start
  6.5 0.0 all-gather.3.cloned.1.call-start
  6.5 2.6 fusion.1
  9.2 0.0 all-gather.3.cloned.1.call-update
  9.2 4.1 %copy.10 = bf16[13,16,8,1024]{3,2,0,1:T(8,128)(2,1)} copy(bf16[13,16,8,1024]{3,2,1,0:T(8,128)(2,1)} %bitcast.14) | data formatting | bytes 6815744 | tf_op jit(solution)/shard_map/all_to_all | solution.py:18
  13.3 7.3 %all-to-all-start = ((bf16[104,16,1024]{2,0,1:T(8,128)(2,1)}), bf16[104,16,1024]{2,0,1:T(8,128)(2,1)}, u32[]{:S(2)}, u32[]{:S(2)}) async-start(bf16[104,16,1024]{2,0,1:T(8,128)(2,1)} %bitcast.13), calls=%async_computation | async-start | bytes 6815744 | tf_op jit(solution)/shard_map/all_to_all | solution.py:18
  20.7 0.0 all-gather.5.cloned.1.call-start
  20.7 156.6 %psum.7 = f32[512]{0:T(512)S(1)} all-reduce(f32[512]{0:T(512)S(1)} %get-tuple-element.5), channel_id=1, replica_groups=mesh['groups'=2,'gx'=16] {'gx'}, use_global_device_ids=true, to_apply=%region_1.0 | all-reduce | flops 512 | bytes 4096 | tf_op jit(solution)/shard_map/psum | solution.py:11
  177.3 24.4 %all-gather.3.cloned.1.call-done = bf16[512,16384]{1,0:T(8,128)(2,1)} async-done(((bf16[512,1024]{1,0:T(8,128)(2,1)}), bf16[512,16384]{1,0:T(8,128)(2,1)}) %all-gather.3.cloned.1.call-update) | async-done | bytes 16777232 | tf_op jit(solution)/shard_map/all_gather | solution.py:13
  201.7 0.0 copy-done
  201.7 0.0 copy-start.1
  201.7 0.0 copy-start.2
  201.7 11.2 %convolution_multiply_fusion.1 = f32[512,104]{0,1:T(8,128)S(1)} fusion(bf16[512,16384]{1,0:T(8,128)(2,1)} %all-gather.3.cloned.1.call-done, bf16[16384,104]{0,1:T(8,128)(2,1)S(1)} %copy-done, f32[512]{0:T(512)S(1)} %add_rsqrt_fusion), kind=kOutput, calls=%fused_computation.8 | convolution fusion | flops 1744883712 | bytes 20400128 | tf_op jit(solution)/shard_map/dot_general | solution.py:14
  213.0 0.0 copy-done.1
  213.0 0.3 copy-done.2
  213.2 6.0 %fusion.3 = bf16[512,104]{0,1:T(8,128)(2,1)} fusion(bf16[512,16384]{1,0:T(8,128)(2,1)S(1)} %copy-done.1, bf16[16384,104]{0,1:T(8,128)(2,1)S(1)} %copy-done.2, f32[512,104]{0,1:T(8,128)S(1)} %convolution_multiply_fusion.1, f32[512]{0:T(512)S(1)} %add_rsqrt_fusion), kind=kOutput, calls=%fused_computation.9 | convolution fusion | flops 1745203200 | bytes 20506624 | tf_op jit(solution)/shard_map/dot_general | solution.py:15
  219.2 0.0 all-gather.5.cloned.1.call-update
  219.2 0.0 all-to-all-done
  219.2 39.4 %all-gather.5.cloned.1.call-done = bf16[512,1664]{0,1:T(8,128)(2,1)} async-done(((bf16[512,104]{0,1:T(8,128)(2,1)}), bf16[512,1664]{0,1:T(8,128)(2,1)}) %all-gather.5.cloned.1.call-update) | async-done | bytes 1703952 | tf_op jit(solution)/shard_map/all_gather | solution.py:20
  258.6 5.5 %convolution_convert_fusion = bf16[512,1024]{1,0:T(8,128)(2,1)} fusion(bf16[512,1664]{0,1:T(8,128)(2,1)} %all-gather.5.cloned.1.call-done, bf16[1664,1024]{1,0:T(8,128)(2,1)} %bitcast.1), kind=kOutput, calls=%fused_computation.5 | convolution fusion | flops 1745354752 | bytes 6160384 | tf_op jit(solution)/shard_map/dot_general | solution.py:19
  (1 shorter events, 0.0 us)
Async XLA Ops:
  6.5 195.2 %copy-start = (bf16[16384,104]{0,1:T(8,128)(2,1)S(1)}, bf16[16384,104]{0,1:T(8,128)(2,1)}, u32[]{:S(2)}) copy-start(bf16[16384,104]{0,1:T(8,128)(2,1)} %param.7) | copy-start | bytes 10223620
  6.5 195.2 %all-gather.3.cloned.1.call-start = ((), (), s32[]{:S(2)}) async-start(), calls=%async_computation.1 | async-start | bytes 17825792 | tf_op jit(solution)/shard_map/all_gather | solution.py:13
  13.3 205.9 %all-to-all-start = ((bf16[104,16,1024]{2,0,1:T(8,128)(2,1)}), bf16[104,16,1024]{2,0,1:T(8,128)(2,1)}, u32[]{:S(2)}, u32[]{:S(2)}) async-start(bf16[104,16,1024]{2,0,1:T(8,128)(2,1)} %bitcast.13), calls=%async_computation | async-start | bytes 6815744 | tf_op jit(solution)/shard_map/all_to_all | solution.py:18
  20.7 237.9 %all-gather.5.cloned.1.call-start = ((), (), s32[]{:S(2)}) async-start(), calls=%async_computation.2 | async-start | bytes 1810432 | tf_op jit(solution)/shard_map/all_gather | solution.py:20
  201.7 11.2 %copy-start.1 = (bf16[512,16384]{1,0:T(8,128)(2,1)S(1)}, bf16[512,16384]{1,0:T(8,128)(2,1)}, u32[]{:S(2)}) copy-start(bf16[512,16384]{1,0:T(8,128)(2,1)} %all-gather.3.cloned.1.call-done) | copy-start | bytes 50331652
  201.7 11.5 %copy-start.2 = (bf16[16384,104]{0,1:T(8,128)(2,1)S(1)}, bf16[16384,104]{0,1:T(8,128)(2,1)}, u32[]{:S(2)}) copy-start(bf16[16384,104]{0,1:T(8,128)(2,1)} %param.8) | copy-start | bytes 10223620
Sparse Core Ops, SparseCore 0:
  9.5 192.1 all-gather.2
  219.4 39.1 all-gather.4
where the time goes:
time: 271 us
  blocking collectives  157 us (58%)
  waiting for transfers between devices  63.8 us (24%)
  matrix products  22.7 us (8%)
  between operations  13.4 us (5%)
  starting transfers between devices  7.39 us (3%)
  local copies, waits for them, and re-layouts  4.36 us (2%)
    psum x1, blocking collectives, body(): total = lax.psum(jnp.sum(values * values, axis=1), 'gx')  157 us
    all_gather x1, waiting for transfers between devices, body(): lax.all_gather(hidden, 'gx', axis=1, tiled=True)  39.4 us
    all_gather x1, waiting for transfers between devices, body(): piece = lax.all_gather(scaled, 'gx', axis=1, tiled=True)  24.4 us
    dot_general x1, matrix products, body(): gate_sum = jnp.dot(piece, gate_weight, preferred_element_type=jnp.float32)  11.2 us
    all_to_all x1, starting transfers between devices, body(): lax.all_to_all(down_weight, 'gx', split_axis=1, concat_axis=0, tiled=True)  7.35 us
    dot_general x1, matrix products, body(): up_sum = jnp.dot(piece, up_weight, preferred_element_type=jnp.float32)  5.96 us
    dot_general x1, matrix products, body(): jnp.dot(lax.all_gather(hidden, 'gx', axis=1, tiled=True), columns, prefer...  5.53 us
  transfers between devices with their start and end apart: 3, of which 2 were waited for; matrix products, arithmetic and copies ran while one was open for 8% of the time, Pallas kernels for 0%

commit v1 on v0

v1 whole, which is shorter than its diff:
```python
import jax
import jax.numpy as jnp
from jax import lax
from jax.sharding import PartitionSpec as P

D = 16384
CHUNKS = 2
BF = jnp.bfloat16
F32 = jnp.float32


def make_body(n, groups):
    planes = n // 4

    def at(p, q):
        return (p % planes) * 4 + q

    def flip(d):
        return [(at(p, q), at(p, q ^ d)) for p in range(planes) for q in range(4)]

    def shift(k, d=0):
        return [(at(p, q), at(p + k, q ^ d)) for p in range(planes) for q in range(4)]

    def body(tokens, gain, gate_weight, up_weight, down_weight):
        me = lax.axis_index("gx")
        plane, quad = me // 4, me % 4
        group = lax.axis_index("groups")
        rows, width = tokens.shape
        hid = gate_weight.shape[1]
        part = width // groups

        values = tokens.astype(F32)
        squares = jnp.sum(values * values, axis=1)
        scaled = (values * gain[None, :]).astype(BF)
        total = jnp.sum(lax.all_gather(squares, "gx"), axis=0)

        both = [w.T.reshape(hid, planes, 4, width) for w in (gate_weight, up_weight)]

        def features(d):
            return jnp.stack(
                [
                    jnp.concatenate(
                        [
                            lax.dynamic_slice(w, (0, (plane + planes - s) % planes, quad ^ d, 0), (hid, 1, 1, width)).reshape(hid, width)
                            for w in both
                        ],
                        axis=0,
                    )
                    for s in range(planes)
                ]
            )

        weights = [features(0)] + [lax.ppermute(features(d), "gx", flip(d)) for d in (1, 2, 3)]

        step = rows // CHUNKS
        current = [scaled[t * step : (t + 1) * step] for t in range(CHUNKS)]
        sums = [[None] * 4 for _ in range(CHUNKS)]
        for s in range(planes):
            for t in range(CHUNKS):
                if s:
                    current[t] = lax.ppermute(current[t], "gx", shift(1))
                for d in range(4):
                    term = lax.dot_general(weights[d][s], current[t], (((1,), (1,)), ((), ())), preferred_element_type=F32)
                    sums[t][d] = term if s == 0 else sums[t][d] + term

        down = down_weight.reshape(hid, planes, 2, 2, groups, part)
        y, c = quad // 2, quad % 2

        def columns(other):
            taken = lax.dynamic_slice(down, (0, 0, 0, c ^ other, group, 0), (hid, planes, 2, 1, 1, part))
            return taken.reshape(hid, planes, 2, part).transpose(1, 2, 0, 3)

        pair = jnp.stack([columns(0), lax.ppermute(columns(1), "gx", flip(1))], axis=2)

        def side(other):
            return lax.dynamic_slice(pair, (0, y ^ other, 0, 0, 0), (planes, 1, 2, hid, part)).reshape(planes, 2, hid, part)

        four = jnp.stack([side(0), lax.ppermute(side(1), "gx", flip(2))], axis=1)
        held = []
        for k in range(planes):
            block = lax.dynamic_index_in_dim(four, (plane + planes - k) % planes, 0, keepdims=False)
            held.append(lax.ppermute(block, "gx", shift(-k)) if k else block)
        held = jnp.stack(held)
        pieces = [held] + [
            lax.ppermute(held, "groups", [((g + r) % groups, g) for g in range(groups)]) for r in range(1, groups)
        ]

        inverse = lax.rsqrt(total / D + 1e-05)[None, :]
        hidden = []
        for t in range(CHUNKS):
            own, near, across, far = sums[t]
            sent = lax.ppermute(jnp.concatenate([near, far], axis=0).astype(BF), "gx", flip(1)).astype(F32)
            own, across = own + sent[: 2 * hid], across + sent[2 * hid :]
            own = own + lax.ppermute(across.astype(BF), "gx", flip(2)).astype(F32)
            scale = inverse[:, t * step : (t + 1) * step]
            gate, up = own[:hid] * scale, own[hid:] * scale
            hidden.append((jax.nn.silu(gate) * up).astype(BF))
        hidden = jnp.concatenate(hidden, axis=1)
        near = []
        for k in range(planes):
            for d in (0, 2):
                near.append(lax.ppermute(hidden, "gx", shift(-k, d)) if k or d else hidden)
        near = jnp.stack(near).reshape(planes, 2, hid, rows)
        far = lax.ppermute(near, "gx", flip(1))
        every = jnp.stack([near, far], axis=2).reshape(n * hid, rows)

        out = jnp.zeros((rows, width), BF)
        for r in range(groups):
            mixed = lax.dot_general(
                every, pieces[r].reshape(n * hid, part), (((0,), (0,)), ((), ())), preferred_element_type=F32
            ).astype(BF)
            out = lax.dynamic_update_slice(out, mixed, (0, (group + r) % groups * part))
        return out

    return body


def solution(mesh):
    body = make_body(mesh.shape["gx"], mesh.shape["groups"])
    in_specs = (P("groups", "gx"), P("gx"), P(None, "gx"), P(None, "gx"), P("gx", None))
    out_specs = P("groups", "gx")
    return jax.shard_map(body, mesh=mesh, in_specs=in_specs, out_specs=out_specs, check_vma=False)
```

time: 271 us -> 268 us (0.989); the launches traced: 271 us -> 263 us
  blocking collectives: 157 us -> 31.4 us
  local copies, waits for them, and re-layouts: 4.36 us -> 66.1 us
  starting transfers between devices: 7.39 us -> 33.8 us
  matrix products: 22.7 us -> 39.1 us
  waiting for transfers between devices: 63.8 us -> 79.6 us
  between operations: 13.4 us -> 0.99 us
  other arithmetic: 2.65 us -> 12.1 us
    psum x1 -> x0, blocking collectives: 157 us -> none  [body(): total = lax.psum(jnp.sum(values * values, axis=1), 'gx')]
    ppermute x0 -> x27, waiting for transfers between devices: none -> 79.6 us  [the longest x6 27.1 us: body(): current[t] = lax.ppermute(current[t], 'gx', shift(1))]
    all_gather x2 -> x0, waiting for transfers between devices: 63.8 us -> none  [the longest x1 39.4 us: body(): lax.all_gather(hidden, 'gx', axis=1, tiled=True)]
    ppermute x0 -> x27, starting transfers between devices: none -> 33.8 us  [the longest x7 12.7 us: body(): near.append(lax.ppermute(hidden, 'gx', shift(-k, d)) if k or d else hidden)]
    all_gather x0 -> x1, blocking collectives: none -> 31.4 us  [body(): total = jnp.sum(lax.all_gather(squares, 'gx'), axis=0)]
    dynamic_slice x0 -> x2, local copies, waits for them, and re-layouts: none -> 26.3 us  [the longest x1 21.4 us: features(): lax.dynamic_slice(w, (0, (plane + planes - s) % planes, quad ^ d, 0), (hi...]
    reshape x0 -> x3, local copies, waits for them, and re-layouts: none -> 22.8 us  [the longest x2 15.2 us: body(): w.T.reshape(hid, planes, 4, width)]
    dot_general x3 -> x34, matrix products: 22.7 us -> 39.1 us  [the longest x32 32.5 us: body(): lax.dot_general(weights[d][s], current[t], (((1,), (1,)), ((), ())), pref...]
  transfers between devices with their start and end apart: 3 -> 27, of which waited for: 2 -> 14; matrix products, arithmetic and copies ran while one was open for 8% -> 41% of each run, Pallas kernels for 0% -> 0%
where the time goes in v1:
time: 268 us; the launch traced here: 263 us
  waiting for transfers between devices  79.6 us (30%)
  local copies, waits for them, and re-layouts  66.1 us (25%)
  matrix products  39.1 us (15%)
  starting transfers between devices  33.8 us (13%)
  blocking collectives  31.4 us (12%)
  other arithmetic  12.1 us (5%)
    dot_general x32, matrix products, body(): lax.dot_general(weights[d][s], current[t], (((1,), (1,)), ((), ())), pref...  32.5 us
    all_gather x1, blocking collectives, body(): total = jnp.sum(lax.all_gather(squares, 'gx'), axis=0)  31.4 us
    ppermute x6, waiting for transfers between devices, body(): current[t] = lax.ppermute(current[t], 'gx', shift(1))  27.1 us
    ppermute x7, waiting for transfers between devices, body(): near.append(lax.ppermute(hidden, 'gx', shift(-k, d)) if k or d else hidden)  23.6 us
    ppermute x1, waiting for transfers between devices, body(): lax.ppermute(held, 'groups', [((g + r) % groups, g) for g in range(groups)])  22.3 us
    dynamic_slice x1, local copies, waits for them, and re-layouts, features(): lax.dynamic_slice(w, (0, (plane + planes - s) % planes, quad ^ d, 0), (hi...  21.4 us
    unnamed x90, local copies, waits for them, and re-layouts  15.2 us
    reshape x2, local copies, waits for them, and re-layouts, body(): w.T.reshape(hid, planes, 4, width)  15.2 us
  transfers between devices with their start and end apart: 27, of which 14 were waited for; matrix products, arithmetic and copies ran while one was open for 41% of the time, Pallas kernels for 0%

profile of v1, /device:TPU:1, one launch (start us, length us, event | category | flops | bytes accessed | tf_op | source)
XLA Modules:
  0.0 263.2 jit_solution(9379814871537607944)
XLA Ops:
  3.6 2.1 collective-permute-start.8
  5.8 6.9 %reshape.141 = bf16[104,4,4,1024]{3,2,1,0:T(4,128)(2,1)S(1)} reshape(bf16[104,16384]{1,0:T(8,128)(2,1)} %bitcast.262) | data formatting | bytes 6815744 | tf_op jit(solution)/shard_map/reshape | solution.py:37
  12.7 8.2 %reshape.139 = bf16[104,4,4,1024]{3,2,1,0:T(4,128)(2,1)} reshape(bf16[104,16384]{1,0:T(8,128)(2,1)} %bitcast.263) | data formatting | bytes 6815744 | tf_op jit(solution)/shard_map/reshape | solution.py:37
  20.9 21.4 %constant_dynamic-slice_fusion.8 = (bf16[104,1,1,1024]{3,2,1,0:T(2,128)(2,1)}, bf16[104,1,1,1024]{3,2,1,0:T(2,128)(2,1)}, bf16[104,1,1,1024]{3,2,1,0:T(2,128)(2,...) fusion(bf16[104,4,4,1024]{3,2,1,0:T(4,128)(2,1)S(1)} %reshape.1, ...), kind=kLoop, calls=%fused_computation.170 | loop fusion | bytes 13631520 | tf_op jit(solution)/shard_map/dynamic_slice | solution.py:44
  44.5 2.1 collective-permute-start.4
  50.1 7.6 %reshape.174 = bf16[104,4,2,2,2,512]{5,4,3,2,1,0:T(2,128)(2,1)S(1)} reshape(bf16[104,16384]{1,0:T(8,128)(2,1)} %param.9) | data formatting | bytes 6815744 | tf_op jit(solution)/shard_map/reshape | solution.py:66
  57.7 4.9 %constant_dynamic-slice_fusion = (bf16[104,4,2,1,1,512]{5,4,3,2,1,0:T(2,128)(2,1)S(1)}, bf16[104,4,2,1,1,512]{5,4,3,2,1,0:T(2,128)(2,1)}) fusion(bf16[104,4,2,2,2,512]{5,4,3,2,1,0:T(2,128)(2,1)S(1)} %reshape.174, s32[]{:T(128)S(6)} %select_n.230, s32[]{:T(128)S(6)} %select_n.229, s32[]{:T(128)S(6)} %select_n.228), kind=kLoop, calls=%fused_computation.162 | loop fusion | bytes 3407884 | tf_op jit(solution)/shard_map/dynamic_slice | solution.py:70
  66.7 31.4 %all-gather.1 = f32[16,1,512]{2,1,0:T(1,128)S(1)} all-gather(f32[1,1,512]{2,1,0:T(1,128)S(1)} %bitcast.311), channel_id=2, replica_groups=mesh['groups'=2,'gx'=16] {'gx'}, dimensions={0}, use_global_device_ids=true | all-gather | bytes 34816 | tf_op jit(solution)/shard_map/all_gather | solution.py:35
  114.3 11.1 %collective-permute-done.9 = bf16[256,1024]{1,0:T(8,128)(2,1)S(1)} collective-permute-done((bf16[256,1024]{1,0:T(8,128)(2,1)}, bf16[256,1024]{1,0:T(8,128)(2,1)S(1)}, u32[]{:S(2)}, u32[]{:S(2)}) %collective-permute-start.9) | collective-permute-done | bytes 524320 | tf_op jit(solution)/shard_map/ppermute | solution.py:61
  125.7 10.9 %collective-permute-done.1 = bf16[256,1024]{1,0:T(8,128)(2,1)S(1)} collective-permute-done((bf16[256,1024]{1,0:T(8,128)(2,1)}, bf16[256,1024]{1,0:T(8,128)(2,1)S(1)}, u32[]{:S(2)}, u32[]{:S(2)}) %collective-permute-start.1) | collective-permute-done | bytes 524320 | tf_op jit(solution)/shard_map/ppermute | solution.py:61
  145.7 5.1 %collective-permute-done.10 = bf16[256,1024]{1,0:T(8,128)(2,1)S(1)} collective-permute-done((bf16[256,1024]{1,0:T(8,128)(2,1)S(1)}, bf16[256,1024]{1,0:T(8,128)(2,1)S(1)}, u32[]{:S(2)}, u32[]{:S(2)}) %collective-permute-start.10) | collective-permute-done | bytes 524320 | tf_op jit(solution)/shard_map/ppermute | solution.py:61
  153.6 3.5 %collective-permute-start.11 = (bf16[416,256]{1,0:T(8,128)(2,1)S(1)}, bf16[416,256]{1,0:T(8,128)(2,1)S(1)}, u32[]{:S(2)}, u32[]{:S(2)}) collective-permute-start(bf16[416,256]{1,0:T(8,128)(2,1)S(1)} %pad_maximum_fusion.20), channel_id=1, source_target_pairs={{0,1},{1,0},{2,3},{3,2},{4,5},{5,4},{6,7},{7,6},{8,9},{9,8},{10,11... | collective-permute-start | bytes 638984 | tf_op jit(solution)/shard_map/ppermute | solution.py:92
  170.1 3.2 %collective-permute-start.24 = (bf16[2,2,104,512]{3,2,1,0:T(8,128)(2,1)S(1)}, bf16[2,2,104,512]{3,2,1,0:T(8,128)(2,1)S(1)}, u32[]{:S(2)}, u32[]{:S(2)}) collective-permute-start(bf16[2,2,104,512]{3,2,1,0:T(8,128)(2,1)S(1)} %get-tuple-element.41), channel_id=1, source_target_pairs={{0,8},{1,9},{2,10},{3,11},{4,12},{5,13},{6,14},{7,15},{8,0},{9,1},... | collective-permute-start | bytes 1277960 | tf_op jit(solution)/shard_map/ppermute | solution.py:82
  173.3 2.0 collective-permute-start.23
  181.8 1.9 collective-permute-done.12
  187.3 1.9 collective-permute-done.13
  190.5 13.6 %collective-permute-done.14 = bf16[104,512]{1,0:T(8,128)(2,1)S(1)} collective-permute-done((bf16[104,512]{1,0:T(8,128)(2,1)S(1)}, bf16[104,512]{1,0:T(8,128)(2,1)S(1)}, u32[]{:S(2)}, u32[]{:S(2)}) %collective-permute-start.14) | collective-permute-done | bytes 106528 | tf_op jit(solution)/shard_map/ppermute | solution.py:102
  204.1 8.4 %collective-permute-start.16 = (bf16[104,512]{1,0:T(8,128)(2,1)S(1)}, bf16[104,512]{1,0:T(8,128)(2,1)S(1)}, u32[]{:S(2)}, u32[]{:S(2)}) collective-permute-start(bf16[104,512]{1,0:T(8,128)(2,1)S(1)} %pad_maximum_fusion.21), channel_id=1, source_target_pairs={{0,8},{1,9},{2,10},{3,11},{4,12},{5,13},{6,14},{7,15},{8,0},{9,1},... | collective-permute-start | bytes 319496 | tf_op jit(solution)/shard_map/ppermute | solution.py:102
  215.3 4.9 %collective-permute-done.16 = bf16[104,512]{1,0:T(8,128)(2,1)S(1)} collective-permute-done((bf16[104,512]{1,0:T(8,128)(2,1)S(1)}, bf16[104,512]{1,0:T(8,128)(2,1)S(1)}, u32[]{:S(2)}, u32[]{:S(2)}) %collective-permute-start.16) | collective-permute-done | bytes 106528 | tf_op jit(solution)/shard_map/ppermute | solution.py:102
  229.1 2.7 %collective-permute-start.20 = (bf16[4,2,104,512]{3,2,1,0:T(8,128)(2,1)}, bf16[4,2,104,512]{3,2,1,0:T(8,128)(2,1)}, u32[]{:S(2)}, u32[]{:S(2)}) collective-permute-start(bf16[4,2,104,512]{3,2,1,0:T(8,128)(2,1)} %bitcast.40), channel_id=1, source_target_pairs={{0,1},{1,0},{2,3},{3,2},{4,5},{5,4},{6,7},{7,6},{8,9},{9,8},{10,11... | collective-permute-start | bytes 2555912 | tf_op jit(solution)/shard_map/ppermute | solution.py:104
  231.8 2.3 collective-permute-done.20
  234.3 2.7 %fusion.3 = bf16[512,1024]{1,0:T(8,128)(2,1)S(1)} fusion(bf16[512,1024]{1,0:T(8,128)(2,1)S(1)} %broadcast_in_dim.2, s32[]{:T(128)S(6)} %select_n.235, bf16[4,2,1,104,512]{4,3,2,1,0:T(8,128)(2,1)} %bitcast.41, bf16[4,2,1,104,512]{4,3,2,1,0:T(8,128)(2,1)} %bitcast.39, bf16[1,2,2,104,512]{4,3,2,1,0:T(8,128)(2,1)S(1)} %bitcast.302, ...), kind=kOutput, calls=%fused_computation.24 | convolution fusion | flops 876085248 | bytes 3932164 | tf_op jit(solution)/shard_map/dot_general | solution.py:109
  237.0 22.3 %collective-permute-done.26 = bf16[4,2,2,104,512]{4,3,2,1,0:T(8,128)(2,1)} collective-permute-done((bf16[4,2,2,104,512]{4,3,2,1,0:T(8,128)(2,1)S(1)}, bf16[4,2,2,104,512]{4,3,2,1,0:T(8,128)(2,1)}, u32[]{:S(2)}, u32[]{:S(2)}) %collective-permute-start.26) | collective-permute-done | bytes 1703968 | tf_op jit(solution)/shard_map/ppermute | solution.py:85
  259.2 3.9 %fusion.5 = bf16[512,1024]{1,0:T(8,128)(2,1)} fusion(bf16[512,1024]{1,0:T(8,128)(2,1)} %copy-done.16, s32[]{:T(128)S(6)} %select_n.237, bf16[4,2,2,104,512]{4,3,2,1,0:T(8,128)(2,1)} %collective-permute-done.26, bf16[4,2,1,104,512]{4,3,2,1,0:T(8,128)(2,1)} %bitcast.41, bf16[4,2,1,104,512]{4,3,2,1,0:T(8,128)(2,1)} %bitcast.39), kind=kOutput, calls=%fused_computation.26 | convolution fusion | flops 873529344 | bytes 3932164 | tf_op jit(solution)/shard_map/dot_general | solution.py:109
  (193 shorter events, 77.1 us)
Async XLA Ops:
  3.6 106.3 %collective-permute-start.8 = (bf16[256,1024]{1,0:T(8,128)(2,1)}, bf16[256,1024]{1,0:T(8,128)(2,1)}, u32[]{:S(2)}, u32[]{:S(2)}) collective-permute-start(bf16[256,1024]{1,0:T(8,128)(2,1)} %get-tuple-element.46), channel_id=1, source_target_pairs={{0,4},{1,5},{2,6},{3,7},{4,8},{5,9},{6,10},{7,11},{8,12},{9,13},{1... | collective-permute-start | bytes 1572872 | tf_op jit(solution)/shard_map/ppermute | solution.py:61
  44.5 92.5 %collective-permute-start.4 = (bf16[4,208,1024]{2,1,0:T(8,128)(2,1)}, bf16[4,208,1024]{2,1,0:T(8,128)(2,1)}, u32[]{:S(2)}, u32[]{:S(2)}) collective-permute-start(bf16[4,208,1024]{2,1,0:T(8,128)(2,1)} %pad_maximum_fusion.1), channel_id=1, source_target_pairs={{0,3},{1,2},{2,1},{3,0},{4,7},{5,6},{6,5},{7,4},{8,11},{9,10},{10,... | collective-permute-start | bytes 5111816 | tf_op jit(solution)/shard_map/ppermute | solution.py:53
  48.8 92.7 %collective-permute-start.3 = (bf16[4,208,1024]{2,1,0:T(8,128)(2,1)}, bf16[4,208,1024]{2,1,0:T(8,128)(2,1)}, u32[]{:S(2)}, u32[]{:S(2)}) collective-permute-start(bf16[4,208,1024]{2,1,0:T(8,128)(2,1)} %pad_maximum_fusion), channel_id=1, source_target_pairs={{0,1},{1,0},{2,3},{3,2},{4,5},{5,4},{6,7},{7,6},{8,9},{9,8},{10,11... | collective-permute-start | bytes 5111816 | tf_op jit(solution)/shard_map/ppermute | solution.py:53
  48.8 61.3 %collective-permute-start = (bf16[256,1024]{1,0:T(8,128)(2,1)}, bf16[256,1024]{1,0:T(8,128)(2,1)}, u32[]{:S(2)}, u32[]{:S(2)}) collective-permute-start(bf16[256,1024]{1,0:T(8,128)(2,1)} %get-tuple-element.45), channel_id=1, source_target_pairs={{0,4},{1,5},{2,6},{3,7},{4,8},{5,9},{6,10},{7,11},{8,12},{9,13},{1... | collective-permute-start | bytes 1572872 | tf_op jit(solution)/shard_map/ppermute | solution.py:61
  64.4 48.5 %collective-permute-start.21 = (bf16[4,2,104,512]{3,2,1,0:T(8,128)(2,1)}, bf16[4,2,104,512]{3,2,1,0:T(8,128)(2,1)}, u32[]{:S(2)}, u32[]{:S(2)}) collective-permute-start(bf16[4,2,104,512]{3,2,1,0:T(8,128)(2,1)} %bitcast.227), channel_id=1, source_target_pairs={{0,1},{1,0},{2,3},{3,2},{4,5},{5,4},{6,7},{7,6},{8,9},{9,8},{10,11... | collective-permute-start | bytes 2555912 | tf_op jit(solution)/shard_map/ppermute | solution.py:73
  110.0 15.4 %collective-permute-start.9 = (bf16[256,1024]{1,0:T(8,128)(2,1)}, bf16[256,1024]{1,0:T(8,128)(2,1)S(1)}, u32[]{:S(2)}, u32[]{:S(2)}) collective-permute-start(bf16[256,1024]{1,0:T(8,128)(2,1)} %collective-permute-done.8), channel_id=1, source_target_pairs={{0,4},{1,5},{2,6},{3,7},{4,8},{5,9},{6,10},{7,11},{8,12},{9,13},{1... | collective-permute-start | bytes 1572872 | tf_op jit(solution)/shard_map/ppermute | solution.py:61
  110.0 26.6 %collective-permute-start.1 = (bf16[256,1024]{1,0:T(8,128)(2,1)}, bf16[256,1024]{1,0:T(8,128)(2,1)S(1)}, u32[]{:S(2)}, u32[]{:S(2)}) collective-permute-start(bf16[256,1024]{1,0:T(8,128)(2,1)} %collective-permute-done), channel_id=1, source_target_pairs={{0,4},{1,5},{2,6},{3,7},{4,8},{5,9},{6,10},{7,11},{8,12},{9,13},{1... | collective-permute-start | bytes 1572872 | tf_op jit(solution)/shard_map/ppermute | solution.py:61
  112.9 60.4 %collective-permute-start.6 = (bf16[4,208,1024]{2,1,0:T(8,128)(2,1)S(1)}, bf16[4,208,1024]{2,1,0:T(8,128)(2,1)S(1)}, u32[]{:S(2)}, u32[]{:S(2)}) collective-permute-start(bf16[4,208,1024]{2,1,0:T(8,128)(2,1)S(1)} %pad_maximum_fusion.2), channel_id=1, source_target_pairs={{0,2},{1,3},{2,0},{3,1},{4,6},{5,7},{6,4},{7,5},{8,10},{9,11},{10,... | collective-permute-start | bytes 5111816 | tf_op jit(solution)/shard_map/ppermute | solution.py:53
  125.4 44.5 %collective-permute-start.22 = (bf16[4,2,104,512]{3,2,1,0:T(8,128)(2,1)S(1)}, bf16[4,2,104,512]{3,2,1,0:T(8,128)(2,1)S(1)}, u32[]{:S(2)}, u32[]{:S(2)}) collective-permute-start(bf16[4,2,104,512]{3,2,1,0:T(8,128)(2,1)S(1)} %get-tuple-element.43), channel_id=1, source_target_pairs={{0,2},{1,3},{2,0},{3,1},{4,6},{5,7},{6,4},{7,5},{8,10},{9,11},{10,... | collective-permute-start | bytes 2555912 | tf_op jit(solution)/shard_map/ppermute | solution.py:78
  136.6 14.2 %collective-permute-start.10 = (bf16[256,1024]{1,0:T(8,128)(2,1)S(1)}, bf16[256,1024]{1,0:T(8,128)(2,1)S(1)}, u32[]{:S(2)}, u32[]{:S(2)}) collective-permute-start(bf16[256,1024]{1,0:T(8,128)(2,1)S(1)} %collective-permute-done.9), channel_id=1, source_target_pairs={{0,4},{1,5},{2,6},{3,7},{4,8},{5,9},{6,10},{7,11},{8,12},{9,13},{1... | collective-permute-start | bytes 1572872 | tf_op jit(solution)/shard_map/ppermute | solution.py:61
  137.0 27.2 %collective-permute-start.2 = (bf16[256,1024]{1,0:T(8,128)(2,1)S(1)}, bf16[256,1024]{1,0:T(8,128)(2,1)S(1)}, u32[]{:S(2)}, u32[]{:S(2)}) collective-permute-start(bf16[256,1024]{1,0:T(8,128)(2,1)S(1)} %collective-permute-done.1), channel_id=1, source_target_pairs={{0,4},{1,5},{2,6},{3,7},{4,8},{5,9},{6,10},{7,11},{8,12},{9,13},{1... | collective-permute-start | bytes 1572872 | tf_op jit(solution)/shard_map/ppermute | solution.py:61
  153.6 25.9 %collective-permute-start.11 = (bf16[416,256]{1,0:T(8,128)(2,1)S(1)}, bf16[416,256]{1,0:T(8,128)(2,1)S(1)}, u32[]{:S(2)}, u32[]{:S(2)}) collective-permute-start(bf16[416,256]{1,0:T(8,128)(2,1)S(1)} %pad_maximum_fusion.20), channel_id=1, source_target_pairs={{0,1},{1,0},{2,3},{3,2},{4,5},{5,4},{6,7},{7,6},{8,9},{9,8},{10,11... | collective-permute-start | bytes 638984 | tf_op jit(solution)/shard_map/ppermute | solution.py:92
  168.2 12.0 %collective-permute-start.5 = (bf16[416,256]{1,0:T(8,128)(2,1)S(1)}, bf16[416,256]{1,0:T(8,128)(2,1)S(1)}, u32[]{:S(2)}, u32[]{:S(2)}) collective-permute-start(bf16[416,256]{1,0:T(8,128)(2,1)S(1)} %pad_maximum_fusion.19), channel_id=1, source_target_pairs={{0,1},{1,0},{2,3},{3,2},{4,5},{5,4},{6,7},{7,6},{8,9},{9,8},{10,11... | collective-permute-start | bytes 638984 | tf_op jit(solution)/shard_map/ppermute | solution.py:92
  170.0 51.6 %collective-permute-start.25 = (bf16[2,2,104,512]{3,2,1,0:T(8,128)(2,1)S(1)}, bf16[2,2,104,512]{3,2,1,0:T(8,128)(2,1)S(1)}, u32[]{:S(2)}, u32[]{:S(2)}) collective-permute-start(bf16[2,2,104,512]{3,2,1,0:T(8,128)(2,1)S(1)} %get-tuple-element.42), channel_id=1, source_target_pairs={{0,4},{1,5},{2,6},{3,7},{4,8},{5,9},{6,10},{7,11},{8,12},{9,13},{1... | collective-permute-start | bytes 1277960 | tf_op jit(solution)/shard_map/ppermute | solution.py:82
  170.1 51.6 %collective-permute-start.24 = (bf16[2,2,104,512]{3,2,1,0:T(8,128)(2,1)S(1)}, bf16[2,2,104,512]{3,2,1,0:T(8,128)(2,1)S(1)}, u32[]{:S(2)}, u32[]{:S(2)}) collective-permute-start(bf16[2,2,104,512]{3,2,1,0:T(8,128)(2,1)S(1)} %get-tuple-element.41), channel_id=1, source_target_pairs={{0,8},{1,9},{2,10},{3,11},{4,12},{5,13},{6,14},{7,15},{8,0},{9,1},... | collective-permute-start | bytes 1277960 | tf_op jit(solution)/shard_map/ppermute | solution.py:82
  173.3 48.4 %collective-permute-start.23 = (bf16[2,2,104,512]{3,2,1,0:T(8,128)(2,1)S(1)}, bf16[2,2,104,512]{3,2,1,0:T(8,128)(2,1)S(1)}, u32[]{:S(2)}, u32[]{:S(2)}) collective-permute-start(bf16[2,2,104,512]{3,2,1,0:T(8,128)(2,1)S(1)} %get-tuple-element.40), channel_id=1, source_target_pairs={{0,12},{1,13},{2,14},{3,15},{4,0},{5,1},{6,2},{7,3},{8,4},{9,5},{1... | collective-permute-start | bytes 1277960 | tf_op jit(solution)/shard_map/ppermute | solution.py:82
  186.3 17.8 %collective-permute-start.14 = (bf16[104,512]{1,0:T(8,128)(2,1)S(1)}, bf16[104,512]{1,0:T(8,128)(2,1)S(1)}, u32[]{:S(2)}, u32[]{:S(2)}) collective-permute-start(bf16[104,512]{1,0:T(8,128)(2,1)S(1)} %pad_maximum_fusion.21), channel_id=1, source_target_pairs={{0,12},{1,13},{2,14},{3,15},{4,0},{5,1},{6,2},{7,3},{8,4},{9,5},{1... | collective-permute-start | bytes 319496 | tf_op jit(solution)/shard_map/ppermute | solution.py:102
  189.2 24.0 %collective-permute-start.15 = (bf16[104,512]{1,0:T(8,128)(2,1)S(1)}, bf16[104,512]{1,0:T(8,128)(2,1)S(1)}, u32[]{:S(2)}, u32[]{:S(2)}) collective-permute-start(bf16[104,512]{1,0:T(8,128)(2,1)S(1)} %pad_maximum_fusion.21), channel_id=1, source_target_pairs={{0,14},{1,15},{2,12},{3,13},{4,2},{5,3},{6,0},{7,1},{8,6},{9,7},{1... | collective-permute-start | bytes 319496 | tf_op jit(solution)/shard_map/ppermute | solution.py:102
  204.1 16.0 %collective-permute-start.16 = (bf16[104,512]{1,0:T(8,128)(2,1)S(1)}, bf16[104,512]{1,0:T(8,128)(2,1)S(1)}, u32[]{:S(2)}, u32[]{:S(2)}) collective-permute-start(bf16[104,512]{1,0:T(8,128)(2,1)S(1)} %pad_maximum_fusion.21), channel_id=1, source_target_pairs={{0,8},{1,9},{2,10},{3,11},{4,12},{5,13},{6,14},{7,15},{8,0},{9,1},... | collective-permute-start | bytes 319496 | tf_op jit(solution)/shard_map/ppermute | solution.py:102
  213.2 11.3 %collective-permute-start.17 = (bf16[104,512]{1,0:T(8,128)(2,1)S(1)}, bf16[104,512]{1,0:T(8,128)(2,1)S(1)}, u32[]{:S(2)}, u32[]{:S(2)}) collective-permute-start(bf16[104,512]{1,0:T(8,128)(2,1)S(1)} %pad_maximum_fusion.21), channel_id=1, source_target_pairs={{0,10},{1,11},{2,8},{3,9},{4,14},{5,15},{6,12},{7,13},{8,2},{9,3},... | collective-permute-start | bytes 319496 | tf_op jit(solution)/shard_map/ppermute | solution.py:102
  220.2 5.8 %collective-permute-start.18 = (bf16[104,512]{1,0:T(8,128)(2,1)S(1)}, bf16[104,512]{1,0:T(8,128)(2,1)S(1)}, u32[]{:S(2)}, u32[]{:S(2)}) collective-permute-start(bf16[104,512]{1,0:T(8,128)(2,1)S(1)} %pad_maximum_fusion.21), channel_id=1, source_target_pairs={{0,4},{1,5},{2,6},{3,7},{4,8},{5,9},{6,10},{7,11},{8,12},{9,13},{1... | collective-permute-start | bytes 319496 | tf_op jit(solution)/shard_map/ppermute | solution.py:102
  221.7 6.7 %collective-permute-start.19 = (bf16[104,512]{1,0:T(8,128)(2,1)S(1)}, bf16[104,512]{1,0:T(8,128)(2,1)S(1)}, u32[]{:S(2)}, u32[]{:S(2)}) collective-permute-start(bf16[104,512]{1,0:T(8,128)(2,1)S(1)} %pad_maximum_fusion.21), channel_id=1, source_target_pairs={{0,6},{1,7},{2,4},{3,5},{4,10},{5,11},{6,8},{7,9},{8,14},{9,15},{1... | collective-permute-start | bytes 319496 | tf_op jit(solution)/shard_map/ppermute | solution.py:102
  222.6 36.6 %collective-permute-start.26 = (bf16[4,2,2,104,512]{4,3,2,1,0:T(8,128)(2,1)S(1)}, bf16[4,2,2,104,512]{4,3,2,1,0:T(8,128)(2,1)}, u32[]{:S(2)}, u32[]{:S(2)}) collective-permute-start(bf16[4,2,2,104,512]{4,3,2,1,0:T(8,128)(2,1)S(1)} %pad_maximum_fusion.4), channel_id=1, source_target_pairs={{16,0},{0,16},{17,1},{1,17},{18,2},{2,18},{19,3},{3,19},{20,4},{4,... | collective-permute-start | bytes 5111816 | tf_op jit(solution)/shard_map/ppermute | solution.py:85
  229.1 5.1 %collective-permute-start.20 = (bf16[4,2,104,512]{3,2,1,0:T(8,128)(2,1)}, bf16[4,2,104,512]{3,2,1,0:T(8,128)(2,1)}, u32[]{:S(2)}, u32[]{:S(2)}) collective-permute-start(bf16[4,2,104,512]{3,2,1,0:T(8,128)(2,1)} %bitcast.40), channel_id=1, source_target_pairs={{0,1},{1,0},{2,3},{3,2},{4,5},{5,4},{6,7},{7,6},{8,9},{9,8},{10,11... | collective-permute-start | bytes 2555912 | tf_op jit(solution)/shard_map/ppermute | solution.py:104
  (28 other events, 186.2 us)

commit v2 on v0

v2 whole, which is shorter than its diff:
```python
import functools

import jax
import jax.numpy as jnp
from jax import lax
from jax.experimental import pallas as pl
from jax.experimental.pallas import tpu as pltpu
from jax.sharding import PartitionSpec as P

D = 16384
BF = jnp.bfloat16
F32 = jnp.float32
ANY = pl.BlockSpec(memory_space=pl.ANY)
VMEM = pl.BlockSpec(memory_space=pltpu.VMEM)
PARAMS = pltpu.CompilerParams(vmem_limit_bytes=48 * 1024 * 1024)
HEAVY = 1
EXTRA = 16


def shape(*dims, dtype=BF):
    return jax.ShapeDtypeStruct(dims, dtype)


def cost(size, flops=0):
    return pl.CostEstimate(flops=HEAVY * flops, bytes_accessed=HEAVY * size, transcendentals=0)


def move(moves, outs, *operands, after=()):
    def kernel(*refs):
        for source, where, target, there in moves(refs[: len(operands)], refs[len(operands) + len(after) :]):
            target[there] = source[where]

    return pl.pallas_call(
        kernel,
        out_shape=outs,
        in_specs=[VMEM] * len(operands) + [ANY] * len(after),
        out_specs=[VMEM] * len(outs),
        compiler_params=PARAMS,
        cost_estimate=cost(4 * sum(o.size for o in outs)),
    )(*operands, *after)


def split(values):
    parts = []
    for _ in range(3):
        parts.append(lax.reduce_precision(values, 8, 7))
        values = values - parts[-1]
    return jnp.pad(jnp.concatenate(parts), ((0, EXTRA - 3), (0, 0))).astype(BF)


def joined(parts):
    parts = parts.astype(F32)
    return parts[0:1] + parts[1:2] + parts[2:3]


def stage(kernel, outs, *operands, after=()):
    def body(*refs):
        kernel(*refs[: len(operands)], *refs[len(operands) + len(after) :])

    return pl.pallas_call(
        body,
        out_shape=outs,
        in_specs=[VMEM] * len(operands) + [ANY] * len(after),
        out_specs=[VMEM] * len(outs),
        compiler_params=PARAMS,
        cost_estimate=cost(4 * sum(o.size for o in outs)),
    )(*operands, *after)


def put_parts(values, out):
    parts = []
    for _ in range(3):
        parts.append(values.astype(BF).astype(F32))
        values = values - parts[-1]
    out[pl.ds(0, EXTRA), :] = jnp.concatenate(parts + [jnp.zeros((EXTRA - 3, values.shape[1]), F32)]).astype(BF)


def leave(sums, total, send):
    count = sums.shape[0] // 4
    put_parts(total[...], send)
    for i, d in enumerate((1, 3)):
        send[pl.ds(EXTRA + i * count, count), :] = sums[pl.ds(d * count, count), :].astype(BF)


def meet(sums, total, came, mine, total_out, send):
    count = sums.shape[0] // 4
    both = total[...] + joined(came[pl.ds(0, EXTRA), :])
    total_out[...] = both
    mine[...] = sums[pl.ds(0, count), :] + came[pl.ds(EXTRA, count), :].astype(F32)
    put_parts(both, send)
    across = sums[pl.ds(2 * count, count), :] + came[pl.ds(EXTRA + count, count), :].astype(F32)
    send[pl.ds(EXTRA, count), :] = across.astype(BF)


def activate(mine, total, came, hidden):
    hid = hidden.shape[0]
    inverse = lax.rsqrt((total[...] + joined(came[pl.ds(0, EXTRA), :])) / D + 1e-05)
    gate = (mine[pl.ds(0, hid), :] + came[pl.ds(EXTRA, hid), :].astype(F32)) * inverse
    up = (mine[pl.ds(hid, hid), :] + came[pl.ds(EXTRA + hid, hid), :].astype(F32)) * inverse
    hidden[...] = (gate / (1.0 + jnp.exp(-gate)) * up).astype(BF)


def arrivals(planes):
    order = [0]
    for s in range(1, planes // 2 + 1):
        order += [s] if 2 * s == planes else [s, planes - s]
    return order


def make_body(n, groups):
    planes = n // 4
    order = arrivals(planes)
    cuts = [range(0, planes // 2), *[range(j, j + 1) for j in range(planes // 2, planes)]] if planes <= 4 else [range(0, planes // 2), range(planes // 2, planes)]
    paired = groups % 2 == 0

    def at(p, q):
        return (p % planes) * 4 + q

    def flip(d):
        return [(at(p, q), at(p, q ^ d)) for p in range(planes) for q in range(4)]

    def shift(k, d=0):
        return [(at(p, q), at(p + k, q ^ d)) for p in range(planes) for q in range(4)]

    def far_flip():
        return [(g * n + i, g * n + j) for g in range(groups) for i, j in flip(2 + g % 2)]

    def swap(r):
        return [((g + r) % groups, g) for g in range(groups)]

    def place():
        me = lax.axis_index("gx")
        return me // 4, me % 4

    def product(spot, rows, blocks, own, near, far, js, total=None, after=()):
        width = blocks[0].shape[1]
        _, two, hid, _ = near.shape
        first, count = js[0], len(js)
        given = [] if total is None else [total]

        def kernel(spot, *refs):
            sources, refs = refs[:count], refs[count:]
            own_gate, own_up, near, far0, far1 = refs[:5]
            out, xs, sems = refs[-3:]
            i = pl.program_id(0)
            copies = [
                pltpu.make_async_copy(x.at[pl.ds(0, rows)], xs.at[k], sems.at[k]) for k, x in enumerate(sources)
            ]

            @pl.when(i == 0)
            def _():
                for copy in copies:
                    copy.start()
                out[...] = refs[5][...] if given else jnp.zeros_like(out)

            for k, copy in enumerate(copies):
                pl.when(i == k)(copy.wait)

            x = xs[i]
            weights = [own_gate[...], own_up[...]] + [w[0, j] for w in (near, far0, far1) for j in range(2)]
            for b, block in enumerate(weights):
                term = lax.dot_general(block, x, (((1,), (1,)), ((), ())), preferred_element_type=F32)
                d = b // 2 if b < 4 else 2 + lax.bitwise_xor(b // 2 - 2, spot[2])
                out[pl.ds(pl.multiple_of((d * 2 + b % 2) * hid, 8), hid), :] += term

        near_block = pl.BlockSpec((1, two, hid, width), lambda i, spot: (i + first, 0, 0, 0))
        far_block = pl.BlockSpec((1, two, hid, width), lambda i, spot: (i, 0, 0, 0))
        mine = pl.BlockSpec((hid, width), lambda i, spot: (0, spot[3 + first + i] * 4 + spot[1]))
        whole = pl.BlockSpec((8 * hid, rows), lambda i, spot: (0, 0))
        return pl.pallas_call(
            kernel,
            grid_spec=pltpu.PrefetchScalarGridSpec(
                num_scalar_prefetch=1,
                grid=(count,),
                in_specs=[ANY] * count
                + [mine, mine, near_block, far_block, far_block]
                + [whole] * len(given)
                + [ANY] * len(after),
                out_specs=whole,
                scratch_shapes=[pltpu.VMEM((count, rows, width), BF), pltpu.SemaphoreType.DMA((count,))],
            ),
            out_shape=shape(8 * hid, rows, dtype=F32),
            compiler_params=PARAMS,
            cost_estimate=cost(16 * hid * width * count, 16 * hid * rows * width * count),
        )(spot, *[blocks[j] for j in js], *own, near, *far, *given, *after)

    def cut(spot, gate_t, up_t, width, ds, first, count, after=()):
        hid = gate_t.shape[0]

        def kernel(spot, *refs):
            outs = refs[2 * len(ds) + len(after) :]
            for d, out in enumerate(outs):
                for j in range(2):
                    out[0, j] = refs[2 * d + j][...]

        def taken(d):
            def index(s, spot):
                other = lax.bitwise_xor(spot[1], d + spot[2] if d == 2 and paired else d)
                return 0, spot[3 + first + s] * 4 + other

            return pl.BlockSpec((hid, width), index)

        return pl.pallas_call(
            kernel,
            grid_spec=pltpu.PrefetchScalarGridSpec(
                num_scalar_prefetch=1,
                grid=(count,),
                in_specs=[taken(d) for d in ds for _ in range(2)] + [ANY] * len(after),
                out_specs=[pl.BlockSpec((1, 2, hid, width), lambda s, spot: (s, 0, 0, 0))] * len(ds),
            ),
            out_shape=[shape(count, 2, hid, width)] * len(ds),
            compiler_params=PARAMS,
            cost_estimate=cost(8 * len(ds) * count * hid * width),
        )(spot, *[gate_t, up_t] * len(ds), *after)

    def mix(side, pieces, share, dc, total=None):
        rows = side.shape[-1]
        part = pieces[0].shape[-1]
        hid = side.shape[2]
        given = [] if total is None else [total]

        def kernel(side, *refs):
            out = refs[-1]
            g = lax.axis_index("groups")
            for r in range(share):
                sums = refs[-2][r] if given else None
                for k in range(planes):
                    for dy in range(2):
                        term = lax.dot_general(
                            side[k, dy],
                            refs[r * planes + k][dy, dc],
                            (((0,), (0,)), ((), ())),
                            preferred_element_type=F32,
                        )
                        sums = term if sums is None else sums + term
                if not given:
                    out[r] = sums
                elif share == 1:
                    out[...] = sums.astype(BF)
                else:
                    out[:, pl.ds(pl.multiple_of((g + r) % share * part, part), part)] = sums.astype(BF)

        return pl.pallas_call(
            kernel,
            out_shape=shape(rows, share * part) if given else shape(share, rows, part, dtype=F32),
            in_specs=[VMEM] * (1 + len(pieces) + len(given)),
            out_specs=VMEM,
            compiler_params=PARAMS,
            cost_estimate=cost(n * hid * (rows + share * part), rows * n * hid * share * part),
        )(side, *pieces, *given)

    def body(tokens, gain, gate_weight, up_weight, down_weight):
        rows, width = tokens.shape
        hid = gate_weight.shape[1]
        share = groups if width // groups % 128 == 0 else 1
        part = width // share
        own = gate_weight.T, up_weight.T
        me = lax.axis_index("gx")
        plane, quad = me // 4, me % 4
        half = lax.axis_index("groups") % 2 if paired else jnp.int32(0)
        spot = jnp.stack([plane, quad, half] + [lax.rem(plane + planes - s, planes) for s in order])

        values = tokens.astype(F32)
        squares = split(jnp.sum(values * values, axis=1)[None, :])
        lanes = min(rows, width)
        extra = jnp.concatenate([squares[:, i : i + lanes] for i in range(0, rows, lanes)])
        scaled = (values * gain[None, :]).astype(BF)
        blocks = [jnp.concatenate([scaled, jnp.pad(extra, ((0, 0), (0, width - lanes)))])]
        for s in order[1:]:
            way = 1 if 2 * s <= planes else -1
            last = blocks[0] if len(blocks) < 3 else blocks[-2]
            blocks.append(lax.ppermute(last, "gx", shift(way)))
        parts = [b[rows + i : rows + i + EXTRA, :lanes] for b in blocks for i in range(0, len(extra), EXTRA)]
        parts = [jnp.concatenate([joined(p) for p in parts[i :: len(extra) // EXTRA]]) for i in range(len(extra) // EXTRA)]
        total = jnp.concatenate([jnp.sum(p, axis=0, keepdims=True) for p in parts], axis=1)

        def first_moves(given, outs):
            _, quad = place()
            g = lax.axis_index("groups") if share > 1 else 0
            moves = []
            for other in range(2):
                for p in range(planes):
                    for y in range(2):
                        target = p * 4 + y * 2 + lax.bitwise_xor(lax.rem(quad, 2), other)
                        columns = pl.ds(pl.multiple_of(target * width + g * part, part), part)
                        moves.append((given[0], (slice(None), columns), outs[other], (y, p)))
            return moves

        keep, send = move(first_moves, [shape(2, planes, hid, part)] * 2, down_weight)
        came = lax.ppermute(send, "gx", flip(1))

        def second_moves(given, outs):
            _, quad = place()
            return [(given[dc], lax.bitwise_xor(quad // 2, 1), outs[0], dc) for dc in range(2)]

        send = move(second_moves, [shape(2, planes, hid, part)], keep, came)[0]
        across = lax.ppermute(send, "gx", flip(2))

        def third_moves(given, outs):
            plane, quad = place()
            moves = []
            for k in range(planes):
                p = lax.rem(plane + planes - k, planes)
                for dc in range(2):
                    moves.append((given[dc], (quad // 2, p), outs[k], (0, dc)))
                    moves.append((given[2], (dc, p), outs[k], (1, dc)))
            return moves

        ready = move(third_moves, [shape(2, 2, hid, part)] * planes, keep, came, across)
        held = [lax.ppermute(h, "gx", shift(-k)) if k else h for k, h in enumerate(ready)]
        pieces = list(held)
        for r in range(1, share):
            pieces += [lax.ppermute(h, "groups", swap(r)) for h in held]

        far = []
        for i, js in enumerate(cuts):
            sends = cut(spot, *own, width, (2,) if paired else (2, 3), js[0], len(js), after=(send,) if i else ())
            if paired:
                came = lax.ppermute(sends[0], ("groups", "gx"), far_flip())
                far.append((came, lax.ppermute(came, "groups", [(i, i ^ 1) for i in range(groups)])))
            else:
                far.append(tuple(lax.ppermute(w, "gx", flip(d)) for d, w in zip((2, 3), sends)))
        near = lax.ppermute(cut(spot, *own, width, (1,), 0, planes)[0], "gx", flip(1))

        sums = None
        crossed = pieces[planes:] if share > 1 else held
        needs = [(ready[0],), (held[1],), (held[-1], crossed[0])]
        later = [(crossed[1],), (crossed[-1], held[2 % planes])]
        for i, js in enumerate(cuts):
            sums = product(spot, rows, blocks, own, near, far[i], js, sums, after=needs[i])

        send = stage(leave, [shape(EXTRA + 4 * hid, rows)], sums, total)[0]
        came = lax.ppermute(send, "gx", flip(1))
        mine, total, send = stage(
            meet, [shape(2 * hid, rows, dtype=F32), shape(1, rows, dtype=F32), shape(EXTRA + 2 * hid, rows)], sums, total, came,
            after=later[0],
        )
        came = lax.ppermute(send, "gx", flip(2))
        hidden = stage(activate, [shape(hid, rows)], mine, total, came, after=later[1])[0]
        beside = [lax.ppermute(hidden, "gx", shift(-k, d)) if k or d else hidden for k in range(planes) for d in (0, 2)]
        beside = move(
            lambda given, outs: [(a, ..., outs[0], (i // 2, i % 2)) for i, a in enumerate(given)],
            [shape(planes, 2, hid, rows)],
            *beside,
        )[0]
        other = lax.ppermute(beside, "gx", flip(1))
        return mix(other, pieces, share, 1, mix(beside, pieces, share, 0))

    return body


def solution(mesh):
    body = make_body(mesh.shape["gx"], mesh.shape["groups"])
    in_specs = (P("groups", "gx"), P("gx"), P(None, "gx"), P(None, "gx"), P("gx", None))
    out_specs = P("groups", "gx")
    return jax.shard_map(body, mesh=mesh, in_specs=in_specs, out_specs=out_specs, check_vma=False)
```

time: 271 us -> 179 us (0.66)
  blocking collectives: 157 us -> 0 us
  Pallas kernels: 0 us -> 40.1 us
  starting transfers between devices: 7.39 us -> 36 us
  waiting for transfers between devices: 63.8 us -> 89.4 us
  matrix products: 22.7 us -> 0 us
  between operations: 13.4 us -> 0.2 us
  local copies, waits for them, and re-layouts: 4.36 us -> 8.38 us
    psum x1 -> x0, blocking collectives: 157 us -> none  [body(): total = lax.psum(jnp.sum(values * values, axis=1), 'gx')]
    ppermute x0 -> x29, waiting for transfers between devices: none -> 89.4 us  [the longest x3 23 us: body(): blocks.append(lax.ppermute(last, 'gx', shift(way)))]
    all_gather x2 -> x0, waiting for transfers between devices: 63.8 us -> none  [the longest x1 39.4 us: body(): lax.all_gather(hidden, 'gx', axis=1, tiled=True)]
    pallas_call x0 -> x16, Pallas kernels: none -> 40.1 us  [the longest x3 20.1 us: product(): pl.pallas_call(kernel, grid_spec=pltpu.PrefetchScalarGridSpec(num_scalar_...]
    ppermute x0 -> x29, starting transfers between devices: none -> 36 us  [the longest x7 8.89 us: body(): lax.ppermute(hidden, 'gx', shift(-k, d))]
    dot_general x3 -> x0, matrix products: 22.7 us -> none  [the longest x1 11.2 us: body(): gate_sum = jnp.dot(piece, gate_weight, preferred_element_type=jnp.float32)]
    unnamed x6 -> x24, local copies, waits for them, and re-layouts: 0.27 us -> 8.3 us
    all_to_all x1 -> x0, starting transfers between devices: 7.35 us -> none  [body(): lax.all_to_all(down_weight, 'gx', split_axis=1, concat_axis=0, tiled=True)]
  transfers between devices with their start and end apart: 3 -> 29, of which waited for: 2 -> 11; matrix products, arithmetic and copies ran while one was open for 8% -> 2% of each run, Pallas kernels for 0% -> 16%
where the time goes in v2:
time: 179 us; the launch traced here: 177 us
  waiting for transfers between devices  89.4 us (50%)
  Pallas kernels  40.1 us (22%)
  starting transfers between devices  36 us (20%)
  local copies, waits for them, and re-layouts  8.38 us (5%)
  other arithmetic  2.94 us (2%)
    ppermute x3, waiting for transfers between devices, body(): blocks.append(lax.ppermute(last, 'gx', shift(way)))  23 us
    pallas_call x3, Pallas kernels, product(): pl.pallas_call(kernel, grid_spec=pltpu.PrefetchScalarGridSpec(num_scalar_...  20.1 us
    ppermute x4, waiting for transfers between devices, body(): pieces += [lax.ppermute(h, 'groups', swap(r)) for h in held]  19.3 us
    ppermute x3, waiting for transfers between devices, body(): lax.ppermute(h, 'gx', shift(-k))  17 us
    ppermute x3, waiting for transfers between devices, body(): came = lax.ppermute(sends[0], ('groups', 'gx'), far_flip())  15.3 us
    ppermute x7, waiting for transfers between devices, body(): lax.ppermute(hidden, 'gx', shift(-k, d))  13.2 us
    ppermute x7, starting transfers between devices, body(): lax.ppermute(hidden, 'gx', shift(-k, d))  8.89 us
    pallas_call x2, Pallas kernels, mix(): pl.pallas_call(kernel, out_shape=shape(rows, share * part) if given else...  8.7 us
  transfers between devices with their start and end apart: 29, of which 11 were waited for; matrix products, arithmetic and copies ran while one was open for 2% of the time, Pallas kernels for 16%

profile of v2, /device:TPU:1, one launch (start us, length us, event | category | flops | bytes accessed | tf_op | source)
XLA Modules:
  0.0 177.0 jit_solution(11310138260503035130)
XLA Ops:
  0.0 2.0 %copy-done.7 = bf16[104,16384]{1,0:T(8,128)(2,1)S(1)} copy-done((bf16[104,16384]{1,0:T(8,128)(2,1)S(1)}, bf16[104,16384]{1,0:T(8,128)(2,1)}, u32[]{:S(2)}) %copy-start.7) | copy-done | bytes 3407896
  5.0 2.3 %collective-permute-start = (bf16[528,1024]{1,0:T(8,128)(2,1)}, bf16[528,1024]{1,0:T(8,128)(2,1)}, u32[]{:S(2)}, u32[]{:S(2)}) collective-permute-start(bf16[528,1024]{1,0:T(8,128)(2,1)} %fusion.3.refs_0_), channel_id=1, source_target_pairs={{0,4},{1,5},{2,6},{3,7},{4,8},{5,9},{6,10},{7,11},{8,12},{9,13},{1... | collective-permute-start | bytes 3244040 | tf_op jit(solution)/shard_map/ppermute | solution.py:272
  7.3 2.0 %collective-permute-start.6 = (bf16[528,1024]{1,0:T(8,128)(2,1)}, bf16[528,1024]{1,0:T(8,128)(2,1)}, u32[]{:S(2)}, u32[]{:S(2)}) collective-permute-start(bf16[528,1024]{1,0:T(8,128)(2,1)} %fusion.3.refs_0_), channel_id=1, source_target_pairs={{0,12},{1,13},{2,14},{3,15},{4,0},{5,1},{6,2},{7,3},{8,4},{9,5},{1... | collective-permute-start | bytes 3244040 | tf_op jit(solution)/shard_map/ppermute | solution.py:272
  9.4 1.7 shard_map.60
  12.4 2.7 %shard_map.55 = bf16[4,2,104,1024]{3,2,1,0:T(8,128)(2,1)S(1)} custom-call(s32[7]{0:T(128)S(1)} %stack.31.spot, bf16[104,16384]{1,0:T(8,128)(2,1)S(1)} %bitcast.14, bf16[104,16384]{1,0:T(8,128)(2,1)} %bitcast.18), custom_call_target="tpu_custom_call" | custom-call | bytes 3407872 | tf_op jit(solution)/shard_map/pallas_call | solution.py:203
  20.8 10.2 %collective-permute-done.9.refs_5_ = bf16[2,2,104,1024]{3,2,1,0:T(8,128)(2,1)S(1)} collective-permute-done((bf16[2,2,104,1024]{3,2,1,0:T(8,128)(2,1)S(1)}, bf16[2,2,104,1024]{3,2,1,0:T(8,128)(2,1)S(1)}, u32[]{:S(2)}, u32[]{:S(2)}) %collective-permute-start.9) | collective-permute-done | bytes 852000 | tf_op jit(solution)/shard_map/ppermute | solution.py:319
  34.5 21.5 %collective-permute-done.6.refs_0_ = bf16[528,1024]{1,0:T(8,128)(2,1)} collective-permute-done((bf16[528,1024]{1,0:T(8,128)(2,1)}, bf16[528,1024]{1,0:T(8,128)(2,1)}, u32[]{:S(2)}, u32[]{:S(2)}) %collective-permute-start.6) | collective-permute-done | bytes 1081376 | tf_op jit(solution)/shard_map/ppermute | solution.py:272
  62.3 5.1 %collective-permute-done.4.refs_4_ = bf16[1,2,104,1024]{3,2,1,0:T(8,128)(2,1)S(1)} collective-permute-done((bf16[1,2,104,1024]{3,2,1,0:T(8,128)(2,1)S(1)}, bf16[1,2,104,1024]{3,2,1,0:T(8,128)(2,1)S(1)}, u32[]{:S(2)}, u32[]{:S(2)}) %collective-permute-start.4) | collective-permute-done | bytes 426016 | tf_op jit(solution)/shard_map/ppermute | solution.py:319
  70.0 3.8 %collective-permute-start.5 = (bf16[1,2,104,1024]{3,2,1,0:T(8,128)(2,1)S(1)}, bf16[1,2,104,1024]{3,2,1,0:T(8,128)(2,1)S(1)}, u32[]{:S(2)}, u32[]{:S(2)}) collective-permute-start(bf16[1,2,104,1024]{3,2,1,0:T(8,128)(2,1)S(1)} %collective-permute-done.4.refs_4_), channel_id=1, source_target_pairs={{0,16},{16,0},{1,17},{17,1},{2,18},{18,2},{3,19},{19,3},{4,20},{20... | collective-permute-start | bytes 1277960 | tf_op jit(solution)/shard_map/ppermute | solution.py:320
  73.8 1.5 collective-permute-done.10.refs_6_
  76.6 8.7 %shard_map.62.refs_6_ = f32[832,512]{1,0:T(8,128)S(1)} custom-call(s32[7]{0:T(128)S(1)} %stack.31.spot, bf16[528,1024]{1,0:T(8,128)(2,1)} %fusion.3.refs_0_, bf16[528,1024]{1,0:T(8,128)(2,1)} %collective-permute-done.refs_1_, bf16[104,16384]{1,0:T(8,128)(2,1)} %bitcast.10, bf16[104,16384]{1,0:T(8,128)(2,1)} %bitcast.21, bf16[4,2,104,1024]{3,2,1,0:T(8,128)(2,1)} %copy-done.1, ...), custom_call_target="tpu_custom_call" | custom-call | flops 1744830464 | bytes 3407872 | tf_op jit(solution)/shard_map/pallas_call | solution.py:170
  86.4 2.1 %collective-permute-start.13 = (bf16[2,2,104,512]{3,2,1,0:T(8,128)(2,1)S(1)}, bf16[2,2,104,512]{3,2,1,0:T(8,128)(2,1)S(1)}, u32[]{:S(2)}, u32[]{:S(2)}) collective-permute-start(bf16[2,2,104,512]{3,2,1,0:T(8,128)(2,1)S(1)} %get-tuple-element.18), channel_id=1, source_target_pairs={{0,4},{1,5},{2,6},{3,7},{4,8},{5,9},{6,10},{7,11},{8,12},{9,13},{1... | collective-permute-start | bytes 1277960 | tf_op jit(solution)/shard_map/ppermute | solution.py:310
  88.6 8.3 %collective-permute-done.12.refs_7_.refs_1_ = bf16[2,2,104,512]{3,2,1,0:T(8,128)(2,1)S(1)} collective-permute-done((bf16[2,2,104,512]{3,2,1,0:T(8,128)(2,1)S(1)}, bf16[2,2,104,512]{3,2,1,0:T(8,128)(2,1)S(1)}, u32[]{:S(2)}, u32[]{:S(2)}) %collective-permute-start.12) | collective-permute-done | bytes 426016 | tf_op jit(solution)/shard_map/ppermute | solution.py:310
  98.3 6.2 %shard_map.63.refs_6_ = f32[832,512]{1,0:T(8,128)S(1)} custom-call(s32[7]{0:T(128)S(1)} %stack.31.spot, bf16[528,1024]{1,0:T(8,128)(2,1)} %collective-permute-done.6.refs_0_, bf16[104,16384]{1,0:T(8,128)(2,1)} %bitcast.11, bf16[104,16384]{1,0:T(8,128)(2,1)} %bitcast.22, bf16[4,2,104,1024]{3,2,1,0:T(8,128)(2,1)S(1)} %copy-done.2, ...), custom_call_target="tpu_custom_call" | custom-call | flops 872415232 | bytes 1703936 | tf_op jit(solution)/shard_map/pallas_call | solution.py:170
  105.8 5.2 %shard_map.64.refs_0_ = f32[832,512]{1,0:T(8,128)S(1)} custom-call(s32[7]{0:T(128)S(1)} %stack.31.spot, bf16[528,1024]{1,0:T(8,128)(2,1)S(1)} %collective-permute-done.1.refs_0_, bf16[104,16384]{1,0:T(8,128)(2,1)} %bitcast.12, bf16[104,16384]{1,0:T(8,128)(2,1)} %bitcast.23, bf16[4,2,104,1024]{3,2,1,0:T(8,128)(2,1)S(1)} %copy-done.2, ...), custom_call_target="tpu_custom_call" | custom-call | flops 872415232 | bytes 1703936 | tf_op jit(solution)/shard_map/pallas_call | solution.py:170
  114.5 8.6 %collective-permute-done.16.refs_3_.refs_5_ = bf16[2,2,104,512]{3,2,1,0:T(8,128)(2,1)S(1)} collective-permute-done((bf16[2,2,104,512]{3,2,1,0:T(8,128)(2,1)S(1)}, bf16[2,2,104,512]{3,2,1,0:T(8,128)(2,1)S(1)}, u32[]{:S(2)}, u32[]{:S(2)}) %collective-permute-start.16) | collective-permute-done | bytes 426016 | tf_op jit(solution)/shard_map/ppermute | solution.py:313
  124.6 8.7 %collective-permute-done.19.refs_4_.refs_2_ = bf16[2,2,104,512]{3,2,1,0:T(8,128)(2,1)S(1)} collective-permute-done((bf16[2,2,104,512]{3,2,1,0:T(8,128)(2,1)S(1)}, bf16[2,2,104,512]{3,2,1,0:T(8,128)(2,1)S(1)}, u32[]{:S(2)}, u32[]{:S(2)}) %collective-permute-start.19) | collective-permute-done | bytes 426016 | tf_op jit(solution)/shard_map/ppermute | solution.py:310
  134.8 2.8 %collective-permute-start.21 = (bf16[104,512]{1,0:T(8,128)(2,1)S(1)}, bf16[104,512]{1,0:T(8,128)(2,1)S(1)}, u32[]{:S(2)}, u32[]{:S(2)}) collective-permute-start(bf16[104,512]{1,0:T(8,128)(2,1)S(1)} %shard_map.67.refs_0_), channel_id=1, source_target_pairs={{0,12},{1,13},{2,14},{3,15},{4,0},{5,1},{6,2},{7,3},{8,4},{9,5},{1... | collective-permute-start | bytes 319496 | tf_op jit(solution)/shard_map/ppermute | solution.py:340
  137.6 3.3 %collective-permute-start.24 = (bf16[104,512]{1,0:T(8,128)(2,1)S(1)}, bf16[104,512]{1,0:T(8,128)(2,1)S(1)}, u32[]{:S(2)}, u32[]{:S(2)}) collective-permute-start(bf16[104,512]{1,0:T(8,128)(2,1)S(1)} %shard_map.67.refs_0_), channel_id=1, source_target_pairs={{0,10},{1,11},{2,8},{3,9},{4,14},{5,15},{6,12},{7,13},{8,2},{9,3},... | collective-permute-start | bytes 319496 | tf_op jit(solution)/shard_map/ppermute | solution.py:340
  142.4 1.8 %collective-permute-done.23.refs_4_ = bf16[104,512]{1,0:T(8,128)(2,1)S(1)} collective-permute-done((bf16[104,512]{1,0:T(8,128)(2,1)S(1)}, bf16[104,512]{1,0:T(8,128)(2,1)S(1)}, u32[]{:S(2)}, u32[]{:S(2)}) %collective-permute-start.23) | collective-permute-done | bytes 106528 | tf_op jit(solution)/shard_map/ppermute | solution.py:340
  144.2 11.4 %collective-permute-done.24.refs_5_ = bf16[104,512]{1,0:T(8,128)(2,1)S(1)} collective-permute-done((bf16[104,512]{1,0:T(8,128)(2,1)S(1)}, bf16[104,512]{1,0:T(8,128)(2,1)S(1)}, u32[]{:S(2)}, u32[]{:S(2)}) %collective-permute-start.24) | collective-permute-done | bytes 106528 | tf_op jit(solution)/shard_map/ppermute | solution.py:340
  157.6 10.7 %collective-permute-done.28.refs_6_ = bf16[2,2,104,512]{3,2,1,0:T(8,128)(2,1)S(1)} collective-permute-done((bf16[2,2,104,512]{3,2,1,0:T(8,128)(2,1)S(1)}, bf16[2,2,104,512]{3,2,1,0:T(8,128)(2,1)S(1)}, u32[]{:S(2)}, u32[]{:S(2)}) %collective-permute-start.28) | collective-permute-done | bytes 426016 | tf_op jit(solution)/shard_map/ppermute | solution.py:313
  168.3 3.7 %shard_map.69.refs_8_ = f32[2,512,512]{2,1,0:T(8,128)} custom-call(bf16[4,2,104,512]{3,2,1,0:T(8,128)(2,1)S(1)} %shard_map.68.side, bf16[2,2,104,512]{3,2,1,0:T(8,128)(2,1)S(1)} %get-tuple-element.16.refs_7_.refs_0_, bf16[2,2,104,512]{3,2,1,0:T(8,128)(2,1)S(1)} %collective-permute-done.12.refs_7_.refs_1_, ...), custom_call_target="tpu_custom_call" | custom-call | flops 872415232 | bytes 2555904 | tf_op jit(solution)/shard_map/pallas_call | solution.py:243
  172.0 5.0 %shard_map.70 = bf16[512,1024]{1,0:T(8,128)(2,1)} custom-call(bf16[4,2,104,512]{3,2,1,0:T(8,128)(2,1)S(1)} %collective-permute-done.27.side, bf16[2,2,104,512]{3,2,1,0:T(8,128)(2,1)S(1)} %get-tuple-element.16.refs_7_.refs_0_, bf16[2,2,104,512]{3,2,1,0:T(8,128)(2,1)S(1)} %collective-permute-done.12.refs_7_.refs_1_, ...), custom_call_target="tpu_custom_call" | custom-call | flops 872415232 | bytes 2555904 | tf_op jit(solution)/shard_map/pallas_call | solution.py:243
  (83 shorter events, 37.5 us)
Async XLA Ops:
  3.0 13.5 %collective-permute-start.3 = (bf16[2,4,104,512]{3,2,1,0:T(8,128)(2,1)}, bf16[2,4,104,512]{3,2,1,0:T(8,128)(2,1)}, u32[]{:S(2)}, u32[]{:S(2)}) collective-permute-start(bf16[2,4,104,512]{3,2,1,0:T(8,128)(2,1)} %get-tuple-element.15), channel_id=1, source_target_pairs={{0,1},{1,0},{2,3},{3,2},{4,5},{5,4},{6,7},{7,6},{8,9},{9,8},{10,11... | collective-permute-start | bytes 2555912 | tf_op jit(solution)/shard_map/ppermute | solution.py:290
  5.0 28.5 %collective-permute-start = (bf16[528,1024]{1,0:T(8,128)(2,1)}, bf16[528,1024]{1,0:T(8,128)(2,1)}, u32[]{:S(2)}, u32[]{:S(2)}) collective-permute-start(bf16[528,1024]{1,0:T(8,128)(2,1)} %fusion.3.refs_0_), channel_id=1, source_target_pairs={{0,4},{1,5},{2,6},{3,7},{4,8},{5,9},{6,10},{7,11},{8,12},{9,13},{1... | collective-permute-start | bytes 3244040 | tf_op jit(solution)/shard_map/ppermute | solution.py:272
  7.3 48.7 %collective-permute-start.6 = (bf16[528,1024]{1,0:T(8,128)(2,1)}, bf16[528,1024]{1,0:T(8,128)(2,1)}, u32[]{:S(2)}, u32[]{:S(2)}) collective-permute-start(bf16[528,1024]{1,0:T(8,128)(2,1)} %fusion.3.refs_0_), channel_id=1, source_target_pairs={{0,12},{1,13},{2,14},{3,15},{4,0},{5,1},{6,2},{7,3},{8,4},{9,5},{1... | collective-permute-start | bytes 3244040 | tf_op jit(solution)/shard_map/ppermute | solution.py:272
  11.1 19.9 %collective-permute-start.9 = (bf16[2,2,104,1024]{3,2,1,0:T(8,128)(2,1)S(1)}, bf16[2,2,104,1024]{3,2,1,0:T(8,128)(2,1)S(1)}, u32[]{:S(2)}, u32[]{:S(2)}) collective-permute-start(bf16[2,2,104,1024]{3,2,1,0:T(8,128)(2,1)S(1)} %shard_map.60), channel_id=1, source_target_pairs={{0,2},{1,3},{2,0},{3,1},{4,6},{5,7},{6,4},{7,5},{8,10},{9,11},{10,... | collective-permute-start | bytes 2555912 | tf_op jit(solution)/shard_map/ppermute | solution.py:319
  15.2 54.9 %collective-permute-start.2 = (bf16[4,2,104,1024]{3,2,1,0:T(8,128)(2,1)S(1)}, bf16[4,2,104,1024]{3,2,1,0:T(8,128)(2,1)S(1)}, u32[]{:S(2)}, u32[]{:S(2)}) collective-permute-start(bf16[4,2,104,1024]{3,2,1,0:T(8,128)(2,1)S(1)} %shard_map.55), channel_id=1, source_target_pairs={{0,1},{1,0},{2,3},{3,2},{4,5},{5,4},{6,7},{7,6},{8,9},{9,8},{10,11... | collective-permute-start | bytes 5111816 | tf_op jit(solution)/shard_map/ppermute | solution.py:323
  17.7 39.5 %collective-permute-start.11 = (bf16[2,4,104,512]{3,2,1,0:T(8,128)(2,1)S(1)}, bf16[2,4,104,512]{3,2,1,0:T(8,128)(2,1)S(1)}, u32[]{:S(2)}, u32[]{:S(2)}) collective-permute-start(bf16[2,4,104,512]{3,2,1,0:T(8,128)(2,1)S(1)} %shard_map.57.refs_2_), channel_id=1, source_target_pairs={{0,2},{1,3},{2,0},{3,1},{4,6},{5,7},{6,4},{7,5},{8,10},{9,11},{10,... | collective-permute-start | bytes 2555912 | tf_op jit(solution)/shard_map/ppermute | solution.py:297
  31.0 31.0 %collective-permute-start.7 = (bf16[1,2,104,1024]{3,2,1,0:T(8,128)(2,1)S(1)}, bf16[1,2,104,1024]{3,2,1,0:T(8,128)(2,1)S(1)}, u32[]{:S(2)}, u32[]{:S(2)}) collective-permute-start(bf16[1,2,104,1024]{3,2,1,0:T(8,128)(2,1)S(1)} %shard_map.59), channel_id=1, source_target_pairs={{0,2},{1,3},{2,0},{3,1},{4,6},{5,7},{6,4},{7,5},{8,10},{9,11},{10,... | collective-permute-start | bytes 1277960 | tf_op jit(solution)/shard_map/ppermute | solution.py:319
  33.5 33.9 %collective-permute-start.4 = (bf16[1,2,104,1024]{3,2,1,0:T(8,128)(2,1)S(1)}, bf16[1,2,104,1024]{3,2,1,0:T(8,128)(2,1)S(1)}, u32[]{:S(2)}, u32[]{:S(2)}) collective-permute-start(bf16[1,2,104,1024]{3,2,1,0:T(8,128)(2,1)S(1)} %shard_map.58), channel_id=1, source_target_pairs={{0,2},{1,3},{2,0},{3,1},{4,6},{5,7},{6,4},{7,5},{8,10},{9,11},{10,... | collective-permute-start | bytes 1277960 | tf_op jit(solution)/shard_map/ppermute | solution.py:319
  56.0 19.4 %collective-permute-start.10 = (bf16[2,2,104,1024]{3,2,1,0:T(8,128)(2,1)S(1)}, bf16[2,2,104,1024]{3,2,1,0:T(8,128)(2,1)S(1)}, u32[]{:S(2)}, u32[]{:S(2)}) collective-permute-start(bf16[2,2,104,1024]{3,2,1,0:T(8,128)(2,1)S(1)} %collective-permute-done.9.refs_5_), channel_id=1, source_target_pairs={{0,16},{16,0},{1,17},{17,1},{2,18},{18,2},{3,19},{19,3},{4,20},{20... | collective-permute-start | bytes 2555912 | tf_op jit(solution)/shard_map/ppermute | solution.py:320
  58.1 47.6 %collective-permute-start.1 = (bf16[528,1024]{1,0:T(8,128)(2,1)}, bf16[528,1024]{1,0:T(8,128)(2,1)S(1)}, u32[]{:S(2)}, u32[]{:S(2)}) collective-permute-start(bf16[528,1024]{1,0:T(8,128)(2,1)} %collective-permute-done.refs_1_), channel_id=1, source_target_pairs={{0,4},{1,5},{2,6},{3,7},{4,8},{5,9},{6,10},{7,11},{8,12},{9,13},{1... | collective-permute-start | bytes 3244040 | tf_op jit(solution)/shard_map/ppermute | solution.py:272
  62.0 24.5 %collective-permute-start.8 = (bf16[1,2,104,1024]{3,2,1,0:T(8,128)(2,1)S(1)}, bf16[1,2,104,1024]{3,2,1,0:T(8,128)(2,1)S(1)}, u32[]{:S(2)}, u32[]{:S(2)}) collective-permute-start(bf16[1,2,104,1024]{3,2,1,0:T(8,128)(2,1)S(1)} %collective-permute-done.7.refs_4_), channel_id=1, source_target_pairs={{0,16},{16,0},{1,17},{17,1},{2,18},{18,2},{3,19},{19,3},{4,20},{20... | collective-permute-start | bytes 1277960 | tf_op jit(solution)/shard_map/ppermute | solution.py:320
  67.4 29.4 %collective-permute-start.12 = (bf16[2,2,104,512]{3,2,1,0:T(8,128)(2,1)S(1)}, bf16[2,2,104,512]{3,2,1,0:T(8,128)(2,1)S(1)}, u32[]{:S(2)}, u32[]{:S(2)}) collective-permute-start(bf16[2,2,104,512]{3,2,1,0:T(8,128)(2,1)S(1)} %get-tuple-element.17), channel_id=1, source_target_pairs={{0,12},{1,13},{2,14},{3,15},{4,0},{5,1},{6,2},{7,3},{8,4},{9,5},{1... | collective-permute-start | bytes 1277960 | tf_op jit(solution)/shard_map/ppermute | solution.py:310
  70.0 35.7 %collective-permute-start.5 = (bf16[1,2,104,1024]{3,2,1,0:T(8,128)(2,1)S(1)}, bf16[1,2,104,1024]{3,2,1,0:T(8,128)(2,1)S(1)}, u32[]{:S(2)}, u32[]{:S(2)}) collective-permute-start(bf16[1,2,104,1024]{3,2,1,0:T(8,128)(2,1)S(1)} %collective-permute-done.4.refs_4_), channel_id=1, source_target_pairs={{0,16},{16,0},{1,17},{17,1},{2,18},{18,2},{3,19},{19,3},{4,20},{20... | collective-permute-start | bytes 1277960 | tf_op jit(solution)/shard_map/ppermute | solution.py:320
  75.3 30.4 %collective-permute-start.14 = (bf16[2,2,104,512]{3,2,1,0:T(8,128)(2,1)S(1)}, bf16[2,2,104,512]{3,2,1,0:T(8,128)(2,1)S(1)}, u32[]{:S(2)}, u32[]{:S(2)}) collective-permute-start(bf16[2,2,104,512]{3,2,1,0:T(8,128)(2,1)S(1)} %get-tuple-element.16.refs_7_.refs_0_), channel_id=1, source_target_pairs={{16,0},{0,16},{17,1},{1,17},{18,2},{2,18},{19,3},{3,19},{20,4},{4,... | collective-permute-start | bytes 1277960 | tf_op jit(solution)/shard_map/ppermute | solution.py:313
  86.4 19.3 %collective-permute-start.13 = (bf16[2,2,104,512]{3,2,1,0:T(8,128)(2,1)S(1)}, bf16[2,2,104,512]{3,2,1,0:T(8,128)(2,1)S(1)}, u32[]{:S(2)}, u32[]{:S(2)}) collective-permute-start(bf16[2,2,104,512]{3,2,1,0:T(8,128)(2,1)S(1)} %get-tuple-element.18), channel_id=1, source_target_pairs={{0,4},{1,5},{2,6},{3,7},{4,8},{5,9},{6,10},{7,11},{8,12},{9,13},{1... | collective-permute-start | bytes 1277960 | tf_op jit(solution)/shard_map/ppermute | solution.py:310
  111.0 12.1 %collective-permute-start.15 = (bf16[432,512]{1,0:T(8,128)(2,1)S(1)}, bf16[432,512]{1,0:T(8,128)(2,1)S(1)}, u32[]{:S(2)}, u32[]{:S(2)}) collective-permute-start(bf16[432,512]{1,0:T(8,128)(2,1)S(1)} %shard_map.65), channel_id=1, source_target_pairs={{0,1},{1,0},{2,3},{3,2},{4,5},{5,4},{6,7},{7,6},{8,9},{9,8},{10,11... | collective-permute-start | bytes 1327112 | tf_op jit(solution)/shard_map/ppermute | solution.py:333
  111.7 11.4 %collective-permute-start.16 = (bf16[2,2,104,512]{3,2,1,0:T(8,128)(2,1)S(1)}, bf16[2,2,104,512]{3,2,1,0:T(8,128)(2,1)S(1)}, u32[]{:S(2)}, u32[]{:S(2)}) collective-permute-start(bf16[2,2,104,512]{3,2,1,0:T(8,128)(2,1)S(1)} %collective-permute-done.12.refs_7_.refs_1_), channel_id=1, source_target_pairs={{16,0},{0,16},{17,1},{1,17},{18,2},{2,18},{19,3},{3,19},{20,4},{4,... | collective-permute-start | bytes 1277960 | tf_op jit(solution)/shard_map/ppermute | solution.py:313
  112.0 21.3 %collective-permute-start.19 = (bf16[2,2,104,512]{3,2,1,0:T(8,128)(2,1)S(1)}, bf16[2,2,104,512]{3,2,1,0:T(8,128)(2,1)S(1)}, u32[]{:S(2)}, u32[]{:S(2)}) collective-permute-start(bf16[2,2,104,512]{3,2,1,0:T(8,128)(2,1)S(1)} %get-tuple-element.22), channel_id=1, source_target_pairs={{0,8},{1,9},{2,10},{3,11},{4,12},{5,13},{6,14},{7,15},{8,0},{9,1},... | collective-permute-start | bytes 1277960 | tf_op jit(solution)/shard_map/ppermute | solution.py:310
  113.3 20.1 %collective-permute-start.18 = (bf16[2,2,104,512]{3,2,1,0:T(8,128)(2,1)S(1)}, bf16[2,2,104,512]{3,2,1,0:T(8,128)(2,1)S(1)}, u32[]{:S(2)}, u32[]{:S(2)}) collective-permute-start(bf16[2,2,104,512]{3,2,1,0:T(8,128)(2,1)S(1)} %collective-permute-done.13.refs_7_.refs_3_), channel_id=1, source_target_pairs={{16,0},{0,16},{17,1},{1,17},{18,2},{2,18},{19,3},{3,19},{20,4},{4,... | collective-permute-start | bytes 1277960 | tf_op jit(solution)/shard_map/ppermute | solution.py:313
  137.6 18.0 %collective-permute-start.24 = (bf16[104,512]{1,0:T(8,128)(2,1)S(1)}, bf16[104,512]{1,0:T(8,128)(2,1)S(1)}, u32[]{:S(2)}, u32[]{:S(2)}) collective-permute-start(bf16[104,512]{1,0:T(8,128)(2,1)S(1)} %shard_map.67.refs_0_), channel_id=1, source_target_pairs={{0,10},{1,11},{2,8},{3,9},{4,14},{5,15},{6,12},{7,13},{8,2},{9,3},... | collective-permute-start | bytes 319496 | tf_op jit(solution)/shard_map/ppermute | solution.py:340
  140.9 14.7 %collective-permute-start.25 = (bf16[104,512]{1,0:T(8,128)(2,1)S(1)}, bf16[104,512]{1,0:T(8,128)(2,1)S(1)}, u32[]{:S(2)}, u32[]{:S(2)}) collective-permute-start(bf16[104,512]{1,0:T(8,128)(2,1)S(1)} %shard_map.67.refs_0_), channel_id=1, source_target_pairs={{0,4},{1,5},{2,6},{3,7},{4,8},{5,9},{6,10},{7,11},{8,12},{9,13},{1... | collective-permute-start | bytes 319496 | tf_op jit(solution)/shard_map/ppermute | solution.py:340
  142.3 13.2 %collective-permute-start.26 = (bf16[104,512]{1,0:T(8,128)(2,1)S(1)}, bf16[104,512]{1,0:T(8,128)(2,1)S(1)}, u32[]{:S(2)}, u32[]{:S(2)}) collective-permute-start(bf16[104,512]{1,0:T(8,128)(2,1)S(1)} %shard_map.67.refs_0_), channel_id=1, source_target_pairs={{0,6},{1,7},{2,4},{3,5},{4,10},{5,11},{6,8},{7,9},{8,14},{9,15},{1... | collective-permute-start | bytes 319496 | tf_op jit(solution)/shard_map/ppermute | solution.py:340
  155.6 16.4 %collective-permute-start.27 = (bf16[4,2,104,512]{3,2,1,0:T(8,128)(2,1)S(1)}, bf16[4,2,104,512]{3,2,1,0:T(8,128)(2,1)S(1)}, u32[]{:S(2)}, u32[]{:S(2)}) collective-permute-start(bf16[4,2,104,512]{3,2,1,0:T(8,128)(2,1)S(1)} %shard_map.68.side), channel_id=1, source_target_pairs={{0,1},{1,0},{2,3},{3,2},{4,5},{5,4},{6,7},{7,6},{8,9},{9,8},{10,11... | collective-permute-start | bytes 2555912 | tf_op jit(solution)/shard_map/ppermute | solution.py:346
  156.9 11.4 %collective-permute-start.28 = (bf16[2,2,104,512]{3,2,1,0:T(8,128)(2,1)S(1)}, bf16[2,2,104,512]{3,2,1,0:T(8,128)(2,1)S(1)}, u32[]{:S(2)}, u32[]{:S(2)}) collective-permute-start(bf16[2,2,104,512]{3,2,1,0:T(8,128)(2,1)S(1)} %collective-permute-done.19.refs_4_.refs_2_), channel_id=1, source_target_pairs={{16,0},{0,16},{17,1},{1,17},{18,2},{2,18},{19,3},{3,19},{20,4},{4,... | collective-permute-start | bytes 1277960 | tf_op jit(solution)/shard_map/ppermute | solution.py:313
  (17 other events, 67.1 us)

commit v3 on v2

--- a/solution.py
+++ b/solution.py
@@ -13,7 +13,7 @@
 ANY = pl.BlockSpec(memory_space=pl.ANY)
 VMEM = pl.BlockSpec(memory_space=pltpu.VMEM)
 PARAMS = pltpu.CompilerParams(vmem_limit_bytes=48 * 1024 * 1024)
-HEAVY = 1
+HEAVY = 20
 EXTRA = 16
 
 
@@ -21,8 +21,8 @@
     return jax.ShapeDtypeStruct(dims, dtype)
 
 
-def cost(size, flops=0):
-    return pl.CostEstimate(flops=HEAVY * flops, bytes_accessed=HEAVY * size, transcendentals=0)
+def cost(size, flops=0, heavy=HEAVY):
+    return pl.CostEstimate(flops=int(heavy * flops), bytes_accessed=int(heavy * size), transcendentals=0)
 
 
 def move(moves, outs, *operands, after=()):
@@ -36,7 +36,7 @@
         in_specs=[VMEM] * len(operands) + [ANY] * len(after),
         out_specs=[VMEM] * len(outs),
         compiler_params=PARAMS,
-        cost_estimate=cost(4 * sum(o.size for o in outs)),
+        cost_estimate=cost(4 * sum(o.size for o in outs), 0, 20),
     )(*operands, *after)
 
 
@@ -63,7 +63,7 @@
         in_specs=[VMEM] * len(operands) + [ANY] * len(after),
         out_specs=[VMEM] * len(outs),
         compiler_params=PARAMS,
-        cost_estimate=cost(4 * sum(o.size for o in outs)),
+        cost_estimate=cost(4 * sum(o.size for o in outs), 0, 0),
     )(*operands, *after)
 
 
@@ -101,16 +101,23 @@
 
 
 def arrivals(planes):
-    order = [0]
-    for s in range(1, planes // 2 + 1):
-        order += [s] if 2 * s == planes else [s, planes - s]
-    return order
+    table = []
+    for p in range(planes):
+        row = [(0, p)]
+        for s in range(1, planes):
+            if p >= s:
+                row.append((2 * s - 1, p - s))
+            if p + s < planes:
+                row.append((2 * s, p + s))
+        table.append(row)
+    return table
 
 
 def make_body(n, groups):
     planes = n // 4
-    order = arrivals(planes)
-    cuts = [range(0, planes // 2), *[range(j, j + 1) for j in range(planes // 2, planes)]] if planes <= 4 else [range(0, planes // 2), range(planes // 2, planes)]
+    table = arrivals(planes)
+    BLOCK, ARRAY = 3, 3 + planes
+    cuts = [range(0, planes // 2), range(planes // 2, planes)]
     paired = groups % 2 == 0
 
     def at(p, q):
@@ -121,6 +128,10 @@
 
     def shift(k, d=0):
         return [(at(p, q), at(p + k, q ^ d)) for p in range(planes) for q in range(4)]
+
+    def line(s, way):
+        senders = range(s - 1, planes - 1) if way > 0 else range(1, planes - s + 1)
+        return [(at(p, q), at(p + way, q)) for p in senders for q in range(4)]
 
     def far_flip():
         return [(g * n + i, g * n + j) for g in range(groups) for i, j in flip(2 + g % 2)]
@@ -136,43 +147,49 @@
         width = blocks[0].shape[1]
         _, two, hid, _ = near.shape
         first, count = js[0], len(js)
+        lists = [sorted(set(row[j][0] for row in table)) for j in js]
+        arrays = sorted(set(sum(lists, [])))
         given = [] if total is None else [total]
 
         def kernel(spot, *refs):
-            sources, refs = refs[:count], refs[count:]
+            sources, refs = refs[: len(arrays)], refs[len(arrays) :]
             own_gate, own_up, near, far0, far1 = refs[:5]
             out, xs, sems = refs[-3:]
             i = pl.program_id(0)
-            copies = [
-                pltpu.make_async_copy(x.at[pl.ds(0, rows)], xs.at[k], sems.at[k]) for k, x in enumerate(sources)
-            ]
+
+            def bring(array, k):
+                return pltpu.make_async_copy(sources[arrays.index(array)].at[pl.ds(0, rows)], xs.at[k], sems.at[k])
 
             @pl.when(i == 0)
             def _():
-                for copy in copies:
-                    copy.start()
+                for k, choices in enumerate(lists):
+                    for array in choices:
+                        pl.when(spot[ARRAY + first + k] == array)(bring(array, k).start)
                 out[...] = refs[5][...] if given else jnp.zeros_like(out)
 
-            for k, copy in enumerate(copies):
-                pl.when(i == k)(copy.wait)
+            for k, choices in enumerate(lists):
+                pl.when(i == k)(bring(choices[0], k).wait)
 
             x = xs[i]
             weights = [own_gate[...], own_up[...]] + [w[0, j] for w in (near, far0, far1) for j in range(2)]
-            for b, block in enumerate(weights):
-                term = lax.dot_general(block, x, (((1,), (1,)), ((), ())), preferred_element_type=F32)
-                d = b // 2 if b < 4 else 2 + lax.bitwise_xor(b // 2 - 2, spot[2])
-                out[pl.ds(pl.multiple_of((d * 2 + b % 2) * hid, 8), hid), :] += term
+            term = lax.dot_general(
+                jnp.concatenate(weights), x, (((1,), (1,)), ((), ())), preferred_element_type=F32
+            )
+            out[pl.ds(0, 4 * hid), :] += term[: 4 * hid]
+            for b in range(2):
+                d = 2 + lax.bitwise_xor(b, spot[2])
+                out[pl.ds(pl.multiple_of(d * 2 * hid, 8), 2 * hid), :] += term[(4 + 2 * b) * hid : (6 + 2 * b) * hid]
 
         near_block = pl.BlockSpec((1, two, hid, width), lambda i, spot: (i + first, 0, 0, 0))
         far_block = pl.BlockSpec((1, two, hid, width), lambda i, spot: (i, 0, 0, 0))
-        mine = pl.BlockSpec((hid, width), lambda i, spot: (0, spot[3 + first + i] * 4 + spot[1]))
+        mine = pl.BlockSpec((hid, width), lambda i, spot: (0, spot[BLOCK + first + i] * 4 + spot[1]))
         whole = pl.BlockSpec((8 * hid, rows), lambda i, spot: (0, 0))
         return pl.pallas_call(
             kernel,
             grid_spec=pltpu.PrefetchScalarGridSpec(
                 num_scalar_prefetch=1,
                 grid=(count,),
-                in_specs=[ANY] * count
+                in_specs=[ANY] * len(arrays)
                 + [mine, mine, near_block, far_block, far_block]
                 + [whole] * len(given)
                 + [ANY] * len(after),
@@ -181,8 +198,8 @@
             ),
             out_shape=shape(8 * hid, rows, dtype=F32),
             compiler_params=PARAMS,
-            cost_estimate=cost(16 * hid * width * count, 16 * hid * rows * width * count),
-        )(spot, *[blocks[j] for j in js], *own, near, *far, *given, *after)
+            cost_estimate=cost(16 * hid * width * count, 16 * hid * rows * width * count, 1),
+        )(spot, *[blocks[m] for m in arrays], *own, near, *far, *given, *after)
 
     def cut(spot, gate_t, up_t, width, ds, first, count, after=()):
         hid = gate_t.shape[0]
@@ -196,7 +213,7 @@
         def taken(d):
             def index(s, spot):
                 other = lax.bitwise_xor(spot[1], d + spot[2] if d == 2 and paired else d)
-                return 0, spot[3 + first + s] * 4 + other
+                return 0, spot[BLOCK + first + s] * 4 + other
 
             return pl.BlockSpec((hid, width), index)
 
@@ -210,7 +227,7 @@
             ),
             out_shape=[shape(count, 2, hid, width)] * len(ds),
             compiler_params=PARAMS,
-            cost_estimate=cost(8 * len(ds) * count * hid * width),
+            cost_estimate=cost(8 * len(ds) * count * hid * width, 0, 20),
         )(spot, *[gate_t, up_t] * len(ds), *after)
 
     def mix(side, pieces, share, dc, total=None):
@@ -222,29 +239,29 @@
         def kernel(side, *refs):
             out = refs[-1]
             g = lax.axis_index("groups")
+            left = jnp.concatenate([side[k, dy] for k in range(planes) for dy in range(2)])
             for r in range(share):
-                sums = refs[-2][r] if given else None
-                for k in range(planes):
-                    for dy in range(2):
-                        term = lax.dot_general(
-                            side[k, dy],
-                            refs[r * planes + k][dy, dc],
-                            (((0,), (0,)), ((), ())),
-                            preferred_element_type=F32,
-                        )
-                        sums = term if sums is None else sums + term
+                held = refs[r * planes : (r + 1) * planes]
+                right = jnp.concatenate([h[dy, 0] for h in held for dy in range(2)])
+                sums = lax.dot_general(left, right, (((0,), (0,)), ((), ())), preferred_element_type=F32)
                 if not given:
                     out[r] = sums
-                elif share == 1:
-                    out[...] = sums.astype(BF)
+                    continue
+                sums = (refs[-2][r] + sums).astype(BF)
+                if share == 1:
+                    out[...] = sums
                 else:
-                    out[:, pl.ds(pl.multiple_of((g + r) % share * part, part), part)] = sums.astype(BF)
-
+                    out[:, pl.ds(pl.multiple_of((g + r) % share * part, part), part)] = sums
+
+        half = pl.BlockSpec((2, 1, hid, part), lambda i: (0, dc, 0, 0))
+        full = [pl.BlockSpec(a.shape, functools.partial(lambda n, i: (0,) * n, a.ndim)) for a in (side, *given)]
+        out_shape = (rows, share * part) if given else (share, rows, part)
         return pl.pallas_call(
             kernel,
-            out_shape=shape(rows, share * part) if given else shape(share, rows, part, dtype=F32),
-            in_specs=[VMEM] * (1 + len(pieces) + len(given)),
-            out_specs=VMEM,
+            grid=(1,),
+            out_shape=shape(*out_shape, dtype=BF if given else F32),
+            in_specs=full[:1] + [half] * len(pieces) + full[1:],
+            out_specs=pl.BlockSpec(out_shape, lambda i: (0,) * len(out_shape)),
             compiler_params=PARAMS,
             cost_estimate=cost(n * hid * (rows + share * part), rows * n * hid * share * part),
         )(side, *pieces, *given)
@@ -258,7 +275,8 @@
         me = lax.axis_index("gx")
         plane, quad = me // 4, me % 4
         half = lax.axis_index("groups") % 2 if paired else jnp.int32(0)
-        spot = jnp.stack([plane, quad, half] + [lax.rem(plane + planes - s, planes) for s in order])
+        turns = jnp.array([[p for _, p in row] + [m for m, _ in row] for row in table], jnp.int32)
+        spot = jnp.concatenate([jnp.stack([plane, quad, half]), lax.dynamic_index_in_dim(turns, plane, 0, keepdims=False)])
 
         values = tokens.astype(F32)
         squares = split(jnp.sum(values * values, axis=1)[None, :])
@@ -266,10 +284,9 @@
         extra = jnp.concatenate([squares[:, i : i + lanes] for i in range(0, rows, lanes)])
         scaled = (values * gain[None, :]).astype(BF)
         blocks = [jnp.concatenate([scaled, jnp.pad(extra, ((0, 0), (0, width - lanes)))])]
-        for s in order[1:]:
-            way = 1 if 2 * s <= planes else -1
-            last = blocks[0] if len(blocks) < 3 else blocks[-2]
-            blocks.append(lax.ppermute(last, "gx", shift(way)))
+        for s in range(1, planes):
+            for way in (1, -1):
+                blocks.append(lax.ppermute(blocks[0] if s == 1 else blocks[-2], "gx", line(s, way)))
         parts = [b[rows + i : rows + i + EXTRA, :lanes] for b in blocks for i in range(0, len(extra), EXTRA)]
         parts = [jnp.concatenate([joined(p) for p in parts[i :: len(extra) // EXTRA]]) for i in range(len(extra) // EXTRA)]
         total = jnp.concatenate([jnp.sum(p, axis=0, keepdims=True) for p in parts], axis=1)
@@ -293,43 +310,46 @@
             _, quad = place()
             return [(given[dc], lax.bitwise_xor(quad // 2, 1), outs[0], dc) for dc in range(2)]
 
-        send = move(second_moves, [shape(2, planes, hid, part)], keep, came)[0]
+        send = move(second_moves, [shape(2, planes, hid, part)], keep, came, after=(blocks[0],))[0]
         across = lax.ppermute(send, "gx", flip(2))
 
-        def third_moves(given, outs):
+        far = []
+        for i, js in enumerate(cuts):
+            sends = cut(spot, *own, width, (2,) if paired else (2, 3), js[0], len(js), after=((send,) if far else (blocks[0],)))
+            if paired:
+                brought = lax.ppermute(sends[0], ("groups", "gx"), far_flip())
+                far.append((brought, lax.ppermute(brought, "groups", [(i, i ^ 1) for i in range(groups)])))
+            else:
+                far.append(tuple(lax.ppermute(w, "gx", flip(d)) for d, w in zip((2, 3), sends)))
+        near = lax.ppermute(cut(spot, *own, width, (1,), 0, planes, after=(blocks[0],))[0], "gx", flip(1))
+
+        sums = product(spot, rows, blocks, own, near, far[0], cuts[0])
+
+
+        def third_moves(ks, given, outs):
             plane, quad = place()
             moves = []
-            for k in range(planes):
+            for i, k in enumerate(ks):
                 p = lax.rem(plane + planes - k, planes)
                 for dc in range(2):
-                    moves.append((given[dc], (quad // 2, p), outs[k], (0, dc)))
-                    moves.append((given[2], (dc, p), outs[k], (1, dc)))
+                    moves.append((given[dc], (quad // 2, p), outs[i], (0, dc)))
+                    moves.append((given[2], (dc, p), outs[i], (1, dc)))
             return moves
 
-        ready = move(third_moves, [shape(2, 2, hid, part)] * planes, keep, came, across)
+        ready = move(
+            functools.partial(third_moves, range(planes)), [shape(2, 2, hid, part)] * planes, keep, came, across, after=(sums, *blocks[-4:-2])
+        )
         held = [lax.ppermute(h, "gx", shift(-k)) if k else h for k, h in enumerate(ready)]
         pieces = list(held)
         for r in range(1, share):
             pieces += [lax.ppermute(h, "groups", swap(r)) for h in held]
 
-        far = []
-        for i, js in enumerate(cuts):
-            sends = cut(spot, *own, width, (2,) if paired else (2, 3), js[0], len(js), after=(send,) if i else ())
-            if paired:
-                came = lax.ppermute(sends[0], ("groups", "gx"), far_flip())
-                far.append((came, lax.ppermute(came, "groups", [(i, i ^ 1) for i in range(groups)])))
-            else:
-                far.append(tuple(lax.ppermute(w, "gx", flip(d)) for d, w in zip((2, 3), sends)))
-        near = lax.ppermute(cut(spot, *own, width, (1,), 0, planes)[0], "gx", flip(1))
-
-        sums = None
         crossed = pieces[planes:] if share > 1 else held
-        needs = [(ready[0],), (held[1],), (held[-1], crossed[0])]
-        later = [(crossed[1],), (crossed[-1], held[2 % planes])]
-        for i, js in enumerate(cuts):
-            sums = product(spot, rows, blocks, own, near, far[i], js, sums, after=needs[i])
-
-        send = stage(leave, [shape(EXTRA + 4 * hid, rows)], sums, total)[0]
+        one, two, three = held[1], held[2 % planes], held[-1]
+        x0, x1, x2, x3 = crossed[0], crossed[1], crossed[2 % planes], crossed[-1]
+        later = [(two,), (one,), (three, x2)]
+        sums = product(spot, rows, blocks, own, near, far[1], cuts[1], sums, after=(x0,))
+        send = stage(leave, [shape(EXTRA + 4 * hid, rows)], sums, total, after=())[0]
         came = lax.ppermute(send, "gx", flip(1))
         mine, total, send = stage(
             meet, [shape(2 * hid, rows, dtype=F32), shape(1, rows, dtype=F32), shape(EXTRA + 2 * hid, rows)], sums, total, came,
@@ -342,6 +362,7 @@
             lambda given, outs: [(a, ..., outs[0], (i // 2, i % 2)) for i, a in enumerate(given)],
             [shape(planes, 2, hid, rows)],
             *beside,
+            after=later[2],
         )[0]
         other = lax.ppermute(beside, "gx", flip(1))
         return mix(other, pieces, share, 1, mix(beside, pieces, share, 0))

time: 179 us -> 160 us (0.89)
  waiting for transfers between devices: 89.4 us -> 72.3 us
  starting transfers between devices: 36 us -> 50.4 us
  Pallas kernels: 40.1 us -> 27.3 us
  local copies, waits for them, and re-layouts: 8.38 us -> 4.2 us
  other arithmetic: 2.94 us -> 5.13 us
    ppermute x4, waiting for transfers between devices: 19.3 us -> 3.86 us  [body(): pieces += [lax.ppermute(h, 'groups', swap(r)) for h in held]]
    ppermute x10 -> x11, waiting for transfers between devices: 39.9 us -> 29.2 us  [the longest x6 27.8 us: body(): lax.ppermute(blocks[0] if s == 1 else blocks[-2], 'gx', line(s, way))]
    pallas_call x3 -> x2, Pallas kernels: 20.1 us -> 13.6 us  [product(): pl.pallas_call(kernel, grid_spec=pltpu.PrefetchScalarGridSpec(num_scalar_...]
    ppermute x3, starting transfers between devices: 4.55 us -> 10.2 us  [body(): lax.ppermute(h, 'gx', shift(-k))]
    unnamed x24 -> x14, local copies, waits for them, and re-layouts: 8.3 us -> 3.52 us
    ppermute x7, starting transfers between devices: 8.89 us -> 4.12 us  [body(): lax.ppermute(hidden, 'gx', shift(-k, d))]
    ppermute x1, waiting for transfers between devices: 0.01 us -> 3.91 us  [body(): across = lax.ppermute(send, 'gx', flip(2))]
    ppermute x7, waiting for transfers between devices: 13.2 us -> 17.1 us  [body(): lax.ppermute(hidden, 'gx', shift(-k, d))]
  transfers between devices with their start and end apart: 29 -> 30, of which waited for: 11 -> 12; matrix products, arithmetic and copies ran while one was open for 2% -> 2% of each run, Pallas kernels for 16% -> 15%
where the time goes in v3:
time: 160 us; the launch traced here: 159 us
  waiting for transfers between devices  72.3 us (45%)
  starting transfers between devices  50.4 us (32%)
  Pallas kernels  27.3 us (17%)
  other arithmetic  5.13 us (3%)
  local copies, waits for them, and re-layouts  4.2 us (3%)
    ppermute x6, waiting for transfers between devices, body(): lax.ppermute(blocks[0] if s == 1 else blocks[-2], 'gx', line(s, way))  27.8 us
    ppermute x3, waiting for transfers between devices, body(): lax.ppermute(h, 'gx', shift(-k))  18.2 us
    ppermute x7, waiting for transfers between devices, body(): lax.ppermute(hidden, 'gx', shift(-k, d))  17.1 us
    pallas_call x2, Pallas kernels, product(): pl.pallas_call(kernel, grid_spec=pltpu.PrefetchScalarGridSpec(num_scalar_...  13.6 us
    ppermute x6, starting transfers between devices, body(): lax.ppermute(blocks[0] if s == 1 else blocks[-2], 'gx', line(s, way))  10.9 us
    ppermute x3, starting transfers between devices, body(): lax.ppermute(h, 'gx', shift(-k))  10.2 us
    ppermute x4, starting transfers between devices, body(): pieces += [lax.ppermute(h, 'groups', swap(r)) for h in held]  7.32 us
    pallas_call x2, Pallas kernels, mix(): pl.pallas_call(kernel, grid=(1,), out_shape=shape(*out_shape, dtype=BF if...  6.59 us
  transfers between devices with their start and end apart: 30, of which 12 were waited for; matrix products, arithmetic and copies ran while one was open for 2% of the time, Pallas kernels for 15%

profile of v3, /device:TPU:1, one launch (start us, length us, event | category | flops | bytes accessed | tf_op | source)
XLA Modules:
  0.0 159.5 jit_solution(14970666932896130221)
XLA Ops:
  0.0 1.8 %fusion.1 = (bf16[512,1024]{1,0:T(8,128)(2,1)S(1)}, f32[512]{0:T(512)S(1)}) fusion(bf16[512,1024]{1,0:T(8,128)(2,1)} %param.6, f32[1024]{0:T(1024)} %param.7), kind=kLoop, calls=%fused_computation.4 | loop fusion | flops 2620928 | bytes 2103296 | tf_op jit(solution)/shard_map/convert_element_type | solution.py:285
  4.1 5.6 %collective-permute-start.1 = (bf16[528,1024]{1,0:T(8,128)(2,1)}, bf16[528,1024]{1,0:T(8,128)(2,1)}, u32[]{:S(2)}, u32[]{:S(2)}) collective-permute-start(bf16[528,1024]{1,0:T(8,128)(2,1)} %fusion.3.refs_2_.refs_0_), channel_id=1, source_target_pairs={{0,4},{1,5},{2,6},{3,7},{4,8},{5,9},{6,10},{7,11},{8,12},{9,13},{1... | collective-permute-start | bytes 3244040 | tf_op jit(solution)/shard_map/ppermute | solution.py:289
  10.6 3.0 %shard_map.64 = bf16[4,2,104,1024]{3,2,1,0:T(8,128)(2,1)S(1)} custom-call(s32[11]{0:T(128)S(1)} %pad_add_fusion.spot, bf16[104,16384]{1,0:T(8,128)(2,1)S(1)} %bitcast.10, bf16[104,16384]{1,0:T(8,128)(2,1)} %bitcast.13, bf16[528,1024]{1,0:T(8,128)(2,1)} %fusion.3.refs_2_.refs_0_), custom_call_target="tpu_custom_call" | custom-call | bytes 68157440 | tf_op jit(solution)/shard_map/pallas_call | solution.py:220
  18.3 12.5 %collective-permute-done.refs_2_.refs_0_ = bf16[528,1024]{1,0:T(8,128)(2,1)} collective-permute-done((bf16[528,1024]{1,0:T(8,128)(2,1)}, bf16[528,1024]{1,0:T(8,128)(2,1)}, u32[]{:S(2)}, u32[]{:S(2)}) %collective-permute-start) | collective-permute-done | bytes 1081376 | tf_op jit(solution)/shard_map/ppermute | solution.py:289
  37.1 2.6 %collective-permute-start.11 = (bf16[2,2,104,1024]{3,2,1,0:T(8,128)(2,1)S(1)}, bf16[2,2,104,1024]{3,2,1,0:T(8,128)(2,1)S(1)}, u32[]{:S(2)}, u32[]{:S(2)}) collective-permute-start(bf16[2,2,104,1024]{3,2,1,0:T(8,128)(2,1)S(1)} %collective-permute-done.10.refs_6_), channel_id=1, source_target_pairs={{0,16},{16,0},{1,17},{17,1},{2,18},{18,2},{3,19},{19,3},{4,20},{20... | collective-permute-start | bytes 2555912 | tf_op jit(solution)/shard_map/ppermute | solution.py:321
  41.8 15.3 %collective-permute-done.3.refs_5_.refs_2_ = bf16[528,1024]{1,0:T(8,128)(2,1)} collective-permute-done((bf16[528,1024]{1,0:T(8,128)(2,1)}, bf16[528,1024]{1,0:T(8,128)(2,1)}, u32[]{:S(2)}, u32[]{:S(2)}) %collective-permute-start.3) | collective-permute-done | bytes 1081376 | tf_op jit(solution)/shard_map/ppermute | solution.py:289
  62.5 6.5 %shard_map.69.refs_3_.refs_10_ = f32[832,512]{1,0:T(8,128)} custom-call(s32[11]{0:T(128)S(1)} %pad_add_fusion.spot, bf16[528,1024]{1,0:T(8,128)(2,1)} %fusion.3.refs_2_.refs_0_, bf16[528,1024]{1,0:T(8,128)(2,1)} %collective-permute-done.1.refs_1_, bf16[528,1024]{1,0:T(8,128)(2,1)} %collective-permute-done.refs_2_.refs_0_, bf16[104,16384]{1,0:T(8,128)(2,1)} %bitcast.8, ...), custom_call_target="tpu_custom_call" | custom-call | flops 1744830464 | bytes 3407872 | tf_op jit(solution)/shard_map/pallas_call | solution.py:187
  69.0 3.9 %collective-permute-done.12.refs_2_ = bf16[2,4,104,512]{3,2,1,0:T(8,128)(2,1)S(1)} collective-permute-done((bf16[2,4,104,512]{3,2,1,0:T(8,128)(2,1)S(1)}, bf16[2,4,104,512]{3,2,1,0:T(8,128)(2,1)S(1)}, u32[]{:S(2)}, u32[]{:S(2)}) %collective-permute-start.12) | collective-permute-done | bytes 852000 | tf_op jit(solution)/shard_map/ppermute | solution.py:314
  73.0 3.5 %collective-permute-start.13 = (bf16[2,2,104,512]{3,2,1,0:T(8,128)(2,1)S(1)}, bf16[2,2,104,512]{3,2,1,0:T(8,128)(2,1)S(1)}, u32[]{:S(2)}, u32[]{:S(2)}) collective-permute-start(bf16[2,2,104,512]{3,2,1,0:T(8,128)(2,1)S(1)} %get-tuple-element.16.refs_0_), channel_id=1, source_target_pairs={{16,0},{0,16},{17,1},{1,17},{18,2},{2,18},{19,3},{3,19},{20,4},{4,... | collective-permute-start | bytes 1277960 | tf_op jit(solution)/shard_map/ppermute | solution.py:345
  76.5 6.8 %collective-permute-start.15 = (bf16[2,2,104,512]{3,2,1,0:T(8,128)(2,1)S(1)}, bf16[2,2,104,512]{3,2,1,0:T(8,128)(2,1)S(1)}, u32[]{:S(2)}, u32[]{:S(2)}) collective-permute-start(bf16[2,2,104,512]{3,2,1,0:T(8,128)(2,1)S(1)} %get-tuple-element.17), channel_id=1, source_target_pairs={{0,8},{1,9},{2,10},{3,11},{4,12},{5,13},{6,14},{7,15},{8,0},{9,1},... | collective-permute-start | bytes 1277960 | tf_op jit(solution)/shard_map/ppermute | solution.py:342
  84.2 3.9 %collective-permute-done.13.refs_11_.refs_4_ = bf16[2,2,104,512]{3,2,1,0:T(8,128)(2,1)S(1)} collective-permute-done((bf16[2,2,104,512]{3,2,1,0:T(8,128)(2,1)S(1)}, bf16[2,2,104,512]{3,2,1,0:T(8,128)(2,1)S(1)}, u32[]{:S(2)}, u32[]{:S(2)}) %collective-permute-start.13) | collective-permute-done | bytes 426016 | tf_op jit(solution)/shard_map/ppermute | solution.py:345
  88.0 7.2 %shard_map.71.refs_0_ = f32[832,512]{1,0:T(8,128)} custom-call(s32[11]{0:T(128)S(1)} %pad_add_fusion.spot, bf16[528,1024]{1,0:T(8,128)(2,1)} %collective-permute-done.refs_2_.refs_0_, bf16[528,1024]{1,0:T(8,128)(2,1)S(1)} %collective-permute-done.2.refs_4_.refs_1_, bf16[528,1024]{1,0:T(8,128)(2,1)} %collective-permute-done.3.refs_5_.refs_2_, ...), custom_call_target="tpu_custom_call" | custom-call | flops 1744830464 | bytes 3407872 | tf_op jit(solution)/shard_map/pallas_call | solution.py:187
  96.7 3.1 %collective-permute-start.14 = (bf16[432,512]{1,0:T(8,128)(2,1)S(1)}, bf16[432,512]{1,0:T(8,128)(2,1)S(1)}, u32[]{:S(2)}, u32[]{:S(2)}) collective-permute-start(bf16[432,512]{1,0:T(8,128)(2,1)S(1)} %shard_map.72), channel_id=1, source_target_pairs={{0,1},{1,0},{2,3},{3,2},{4,5},{5,4},{6,7},{7,6},{8,9},{9,8},{10,11... | collective-permute-start | bytes 1327112 | tf_op jit(solution)/shard_map/ppermute | solution.py:353
  99.8 3.4 %collective-permute-start.17 = (bf16[2,2,104,512]{3,2,1,0:T(8,128)(2,1)S(1)}, bf16[2,2,104,512]{3,2,1,0:T(8,128)(2,1)S(1)}, u32[]{:S(2)}, u32[]{:S(2)}) collective-permute-start(bf16[2,2,104,512]{3,2,1,0:T(8,128)(2,1)S(1)} %get-tuple-element.21), channel_id=1, source_target_pairs={{0,12},{1,13},{2,14},{3,15},{4,0},{5,1},{6,2},{7,3},{8,4},{9,5},{1... | collective-permute-start | bytes 1277960 | tf_op jit(solution)/shard_map/ppermute | solution.py:342
  105.8 6.6 %collective-permute-done.17.refs_3_.refs_1_ = bf16[2,2,104,512]{3,2,1,0:T(8,128)(2,1)S(1)} collective-permute-done((bf16[2,2,104,512]{3,2,1,0:T(8,128)(2,1)S(1)}, bf16[2,2,104,512]{3,2,1,0:T(8,128)(2,1)S(1)}, u32[]{:S(2)}, u32[]{:S(2)}) %collective-permute-start.17) | collective-permute-done | bytes 426016 | tf_op jit(solution)/shard_map/ppermute | solution.py:342
  113.8 11.6 %collective-permute-done.25.refs_8_.refs_3_ = bf16[2,2,104,512]{3,2,1,0:T(8,128)(2,1)S(1)} collective-permute-done((bf16[2,2,104,512]{3,2,1,0:T(8,128)(2,1)S(1)}, bf16[2,2,104,512]{3,2,1,0:T(8,128)(2,1)S(1)}, u32[]{:S(2)}, u32[]{:S(2)}) %collective-permute-start.25) | collective-permute-done | bytes 426016 | tf_op jit(solution)/shard_map/ppermute | solution.py:342
  128.7 1.9 %collective-permute-done.18.refs_1_ = bf16[104,512]{1,0:T(8,128)(2,1)S(1)} collective-permute-done((bf16[104,512]{1,0:T(8,128)(2,1)S(1)}, bf16[104,512]{1,0:T(8,128)(2,1)S(1)}, u32[]{:S(2)}, u32[]{:S(2)}) %collective-permute-start.18) | collective-permute-done | bytes 106528 | tf_op jit(solution)/shard_map/ppermute | solution.py:360
  131.9 2.1 %collective-permute-start.22 = (bf16[104,512]{1,0:T(8,128)(2,1)S(1)}, bf16[104,512]{1,0:T(8,128)(2,1)S(1)}, u32[]{:S(2)}, u32[]{:S(2)}) collective-permute-start(bf16[104,512]{1,0:T(8,128)(2,1)S(1)} %shard_map.74.refs_0_), channel_id=1, source_target_pairs={{0,10},{1,11},{2,8},{3,9},{4,14},{5,15},{6,12},{7,13},{8,2},{9,3},... | collective-permute-start | bytes 319496 | tf_op jit(solution)/shard_map/ppermute | solution.py:360
  134.1 7.7 %collective-permute-done.21.refs_4_ = bf16[104,512]{1,0:T(8,128)(2,1)S(1)} collective-permute-done((bf16[104,512]{1,0:T(8,128)(2,1)S(1)}, bf16[104,512]{1,0:T(8,128)(2,1)S(1)}, u32[]{:S(2)}, u32[]{:S(2)}) %collective-permute-start.21) | collective-permute-done | bytes 106528 | tf_op jit(solution)/shard_map/ppermute | solution.py:360
  141.8 4.2 %collective-permute-done.22.refs_5_ = bf16[104,512]{1,0:T(8,128)(2,1)S(1)} collective-permute-done((bf16[104,512]{1,0:T(8,128)(2,1)S(1)}, bf16[104,512]{1,0:T(8,128)(2,1)S(1)}, u32[]{:S(2)}, u32[]{:S(2)}) %collective-permute-start.22) | collective-permute-done | bytes 106528 | tf_op jit(solution)/shard_map/ppermute | solution.py:360
  146.0 2.0 %collective-permute-done.24.refs_7_ = bf16[104,512]{1,0:T(8,128)(2,1)S(1)} collective-permute-done((bf16[104,512]{1,0:T(8,128)(2,1)S(1)}, bf16[104,512]{1,0:T(8,128)(2,1)S(1)}, u32[]{:S(2)}, u32[]{:S(2)}) %collective-permute-start.24) | collective-permute-done | bytes 106528 | tf_op jit(solution)/shard_map/ppermute | solution.py:360
  148.1 4.8 %collective-permute-start.27 = (bf16[4,2,104,512]{3,2,1,0:T(8,128)(2,1)S(1)}, bf16[4,2,104,512]{3,2,1,0:T(8,128)(2,1)S(1)}, u32[]{:S(2)}, u32[]{:S(2)}) collective-permute-start(bf16[4,2,104,512]{3,2,1,0:T(8,128)(2,1)S(1)} %shard_map.75.side), channel_id=1, source_target_pairs={{0,1},{1,0},{2,3},{3,2},{4,5},{5,4},{6,7},{7,6},{8,9},{9,8},{10,11... | collective-permute-start | bytes 2555912 | tf_op jit(solution)/shard_map/ppermute | solution.py:367
  152.9 2.6 %shard_map.76.refs_8_ = f32[2,512,512]{2,1,0:T(8,128)} custom-call(bf16[4,2,104,512]{3,2,1,0:T(8,128)(2,1)S(1)} %shard_map.75.side, bf16[2,2,104,512]{3,2,1,0:T(8,128)(2,1)S(1)} %get-tuple-element.16.refs_0_, bf16[2,2,104,512]{3,2,1,0:T(8,128)(2,1)S(1)} %collective-permute-done.17.refs_3_.refs_1_, ...), custom_call_target="tpu_custom_call" | custom-call | flops 17448304640 | bytes 51118080 | tf_op jit(solution)/shard_map/pallas_call | solution.py:259
  155.5 3.9 %shard_map.77 = bf16[512,1024]{1,0:T(8,128)(2,1)} custom-call(bf16[4,2,104,512]{3,2,1,0:T(8,128)(2,1)S(1)} %collective-permute-done.27.side, bf16[2,2,104,512]{3,2,1,0:T(8,128)(2,1)S(1)} %get-tuple-element.16.refs_0_, bf16[2,2,104,512]{3,2,1,0:T(8,128)(2,1)S(1)} %collective-permute-done.17.refs_3_.refs_1_, ...), custom_call_target="tpu_custom_call" | custom-call | flops 17448304640 | bytes 51118080 | tf_op jit(solution)/shard_map/pallas_call | solution.py:259
  (77 shorter events, 32.7 us)
Async XLA Ops:
  2.9 27.9 %collective-permute-start = (bf16[528,1024]{1,0:T(8,128)(2,1)}, bf16[528,1024]{1,0:T(8,128)(2,1)}, u32[]{:S(2)}, u32[]{:S(2)}) collective-permute-start(bf16[528,1024]{1,0:T(8,128)(2,1)} %fusion.3.refs_2_.refs_0_), channel_id=1, source_target_pairs={{4,0},{5,1},{6,2},{7,3},{8,4},{9,5},{10,6},{11,7},{12,8},{13,9},{1... | collective-permute-start | bytes 3244040 | tf_op jit(solution)/shard_map/ppermute | solution.py:289
  4.1 27.9 %collective-permute-start.1 = (bf16[528,1024]{1,0:T(8,128)(2,1)}, bf16[528,1024]{1,0:T(8,128)(2,1)}, u32[]{:S(2)}, u32[]{:S(2)}) collective-permute-start(bf16[528,1024]{1,0:T(8,128)(2,1)} %fusion.3.refs_2_.refs_0_), channel_id=1, source_target_pairs={{0,4},{1,5},{2,6},{3,7},{4,8},{5,9},{6,10},{7,11},{8,12},{9,13},{1... | collective-permute-start | bytes 3244040 | tf_op jit(solution)/shard_map/ppermute | solution.py:289
  13.5 27.0 %collective-permute-start.6 = (bf16[4,2,104,1024]{3,2,1,0:T(8,128)(2,1)S(1)}, bf16[4,2,104,1024]{3,2,1,0:T(8,128)(2,1)}, u32[]{:S(2)}, u32[]{:S(2)}) collective-permute-start(bf16[4,2,104,1024]{3,2,1,0:T(8,128)(2,1)S(1)} %shard_map.64), channel_id=1, source_target_pairs={{0,1},{1,0},{2,3},{3,2},{4,5},{5,4},{6,7},{7,6},{8,9},{9,8},{10,11... | collective-permute-start | bytes 5111816 | tf_op jit(solution)/shard_map/ppermute | solution.py:324
  14.7 18.1 %collective-permute-start.7 = (bf16[2,4,104,512]{3,2,1,0:T(8,128)(2,1)S(1)}, bf16[2,4,104,512]{3,2,1,0:T(8,128)(2,1)S(1)}, u32[]{:S(2)}, u32[]{:S(2)}) collective-permute-start(bf16[2,4,104,512]{3,2,1,0:T(8,128)(2,1)S(1)} %get-tuple-element.15), channel_id=1, source_target_pairs={{0,1},{1,0},{2,3},{3,2},{4,5},{5,4},{6,7},{7,6},{8,9},{9,8},{10,11... | collective-permute-start | bytes 2555912 | tf_op jit(solution)/shard_map/ppermute | solution.py:307
  16.5 20.6 %collective-permute-start.10 = (bf16[2,2,104,1024]{3,2,1,0:T(8,128)(2,1)S(1)}, bf16[2,2,104,1024]{3,2,1,0:T(8,128)(2,1)S(1)}, u32[]{:S(2)}, u32[]{:S(2)}) collective-permute-start(bf16[2,2,104,1024]{3,2,1,0:T(8,128)(2,1)S(1)} %shard_map.68), channel_id=1, source_target_pairs={{0,2},{1,3},{2,0},{3,1},{4,6},{5,7},{6,4},{7,5},{8,10},{9,11},{10,... | collective-permute-start | bytes 2555912 | tf_op jit(solution)/shard_map/ppermute | solution.py:320
  30.8 26.3 %collective-permute-start.3 = (bf16[528,1024]{1,0:T(8,128)(2,1)}, bf16[528,1024]{1,0:T(8,128)(2,1)}, u32[]{:S(2)}, u32[]{:S(2)}) collective-permute-start(bf16[528,1024]{1,0:T(8,128)(2,1)} %collective-permute-done.refs_2_.refs_0_), channel_id=1, source_target_pairs={{4,0},{5,1},{6,2},{7,3},{8,4},{9,5},{10,6},{11,7},{20,16},{21,17},... | collective-permute-start | bytes 3244040 | tf_op jit(solution)/shard_map/ppermute | solution.py:289
  32.1 26.3 %collective-permute-start.2 = (bf16[528,1024]{1,0:T(8,128)(2,1)}, bf16[528,1024]{1,0:T(8,128)(2,1)S(1)}, u32[]{:S(2)}, u32[]{:S(2)}) collective-permute-start(bf16[528,1024]{1,0:T(8,128)(2,1)} %collective-permute-done.1.refs_1_), channel_id=1, source_target_pairs={{4,8},{5,9},{6,10},{7,11},{8,12},{9,13},{10,14},{11,15},{20,24},{2... | collective-permute-start | bytes 3244040 | tf_op jit(solution)/shard_map/ppermute | solution.py:289
  34.6 26.0 %collective-permute-start.8 = (bf16[2,2,104,1024]{3,2,1,0:T(8,128)(2,1)S(1)}, bf16[2,2,104,1024]{3,2,1,0:T(8,128)(2,1)S(1)}, u32[]{:S(2)}, u32[]{:S(2)}) collective-permute-start(bf16[2,2,104,1024]{3,2,1,0:T(8,128)(2,1)S(1)} %shard_map.67), channel_id=1, source_target_pairs={{0,2},{1,3},{2,0},{3,1},{4,6},{5,7},{6,4},{7,5},{8,10},{9,11},{10,... | collective-permute-start | bytes 2555912 | tf_op jit(solution)/shard_map/ppermute | solution.py:320
  37.1 24.2 %collective-permute-start.11 = (bf16[2,2,104,1024]{3,2,1,0:T(8,128)(2,1)S(1)}, bf16[2,2,104,1024]{3,2,1,0:T(8,128)(2,1)S(1)}, u32[]{:S(2)}, u32[]{:S(2)}) collective-permute-start(bf16[2,2,104,1024]{3,2,1,0:T(8,128)(2,1)S(1)} %collective-permute-done.10.refs_6_), channel_id=1, source_target_pairs={{0,16},{16,0},{1,17},{17,1},{2,18},{18,2},{3,19},{19,3},{4,20},{20... | collective-permute-start | bytes 2555912 | tf_op jit(solution)/shard_map/ppermute | solution.py:321
  40.6 32.3 %collective-permute-start.12 = (bf16[2,4,104,512]{3,2,1,0:T(8,128)(2,1)S(1)}, bf16[2,4,104,512]{3,2,1,0:T(8,128)(2,1)S(1)}, u32[]{:S(2)}, u32[]{:S(2)}) collective-permute-start(bf16[2,4,104,512]{3,2,1,0:T(8,128)(2,1)S(1)} %shard_map.66.refs_2_), channel_id=1, source_target_pairs={{0,2},{1,3},{2,0},{3,1},{4,6},{5,7},{6,4},{7,5},{8,10},{9,11},{10,... | collective-permute-start | bytes 2555912 | tf_op jit(solution)/shard_map/ppermute | solution.py:314
  57.1 26.9 %collective-permute-start.5 = (bf16[528,1024]{1,0:T(8,128)(2,1)}, bf16[528,1024]{1,0:T(8,128)(2,1)S(1)}, u32[]{:S(2)}, u32[]{:S(2)}) collective-permute-start(bf16[528,1024]{1,0:T(8,128)(2,1)} %collective-permute-done.3.refs_5_.refs_2_), channel_id=1, source_target_pairs={{4,0},{5,1},{6,2},{7,3},{20,16},{21,17},{22,18},{23,19}} | collective-permute-start | bytes 3244040 | tf_op jit(solution)/shard_map/ppermute | solution.py:289
  58.4 25.7 %collective-permute-start.4 = (bf16[528,1024]{1,0:T(8,128)(2,1)S(1)}, bf16[528,1024]{1,0:T(8,128)(2,1)S(1)}, u32[]{:S(2)}, u32[]{:S(2)}) collective-permute-start(bf16[528,1024]{1,0:T(8,128)(2,1)S(1)} %collective-permute-done.2.refs_4_.refs_1_), channel_id=1, source_target_pairs={{8,12},{9,13},{10,14},{11,15},{24,28},{25,29},{26,30},{27,31}} | collective-permute-start | bytes 3244040 | tf_op jit(solution)/shard_map/ppermute | solution.py:289
  60.6 23.6 %collective-permute-start.9 = (bf16[2,2,104,1024]{3,2,1,0:T(8,128)(2,1)S(1)}, bf16[2,2,104,1024]{3,2,1,0:T(8,128)(2,1)S(1)}, u32[]{:S(2)}, u32[]{:S(2)}) collective-permute-start(bf16[2,2,104,1024]{3,2,1,0:T(8,128)(2,1)S(1)} %collective-permute-done.8.refs_8_), channel_id=1, source_target_pairs={{0,16},{16,0},{1,17},{17,1},{2,18},{18,2},{3,19},{19,3},{4,20},{20... | collective-permute-start | bytes 2555912 | tf_op jit(solution)/shard_map/ppermute | solution.py:321
  73.0 15.0 %collective-permute-start.13 = (bf16[2,2,104,512]{3,2,1,0:T(8,128)(2,1)S(1)}, bf16[2,2,104,512]{3,2,1,0:T(8,128)(2,1)S(1)}, u32[]{:S(2)}, u32[]{:S(2)}) collective-permute-start(bf16[2,2,104,512]{3,2,1,0:T(8,128)(2,1)S(1)} %get-tuple-element.16.refs_0_), channel_id=1, source_target_pairs={{16,0},{0,16},{17,1},{1,17},{18,2},{2,18},{19,3},{3,19},{20,4},{4,... | collective-permute-start | bytes 1277960 | tf_op jit(solution)/shard_map/ppermute | solution.py:345
  76.5 26.7 %collective-permute-start.15 = (bf16[2,2,104,512]{3,2,1,0:T(8,128)(2,1)S(1)}, bf16[2,2,104,512]{3,2,1,0:T(8,128)(2,1)S(1)}, u32[]{:S(2)}, u32[]{:S(2)}) collective-permute-start(bf16[2,2,104,512]{3,2,1,0:T(8,128)(2,1)S(1)} %get-tuple-element.17), channel_id=1, source_target_pairs={{0,8},{1,9},{2,10},{3,11},{4,12},{5,13},{6,14},{7,15},{8,0},{9,1},... | collective-permute-start | bytes 1277960 | tf_op jit(solution)/shard_map/ppermute | solution.py:342
  99.8 12.6 %collective-permute-start.17 = (bf16[2,2,104,512]{3,2,1,0:T(8,128)(2,1)S(1)}, bf16[2,2,104,512]{3,2,1,0:T(8,128)(2,1)S(1)}, u32[]{:S(2)}, u32[]{:S(2)}) collective-permute-start(bf16[2,2,104,512]{3,2,1,0:T(8,128)(2,1)S(1)} %get-tuple-element.21), channel_id=1, source_target_pairs={{0,12},{1,13},{2,14},{3,15},{4,0},{5,1},{6,2},{7,3},{8,4},{9,5},{1... | collective-permute-start | bytes 1277960 | tf_op jit(solution)/shard_map/ppermute | solution.py:342
  103.2 22.3 %collective-permute-start.25 = (bf16[2,2,104,512]{3,2,1,0:T(8,128)(2,1)S(1)}, bf16[2,2,104,512]{3,2,1,0:T(8,128)(2,1)S(1)}, u32[]{:S(2)}, u32[]{:S(2)}) collective-permute-start(bf16[2,2,104,512]{3,2,1,0:T(8,128)(2,1)S(1)} %get-tuple-element.22), channel_id=1, source_target_pairs={{0,4},{1,5},{2,6},{3,7},{4,8},{5,9},{6,10},{7,11},{8,12},{9,13},{1... | collective-permute-start | bytes 1277960 | tf_op jit(solution)/shard_map/ppermute | solution.py:342
  103.2 25.3 %collective-permute-start.26 = (bf16[2,2,104,512]{3,2,1,0:T(8,128)(2,1)S(1)}, bf16[2,2,104,512]{3,2,1,0:T(8,128)(2,1)S(1)}, u32[]{:S(2)}, u32[]{:S(2)}) collective-permute-start(bf16[2,2,104,512]{3,2,1,0:T(8,128)(2,1)S(1)} %collective-permute-done.15.refs_3_.refs_2_), channel_id=1, source_target_pairs={{16,0},{0,16},{17,1},{1,17},{18,2},{2,18},{19,3},{3,19},{20,4},{4,... | collective-permute-start | bytes 1277960 | tf_op jit(solution)/shard_map/ppermute | solution.py:345
  104.5 22.1 %collective-permute-start.16 = (bf16[224,512]{1,0:T(8,128)(2,1)S(1)}, bf16[224,512]{1,0:T(8,128)(2,1)S(1)}, u32[]{:S(2)}, u32[]{:S(2)}) collective-permute-start(bf16[224,512]{1,0:T(8,128)(2,1)S(1)} %get-tuple-element.20), channel_id=1, source_target_pairs={{0,2},{1,3},{2,0},{3,1},{4,6},{5,7},{6,4},{7,5},{8,10},{9,11},{10,... | collective-permute-start | bytes 688136 | tf_op jit(solution)/shard_map/ppermute | solution.py:358
  112.4 40.5 %collective-permute-start.28 = (bf16[2,2,104,512]{3,2,1,0:T(8,128)(2,1)S(1)}, bf16[2,2,104,512]{3,2,1,0:T(8,128)(2,1)S(1)}, u32[]{:S(2)}, u32[]{:S(2)}) collective-permute-start(bf16[2,2,104,512]{3,2,1,0:T(8,128)(2,1)S(1)} %collective-permute-done.17.refs_3_.refs_1_), channel_id=1, source_target_pairs={{16,0},{0,16},{17,1},{1,17},{18,2},{2,18},{19,3},{3,19},{20,4},{4,... | collective-permute-start | bytes 1277960 | tf_op jit(solution)/shard_map/ppermute | solution.py:345
  125.4 27.5 %collective-permute-start.29 = (bf16[2,2,104,512]{3,2,1,0:T(8,128)(2,1)S(1)}, bf16[2,2,104,512]{3,2,1,0:T(8,128)(2,1)S(1)}, u32[]{:S(2)}, u32[]{:S(2)}) collective-permute-start(bf16[2,2,104,512]{3,2,1,0:T(8,128)(2,1)S(1)} %collective-permute-done.25.refs_8_.refs_3_), channel_id=1, source_target_pairs={{16,0},{0,16},{17,1},{1,17},{18,2},{2,18},{19,3},{3,19},{20,4},{4,... | collective-permute-start | bytes 1277960 | tf_op jit(solution)/shard_map/ppermute | solution.py:345
  130.7 11.1 %collective-permute-start.21 = (bf16[104,512]{1,0:T(8,128)(2,1)S(1)}, bf16[104,512]{1,0:T(8,128)(2,1)S(1)}, u32[]{:S(2)}, u32[]{:S(2)}) collective-permute-start(bf16[104,512]{1,0:T(8,128)(2,1)S(1)} %shard_map.74.refs_0_), channel_id=1, source_target_pairs={{0,8},{1,9},{2,10},{3,11},{4,12},{5,13},{6,14},{7,15},{8,0},{9,1},... | collective-permute-start | bytes 319496 | tf_op jit(solution)/shard_map/ppermute | solution.py:360
  131.9 14.1 %collective-permute-start.22 = (bf16[104,512]{1,0:T(8,128)(2,1)S(1)}, bf16[104,512]{1,0:T(8,128)(2,1)S(1)}, u32[]{:S(2)}, u32[]{:S(2)}) collective-permute-start(bf16[104,512]{1,0:T(8,128)(2,1)S(1)} %shard_map.74.refs_0_), channel_id=1, source_target_pairs={{0,10},{1,11},{2,8},{3,9},{4,14},{5,15},{6,12},{7,13},{8,2},{9,3},... | collective-permute-start | bytes 319496 | tf_op jit(solution)/shard_map/ppermute | solution.py:360
  134.0 12.0 %collective-permute-start.23 = (bf16[104,512]{1,0:T(8,128)(2,1)S(1)}, bf16[104,512]{1,0:T(8,128)(2,1)S(1)}, u32[]{:S(2)}, u32[]{:S(2)}) collective-permute-start(bf16[104,512]{1,0:T(8,128)(2,1)S(1)} %shard_map.74.refs_0_), channel_id=1, source_target_pairs={{0,4},{1,5},{2,6},{3,7},{4,8},{5,9},{6,10},{7,11},{8,12},{9,13},{1... | collective-permute-start | bytes 319496 | tf_op jit(solution)/shard_map/ppermute | solution.py:360
  (13 other events, 60.7 us)

commit v4 on v3

--- a/solution.py
+++ b/solution.py
@@ -36,7 +36,7 @@
         in_specs=[VMEM] * len(operands) + [ANY] * len(after),
         out_specs=[VMEM] * len(outs),
         compiler_params=PARAMS,
-        cost_estimate=cost(4 * sum(o.size for o in outs), 0, 20),
+        cost_estimate=cost(4 * sum(o.size for o in outs), 0, 1),
     )(*operands, *after)
 
 
@@ -63,7 +63,7 @@
         in_specs=[VMEM] * len(operands) + [ANY] * len(after),
         out_specs=[VMEM] * len(outs),
         compiler_params=PARAMS,
-        cost_estimate=cost(4 * sum(o.size for o in outs), 0, 0),
+        cost_estimate=cost(4 * sum(o.size for o in outs), 0, 1),
     )(*operands, *after)
 
 
@@ -75,20 +75,13 @@
     out[pl.ds(0, EXTRA), :] = jnp.concatenate(parts + [jnp.zeros((EXTRA - 3, values.shape[1]), F32)]).astype(BF)
 
 
-def leave(sums, total, send):
-    count = sums.shape[0] // 4
-    put_parts(total[...], send)
-    for i, d in enumerate((1, 3)):
-        send[pl.ds(EXTRA + i * count, count), :] = sums[pl.ds(d * count, count), :].astype(BF)
-
-
-def meet(sums, total, came, mine, total_out, send):
-    count = sums.shape[0] // 4
+def meet(keep, total, came, mine, total_out, send):
+    count = keep.shape[0] // 2
     both = total[...] + joined(came[pl.ds(0, EXTRA), :])
     total_out[...] = both
-    mine[...] = sums[pl.ds(0, count), :] + came[pl.ds(EXTRA, count), :].astype(F32)
+    mine[...] = keep[pl.ds(0, count), :] + came[pl.ds(EXTRA, count), :].astype(F32)
     put_parts(both, send)
-    across = sums[pl.ds(2 * count, count), :] + came[pl.ds(EXTRA + count, count), :].astype(F32)
+    across = keep[pl.ds(count, count), :] + came[pl.ds(EXTRA + count, count), :].astype(F32)
     send[pl.ds(EXTRA, count), :] = across.astype(BF)
 
 
@@ -117,7 +110,7 @@
     planes = n // 4
     table = arrivals(planes)
     BLOCK, ARRAY = 3, 3 + planes
-    cuts = [range(0, planes // 2), range(planes // 2, planes)]
+    cuts = [range(0, planes - 1), range(planes - 1, planes)]
     paired = groups % 2 == 0
 
     def at(p, q):
@@ -143,18 +136,22 @@
         me = lax.axis_index("gx")
         return me // 4, me % 4
 
-    def product(spot, rows, blocks, own, near, far, js, total=None, after=()):
+    def product(spot, rows, blocks, own, near, far, js, total=None, squares=None, after=()):
         width = blocks[0].shape[1]
         _, two, hid, _ = near.shape
         first, count = js[0], len(js)
         lists = [sorted(set(row[j][0] for row in table)) for j in js]
         arrays = sorted(set(sum(lists, [])))
-        given = [] if total is None else [total]
+        last = squares is not None
+        given = ([] if total is None else [total]) + ([squares] if last else [])
 
         def kernel(spot, *refs):
             sources, refs = refs[: len(arrays)], refs[len(arrays) :]
             own_gate, own_up, near, far0, far1 = refs[:5]
-            out, xs, sems = refs[-3:]
+            if last:
+                keep, send, out, xs, sems = refs[-5:]
+            else:
+                out, xs, sems = refs[-3:]
             i = pl.program_id(0)
 
             def bring(array, k):
@@ -165,7 +162,7 @@
                 for k, choices in enumerate(lists):
                     for array in choices:
                         pl.when(spot[ARRAY + first + k] == array)(bring(array, k).start)
-                out[...] = refs[5][...] if given else jnp.zeros_like(out)
+                out[...] = jnp.zeros_like(out) if total is None else refs[5][...]
 
             for k, choices in enumerate(lists):
                 pl.when(i == k)(bring(choices[0], k).wait)
@@ -179,11 +176,28 @@
             for b in range(2):
                 d = 2 + lax.bitwise_xor(b, spot[2])
                 out[pl.ds(pl.multiple_of(d * 2 * hid, 8), 2 * hid), :] += term[(4 + 2 * b) * hid : (6 + 2 * b) * hid]
+            if last:
+
+                @pl.when(i == count - 1)
+                def _():
+                    put_parts(refs[4 + len(given)][...], send)
+                    for b in range(2):
+                        keep[pl.ds(b * 2 * hid, 2 * hid), :] = out[pl.ds(b * 4 * hid, 2 * hid), :]
+                        send[pl.ds(EXTRA + b * 2 * hid, 2 * hid), :] = out[pl.ds((4 * b + 2) * hid, 2 * hid), :].astype(BF)
 
         near_block = pl.BlockSpec((1, two, hid, width), lambda i, spot: (i + first, 0, 0, 0))
         far_block = pl.BlockSpec((1, two, hid, width), lambda i, spot: (i, 0, 0, 0))
         mine = pl.BlockSpec((hid, width), lambda i, spot: (0, spot[BLOCK + first + i] * 4 + spot[1]))
-        whole = pl.BlockSpec((8 * hid, rows), lambda i, spot: (0, 0))
+
+        def whole(*dims):
+            return pl.BlockSpec(dims, lambda i, spot: (0, 0))
+
+        scratch = [pltpu.VMEM((count, rows, width), BF), pltpu.SemaphoreType.DMA((count,))]
+        if last:
+            outs = [shape(4 * hid, rows, dtype=F32), shape(EXTRA + 4 * hid, rows)]
+            scratch = [pltpu.VMEM((8 * hid, rows), F32)] + scratch
+        else:
+            outs = shape(8 * hid, rows, dtype=F32)
         return pl.pallas_call(
             kernel,
             grid_spec=pltpu.PrefetchScalarGridSpec(
@@ -191,14 +205,14 @@
                 grid=(count,),
                 in_specs=[ANY] * len(arrays)
                 + [mine, mine, near_block, far_block, far_block]
-                + [whole] * len(given)
+                + [whole(*g.shape) for g in given]
                 + [ANY] * len(after),
-                out_specs=whole,
-                scratch_shapes=[pltpu.VMEM((count, rows, width), BF), pltpu.SemaphoreType.DMA((count,))],
+                out_specs=[whole(*o.shape) for o in outs] if last else whole(*outs.shape),
+                scratch_shapes=scratch,
             ),
-            out_shape=shape(8 * hid, rows, dtype=F32),
+            out_shape=outs,
             compiler_params=PARAMS,
-            cost_estimate=cost(16 * hid * width * count, 16 * hid * rows * width * count, 1),
+            cost_estimate=cost(16 * hid * width * count, 16 * hid * rows * width * count, 1 if last else 1),
         )(spot, *[blocks[m] for m in arrays], *own, near, *far, *given, *after)
 
     def cut(spot, gate_t, up_t, width, ds, first, count, after=()):
@@ -227,7 +241,7 @@
             ),
             out_shape=[shape(count, 2, hid, width)] * len(ds),
             compiler_params=PARAMS,
-            cost_estimate=cost(8 * len(ds) * count * hid * width, 0, 20),
+            cost_estimate=cost(8 * len(ds) * count * hid * width, 0, 1),
         )(spot, *[gate_t, up_t] * len(ds), *after)
 
     def mix(side, pieces, share, dc, total=None):
@@ -291,6 +305,11 @@
         parts = [jnp.concatenate([joined(p) for p in parts[i :: len(extra) // EXTRA]]) for i in range(len(extra) // EXTRA)]
         total = jnp.concatenate([jnp.sum(p, axis=0, keepdims=True) for p in parts], axis=1)
 
+        def far_cut(i, after):
+            return cut(spot, *own, width, (2,) if paired else (2, 3), cuts[i][0], len(cuts[i]), after=after)
+
+        first_sends = far_cut(0, (blocks[0],))
+
         def first_moves(given, outs):
             _, quad = place()
             g = lax.axis_index("groups") if share > 1 else 0
@@ -303,7 +322,7 @@
                         moves.append((given[0], (slice(None), columns), outs[other], (y, p)))
             return moves
 
-        keep, send = move(first_moves, [shape(2, planes, hid, part)] * 2, down_weight)
+        keep, send = move(first_moves, [shape(2, planes, hid, part)] * 2, down_weight, after=first_sends)
         came = lax.ppermute(send, "gx", flip(1))
 
         def second_moves(given, outs):
@@ -315,15 +334,13 @@
 
         far = []
         for i, js in enumerate(cuts):
-            sends = cut(spot, *own, width, (2,) if paired else (2, 3), js[0], len(js), after=((send,) if far else (blocks[0],)))
+            sends = far_cut(1, (send, *blocks[3:5])) if i else first_sends
             if paired:
                 brought = lax.ppermute(sends[0], ("groups", "gx"), far_flip())
                 far.append((brought, lax.ppermute(brought, "groups", [(i, i ^ 1) for i in range(groups)])))
             else:
                 far.append(tuple(lax.ppermute(w, "gx", flip(d)) for d, w in zip((2, 3), sends)))
-        near = lax.ppermute(cut(spot, *own, width, (1,), 0, planes, after=(blocks[0],))[0], "gx", flip(1))
-
-        sums = product(spot, rows, blocks, own, near, far[0], cuts[0])
+        near = lax.ppermute(cut(spot, *own, width, (1,), 0, planes, after=first_sends)[0], "gx", flip(1))
 
 
         def third_moves(ks, given, outs):
@@ -337,8 +354,9 @@
             return moves
 
         ready = move(
-            functools.partial(third_moves, range(planes)), [shape(2, 2, hid, part)] * planes, keep, came, across, after=(sums, *blocks[-4:-2])
+            functools.partial(third_moves, range(planes)), [shape(2, 2, hid, part)] * planes, keep, came, across, after=blocks[-4:-2]
         )
+        sums = product(spot, rows, blocks, own, near, far[0], cuts[0], after=(across,))
         held = [lax.ppermute(h, "gx", shift(-k)) if k else h for k, h in enumerate(ready)]
         pieces = list(held)
         for r in range(1, share):
@@ -347,12 +365,11 @@
         crossed = pieces[planes:] if share > 1 else held
         one, two, three = held[1], held[2 % planes], held[-1]
         x0, x1, x2, x3 = crossed[0], crossed[1], crossed[2 % planes], crossed[-1]
-        later = [(two,), (one,), (three, x2)]
-        sums = product(spot, rows, blocks, own, near, far[1], cuts[1], sums, after=(x0,))
-        send = stage(leave, [shape(EXTRA + 4 * hid, rows)], sums, total, after=())[0]
+        later = [(one, two), (), (three, x2, x1)]
+        keep, send = product(spot, rows, blocks, own, near, far[1], cuts[1], sums, total, after=(x0,))
         came = lax.ppermute(send, "gx", flip(1))
         mine, total, send = stage(
-            meet, [shape(2 * hid, rows, dtype=F32), shape(1, rows, dtype=F32), shape(EXTRA + 2 * hid, rows)], sums, total, came,
+            meet, [shape(2 * hid, rows, dtype=F32), shape(1, rows, dtype=F32), shape(EXTRA + 2 * hid, rows)], keep, total, came,
             after=later[0],
         )
         came = lax.ppermute(send, "gx", flip(2))

time: 160 us -> 157 us (0.981)
  waiting for transfers between devices: 72.3 us -> 67.1 us
  local copies, waits for them, and re-layouts: 4.2 us -> 0.7 us
  starting transfers between devices: 50.4 us -> 53.1 us
  Pallas kernels: 27.3 us -> 29.3 us
    ppermute x2, waiting for transfers between devices: 0.01 us -> 11.5 us  [body(): lax.ppermute(brought, 'groups', [(i, i ^ 1) for i in range(groups)])]
    ppermute x7, starting transfers between devices: 4.12 us -> 12.6 us  [body(): lax.ppermute(hidden, 'gx', shift(-k, d))]
    ppermute x7, waiting for transfers between devices: 17.1 us -> 11.3 us  [body(): lax.ppermute(hidden, 'gx', shift(-k, d))]
    ppermute x3, starting transfers between devices: 10.2 us -> 4.4 us  [body(): lax.ppermute(h, 'gx', shift(-k))]
    ppermute x6, waiting for transfers between devices: 27.8 us -> 23.4 us  [body(): lax.ppermute(blocks[0] if s == 1 else blocks[-2], 'gx', line(s, way))]
    ppermute x1, waiting for transfers between devices: 3.91 us -> 0.01 us  [body(): across = lax.ppermute(send, 'gx', flip(2))]
    ppermute x4, waiting for transfers between devices: 3.86 us -> 0.01 us  [body(): pieces += [lax.ppermute(h, 'groups', swap(r)) for h in held]]
    unnamed x14 -> x6, local copies, waits for them, and re-layouts: 3.52 us -> 0.01 us
  transfers between devices with their start and end apart: 30 -> 30, of which waited for: 12 -> 9; matrix products, arithmetic and copies ran while one was open for 2% -> 2% of each run, Pallas kernels for 15% -> 16%
where the time goes in v4:
time: 157 us; the launch traced here: 156 us
  waiting for transfers between devices  67.1 us (43%)
  starting transfers between devices  53.1 us (34%)
  Pallas kernels  29.3 us (19%)
  other arithmetic  5.86 us (4%)
    ppermute x6, waiting for transfers between devices, body(): lax.ppermute(blocks[0] if s == 1 else blocks[-2], 'gx', line(s, way))  23.4 us
    ppermute x3, waiting for transfers between devices, body(): lax.ppermute(h, 'gx', shift(-k))  17.5 us
    pallas_call x2, Pallas kernels, product(): pl.pallas_call(kernel, grid_spec=pltpu.PrefetchScalarGridSpec(num_scalar_...  12.9 us
    ppermute x7, starting transfers between devices, body(): lax.ppermute(hidden, 'gx', shift(-k, d))  12.6 us
    ppermute x2, waiting for transfers between devices, body(): lax.ppermute(brought, 'groups', [(i, i ^ 1) for i in range(groups)])  11.5 us
    ppermute x7, waiting for transfers between devices, body(): lax.ppermute(hidden, 'gx', shift(-k, d))  11.3 us
    ppermute x6, starting transfers between devices, body(): lax.ppermute(blocks[0] if s == 1 else blocks[-2], 'gx', line(s, way))  11 us
    pallas_call x3, Pallas kernels, cut(): pl.pallas_call(kernel, grid_spec=pltpu.PrefetchScalarGridSpec(num_scalar_...  7.21 us
  transfers between devices with their start and end apart: 30, of which 9 were waited for; matrix products, arithmetic and copies ran while one was open for 2% of the time, Pallas kernels for 16%

profile of v4, /device:TPU:1, one launch (start us, length us, event | category | flops | bytes accessed | tf_op | source)
XLA Modules:
  0.0 156.2 jit_solution(1599013742756417911)
XLA Ops:
  0.0 1.8 %fusion.1 = (bf16[512,1024]{1,0:T(8,128)(2,1)S(1)}, f32[512]{0:T(512)S(1)}) fusion(bf16[512,1024]{1,0:T(8,128)(2,1)} %param.6, f32[1024]{0:T(1024)} %param.7), kind=kLoop, calls=%fused_computation.4 | loop fusion | flops 2620928 | bytes 2103296 | tf_op jit(solution)/shard_map/convert_element_type | solution.py:299
  4.2 5.7 %collective-permute-start = (bf16[528,1024]{1,0:T(8,128)(2,1)}, bf16[528,1024]{1,0:T(8,128)(2,1)}, u32[]{:S(2)}, u32[]{:S(2)}) collective-permute-start(bf16[528,1024]{1,0:T(8,128)(2,1)} %fusion.3.refs_2_.refs_0_), channel_id=1, source_target_pairs={{0,4},{1,5},{2,6},{3,7},{4,8},{5,9},{6,10},{7,11},{8,12},{9,13},{1... | collective-permute-start | bytes 3244040 | tf_op jit(solution)/shard_map/ppermute | solution.py:303
  10.7 2.6 %shard_map.64.refs_2_.refs_1_ = bf16[3,2,104,1024]{3,2,1,0:T(8,128)(2,1)S(1)} custom-call(s32[11]{0:T(128)S(1)} %pad_add_fusion.spot, bf16[104,16384]{1,0:T(8,128)(2,1)S(1)} %bitcast.12, bf16[104,16384]{1,0:T(8,128)(2,1)} %bitcast.13, bf16[528,1024]{1,0:T(8,128)(2,1)} %fusion.3.refs_2_.refs_0_), custom_call_target="tpu_custom_call" | custom-call | bytes 2555904 | tf_op jit(solution)/shard_map/pallas_call | solution.py:234
  14.7 2.1 %shard_map.66 = (bf16[2,4,104,512]{3,2,1,0:T(8,128)(2,1)S(1)}, bf16[2,4,104,512]{3,2,1,0:T(8,128)(2,1)S(1)}) custom-call(bf16[104,16384]{1,0:T(8,128)(2,1)} %refs_0_.1, bf16[3,2,104,1024]{3,2,1,0:T(8,128)(2,1)S(1)} %shard_map.64.refs_2_.refs_1_), custom_call_target="tpu_custom_call" | custom-call | bytes 3407872 | tf_op jit(solution)/shard_map/pallas_call | solution.py:33
  16.8 1.6 %collective-permute-start.7 = (bf16[2,4,104,512]{3,2,1,0:T(8,128)(2,1)S(1)}, bf16[2,4,104,512]{3,2,1,0:T(8,128)(2,1)S(1)}, u32[]{:S(2)}, u32[]{:S(2)}) collective-permute-start(bf16[2,4,104,512]{3,2,1,0:T(8,128)(2,1)S(1)} %get-tuple-element.17), channel_id=1, source_target_pairs={{0,1},{1,0},{2,3},{3,2},{4,5},{5,4},{6,7},{7,6},{8,9},{9,8},{10,11... | collective-permute-start | bytes 2555912 | tf_op jit(solution)/shard_map/ppermute | solution.py:326
  18.4 12.4 %collective-permute-done.2.refs_2_ = bf16[528,1024]{1,0:T(8,128)(2,1)} collective-permute-done((bf16[528,1024]{1,0:T(8,128)(2,1)}, bf16[528,1024]{1,0:T(8,128)(2,1)}, u32[]{:S(2)}, u32[]{:S(2)}) %collective-permute-start.2) | collective-permute-done | bytes 1081376 | tf_op jit(solution)/shard_map/ppermute | solution.py:303
  32.8 3.0 %shard_map.65 = bf16[4,2,104,1024]{3,2,1,0:T(8,128)(2,1)S(1)} custom-call(s32[11]{0:T(128)S(1)} %pad_add_fusion.spot, bf16[104,16384]{1,0:T(8,128)(2,1)} %bitcast.8, bf16[104,16384]{1,0:T(8,128)(2,1)} %bitcast.14, bf16[3,2,104,1024]{3,2,1,0:T(8,128)(2,1)S(1)} %shard_map.64.refs_2_.refs_1_), custom_call_target="tpu_custom_call" | custom-call | bytes 3407872 | tf_op jit(solution)/shard_map/pallas_call | solution.py:234
  38.7 3.4 %collective-permute-done.10.refs_8_ = bf16[3,2,104,1024]{3,2,1,0:T(8,128)(2,1)S(1)} collective-permute-done((bf16[3,2,104,1024]{3,2,1,0:T(8,128)(2,1)S(1)}, bf16[3,2,104,1024]{3,2,1,0:T(8,128)(2,1)S(1)}, u32[]{:S(2)}, u32[]{:S(2)}) %collective-permute-start.10) | collective-permute-done | bytes 1277984 | tf_op jit(solution)/shard_map/ppermute | solution.py:339
  42.1 4.0 %collective-permute-start.11 = (bf16[3,2,104,1024]{3,2,1,0:T(8,128)(2,1)S(1)}, bf16[3,2,104,1024]{3,2,1,0:T(8,128)(2,1)}, u32[]{:S(2)}, u32[]{:S(2)}) collective-permute-start(bf16[3,2,104,1024]{3,2,1,0:T(8,128)(2,1)S(1)} %collective-permute-done.10.refs_8_), channel_id=1, source_target_pairs={{0,16},{16,0},{1,17},{17,1},{2,18},{18,2},{3,19},{19,3},{4,20},{20... | collective-permute-start | bytes 3833864 | tf_op jit(solution)/shard_map/ppermute | solution.py:340
  46.1 11.0 %collective-permute-done.3.refs_4_.refs_1_ = bf16[528,1024]{1,0:T(8,128)(2,1)} collective-permute-done((bf16[528,1024]{1,0:T(8,128)(2,1)}, bf16[528,1024]{1,0:T(8,128)(2,1)}, u32[]{:S(2)}, u32[]{:S(2)}) %collective-permute-start.3) | collective-permute-done | bytes 1081376 | tf_op jit(solution)/shard_map/ppermute | solution.py:303
  60.6 1.6 %shard_map.68 = bf16[1,2,104,1024]{3,2,1,0:T(8,128)(2,1)S(1)} custom-call(s32[11]{0:T(128)S(1)} %pad_add_fusion.spot, bf16[104,16384]{1,0:T(8,128)(2,1)} %bitcast.9, bf16[104,16384]{1,0:T(8,128)(2,1)} %bitcast.15, bf16[2,4,104,512]{3,2,1,0:T(8,128)(2,1)S(1)} %shard_map.67.refs_2_, bf16[528,1024]{1,0:T(8,128)(2,1)S(1)} %collective-permute-done.1.refs_3_.refs_0_, ...), custom_call_target="tpu_custom_call" | custom-call | bytes 851968 | tf_op jit(solution)/shard_map/pallas_call | solution.py:234
  63.9 3.6 %collective-permute-start.13 = (bf16[2,2,104,512]{3,2,1,0:T(8,128)(2,1)S(1)}, bf16[2,2,104,512]{3,2,1,0:T(8,128)(2,1)S(1)}, u32[]{:S(2)}, u32[]{:S(2)}) collective-permute-start(bf16[2,2,104,512]{3,2,1,0:T(8,128)(2,1)S(1)} %get-tuple-element.18.refs_0_), channel_id=1, source_target_pairs={{16,0},{0,16},{17,1},{1,17},{18,2},{2,18},{19,3},{3,19},{20,4},{4,... | collective-permute-start | bytes 1277960 | tf_op jit(solution)/shard_map/ppermute | solution.py:363
  67.5 6.2 %collective-permute-done.11.refs_9_ = bf16[3,2,104,1024]{3,2,1,0:T(8,128)(2,1)} collective-permute-done((bf16[3,2,104,1024]{3,2,1,0:T(8,128)(2,1)S(1)}, bf16[3,2,104,1024]{3,2,1,0:T(8,128)(2,1)}, u32[]{:S(2)}, u32[]{:S(2)}) %collective-permute-start.11) | collective-permute-done | bytes 1277984 | tf_op jit(solution)/shard_map/ppermute | solution.py:340
  73.7 1.7 %collective-permute-start.15 = (bf16[2,2,104,512]{3,2,1,0:T(8,128)(2,1)S(1)}, bf16[2,2,104,512]{3,2,1,0:T(8,128)(2,1)S(1)}, u32[]{:S(2)}, u32[]{:S(2)}) collective-permute-start(bf16[2,2,104,512]{3,2,1,0:T(8,128)(2,1)S(1)} %get-tuple-element.21), channel_id=1, source_target_pairs={{0,12},{1,13},{2,14},{3,15},{4,0},{5,1},{6,2},{7,3},{8,4},{9,5},{1... | collective-permute-start | bytes 1277960 | tf_op jit(solution)/shard_map/ppermute | solution.py:360
  75.4 8.2 %shard_map.69.refs_9_ = f32[832,512]{1,0:T(8,128)} custom-call(s32[11]{0:T(128)S(1)} %pad_add_fusion.spot, bf16[528,1024]{1,0:T(8,128)(2,1)} %fusion.3.refs_2_.refs_0_, bf16[528,1024]{1,0:T(8,128)(2,1)} %collective-permute-done.refs_1_, bf16[528,1024]{1,0:T(8,128)(2,1)} %collective-permute-done.2.refs_2_, ...), custom_call_target="tpu_custom_call" | custom-call | flops 2617245696 | bytes 5111808 | tf_op jit(solution)/shard_map/pallas_call | solution.py:201
  86.8 5.4 %collective-permute-done.9.refs_8_ = bf16[1,2,104,1024]{3,2,1,0:T(8,128)(2,1)S(1)} collective-permute-done((bf16[1,2,104,1024]{3,2,1,0:T(8,128)(2,1)S(1)}, bf16[1,2,104,1024]{3,2,1,0:T(8,128)(2,1)S(1)}, u32[]{:S(2)}, u32[]{:S(2)}) %collective-permute-start.9) | collective-permute-done | bytes 426016 | tf_op jit(solution)/shard_map/ppermute | solution.py:340
  92.1 4.8 %shard_map.71 = (f32[416,512]{1,0:T(8,128)S(1)}, bf16[432,512]{1,0:T(8,128)(2,1)S(1)}) custom-call(s32[11]{0:T(128)S(1)} %pad_add_fusion.spot, bf16[528,1024]{1,0:T(8,128)(2,1)S(1)} %collective-permute-done.1.refs_3_.refs_0_, bf16[528,1024]{1,0:T(8,128)(2,1)} %collective-permute-done.3.refs_4_.refs_1_, bf16[528,1024]{1,0:T(8,128)(2,1)S(1)} %collective-permute-done.4.refs_2_, ...), custom_call_target="tpu_custom_call" | custom-call | flops 872415232 | bytes 1703936 | tf_op jit(solution)/shard_map/pallas_call | solution.py:201
  96.9 5.0 %collective-permute-start.14 = (bf16[432,512]{1,0:T(8,128)(2,1)S(1)}, bf16[432,512]{1,0:T(8,128)(2,1)S(1)}, u32[]{:S(2)}, u32[]{:S(2)}) collective-permute-start(bf16[432,512]{1,0:T(8,128)(2,1)S(1)} %get-tuple-element.20), channel_id=1, source_target_pairs={{0,1},{1,0},{2,3},{3,2},{4,5},{5,4},{6,7},{7,6},{8,9},{9,8},{10,11... | collective-permute-start | bytes 1327112 | tf_op jit(solution)/shard_map/ppermute | solution.py:370
  106.5 16.4 %collective-permute-done.25.refs_8_.refs_3_ = bf16[2,2,104,512]{3,2,1,0:T(8,128)(2,1)S(1)} collective-permute-done((bf16[2,2,104,512]{3,2,1,0:T(8,128)(2,1)S(1)}, bf16[2,2,104,512]{3,2,1,0:T(8,128)(2,1)S(1)}, u32[]{:S(2)}, u32[]{:S(2)}) %collective-permute-start.25) | collective-permute-done | bytes 426016 | tf_op jit(solution)/shard_map/ppermute | solution.py:360
  126.8 6.4 %collective-permute-start.21 = (bf16[104,512]{1,0:T(8,128)(2,1)S(1)}, bf16[104,512]{1,0:T(8,128)(2,1)S(1)}, u32[]{:S(2)}, u32[]{:S(2)}) collective-permute-start(bf16[104,512]{1,0:T(8,128)(2,1)S(1)} %shard_map.73.refs_0_), channel_id=1, source_target_pairs={{0,8},{1,9},{2,10},{3,11},{4,12},{5,13},{6,14},{7,15},{8,0},{9,1},... | collective-permute-start | bytes 319496 | tf_op jit(solution)/shard_map/ppermute | solution.py:377
  134.6 2.1 %collective-permute-start.24 = (bf16[104,512]{1,0:T(8,128)(2,1)S(1)}, bf16[104,512]{1,0:T(8,128)(2,1)S(1)}, u32[]{:S(2)}, u32[]{:S(2)}) collective-permute-start(bf16[104,512]{1,0:T(8,128)(2,1)S(1)} %shard_map.73.refs_0_), channel_id=1, source_target_pairs={{0,6},{1,7},{2,4},{3,5},{4,10},{5,11},{6,8},{7,9},{8,14},{9,15},{1... | collective-permute-start | bytes 319496 | tf_op jit(solution)/shard_map/ppermute | solution.py:377
  136.8 11.2 %collective-permute-done.22.refs_5_ = bf16[104,512]{1,0:T(8,128)(2,1)S(1)} collective-permute-done((bf16[104,512]{1,0:T(8,128)(2,1)S(1)}, bf16[104,512]{1,0:T(8,128)(2,1)S(1)}, u32[]{:S(2)}, u32[]{:S(2)}) %collective-permute-start.22) | collective-permute-done | bytes 106528 | tf_op jit(solution)/shard_map/ppermute | solution.py:377
  149.6 2.6 %shard_map.75.refs_8_ = f32[2,512,512]{2,1,0:T(8,128)} custom-call(bf16[4,2,104,512]{3,2,1,0:T(8,128)(2,1)S(1)} %shard_map.74.side, bf16[2,2,104,512]{3,2,1,0:T(8,128)(2,1)S(1)} %get-tuple-element.18.refs_0_, bf16[2,2,104,512]{3,2,1,0:T(8,128)(2,1)S(1)} %collective-permute-done.15.refs_3_.refs_1_, ...), custom_call_target="tpu_custom_call" | custom-call | flops 17448304640 | bytes 51118080 | tf_op jit(solution)/shard_map/pallas_call | solution.py:273
  152.3 3.9 %shard_map.76 = bf16[512,1024]{1,0:T(8,128)(2,1)} custom-call(bf16[4,2,104,512]{3,2,1,0:T(8,128)(2,1)S(1)} %collective-permute-done.28.side, bf16[2,2,104,512]{3,2,1,0:T(8,128)(2,1)S(1)} %get-tuple-element.18.refs_0_, bf16[2,2,104,512]{3,2,1,0:T(8,128)(2,1)S(1)} %collective-permute-done.15.refs_3_.refs_1_, ...), custom_call_target="tpu_custom_call" | custom-call | flops 17448304640 | bytes 51118080 | tf_op jit(solution)/shard_map/pallas_call | solution.py:273
  (68 shorter events, 29.2 us)
Async XLA Ops:
  2.9 27.9 %collective-permute-start.2 = (bf16[528,1024]{1,0:T(8,128)(2,1)}, bf16[528,1024]{1,0:T(8,128)(2,1)}, u32[]{:S(2)}, u32[]{:S(2)}) collective-permute-start(bf16[528,1024]{1,0:T(8,128)(2,1)} %fusion.3.refs_2_.refs_0_), channel_id=1, source_target_pairs={{4,0},{5,1},{6,2},{7,3},{8,4},{9,5},{10,6},{11,7},{12,8},{13,9},{1... | collective-permute-start | bytes 3244040 | tf_op jit(solution)/shard_map/ppermute | solution.py:303
  4.2 27.9 %collective-permute-start = (bf16[528,1024]{1,0:T(8,128)(2,1)}, bf16[528,1024]{1,0:T(8,128)(2,1)}, u32[]{:S(2)}, u32[]{:S(2)}) collective-permute-start(bf16[528,1024]{1,0:T(8,128)(2,1)} %fusion.3.refs_2_.refs_0_), channel_id=1, source_target_pairs={{0,4},{1,5},{2,6},{3,7},{4,8},{5,9},{6,10},{7,11},{8,12},{9,13},{1... | collective-permute-start | bytes 3244040 | tf_op jit(solution)/shard_map/ppermute | solution.py:303
  13.3 28.8 %collective-permute-start.10 = (bf16[3,2,104,1024]{3,2,1,0:T(8,128)(2,1)S(1)}, bf16[3,2,104,1024]{3,2,1,0:T(8,128)(2,1)S(1)}, u32[]{:S(2)}, u32[]{:S(2)}) collective-permute-start(bf16[3,2,104,1024]{3,2,1,0:T(8,128)(2,1)S(1)} %shard_map.64.refs_2_.refs_1_), channel_id=1, source_target_pairs={{0,2},{1,3},{2,0},{3,1},{4,6},{5,7},{6,4},{7,5},{8,10},{9,11},{10,... | collective-permute-start | bytes 3833864 | tf_op jit(solution)/shard_map/ppermute | solution.py:339
  16.8 20.3 %collective-permute-start.7 = (bf16[2,4,104,512]{3,2,1,0:T(8,128)(2,1)S(1)}, bf16[2,4,104,512]{3,2,1,0:T(8,128)(2,1)S(1)}, u32[]{:S(2)}, u32[]{:S(2)}) collective-permute-start(bf16[2,4,104,512]{3,2,1,0:T(8,128)(2,1)S(1)} %get-tuple-element.17), channel_id=1, source_target_pairs={{0,1},{1,0},{2,3},{3,2},{4,5},{5,4},{6,7},{7,6},{8,9},{9,8},{10,11... | collective-permute-start | bytes 2555912 | tf_op jit(solution)/shard_map/ppermute | solution.py:326
  30.8 26.3 %collective-permute-start.3 = (bf16[528,1024]{1,0:T(8,128)(2,1)}, bf16[528,1024]{1,0:T(8,128)(2,1)}, u32[]{:S(2)}, u32[]{:S(2)}) collective-permute-start(bf16[528,1024]{1,0:T(8,128)(2,1)} %collective-permute-done.2.refs_2_), channel_id=1, source_target_pairs={{4,0},{5,1},{6,2},{7,3},{8,4},{9,5},{10,6},{11,7},{20,16},{21,17},... | collective-permute-start | bytes 3244040 | tf_op jit(solution)/shard_map/ppermute | solution.py:303
  32.1 27.0 %collective-permute-start.1 = (bf16[528,1024]{1,0:T(8,128)(2,1)}, bf16[528,1024]{1,0:T(8,128)(2,1)S(1)}, u32[]{:S(2)}, u32[]{:S(2)}) collective-permute-start(bf16[528,1024]{1,0:T(8,128)(2,1)} %collective-permute-done.refs_1_), channel_id=1, source_target_pairs={{4,8},{5,9},{6,10},{7,11},{8,12},{9,13},{10,14},{11,15},{20,24},{2... | collective-permute-start | bytes 3244040 | tf_op jit(solution)/shard_map/ppermute | solution.py:303
  35.8 28.0 %collective-permute-start.6 = (bf16[4,2,104,1024]{3,2,1,0:T(8,128)(2,1)S(1)}, bf16[4,2,104,1024]{3,2,1,0:T(8,128)(2,1)S(1)}, u32[]{:S(2)}, u32[]{:S(2)}) collective-permute-start(bf16[4,2,104,1024]{3,2,1,0:T(8,128)(2,1)S(1)} %shard_map.65), channel_id=1, source_target_pairs={{0,1},{1,0},{2,3},{3,2},{4,5},{5,4},{6,7},{7,6},{8,9},{9,8},{10,11... | collective-permute-start | bytes 5111816 | tf_op jit(solution)/shard_map/ppermute | solution.py:343
  37.2 25.0 %collective-permute-start.12 = (bf16[2,4,104,512]{3,2,1,0:T(8,128)(2,1)S(1)}, bf16[2,4,104,512]{3,2,1,0:T(8,128)(2,1)S(1)}, u32[]{:S(2)}, u32[]{:S(2)}) collective-permute-start(bf16[2,4,104,512]{3,2,1,0:T(8,128)(2,1)S(1)} %shard_map.67.refs_2_), channel_id=1, source_target_pairs={{0,2},{1,3},{2,0},{3,1},{4,6},{5,7},{6,4},{7,5},{8,10},{9,11},{10,... | collective-permute-start | bytes 2555912 | tf_op jit(solution)/shard_map/ppermute | solution.py:333
  42.1 31.6 %collective-permute-start.11 = (bf16[3,2,104,1024]{3,2,1,0:T(8,128)(2,1)S(1)}, bf16[3,2,104,1024]{3,2,1,0:T(8,128)(2,1)}, u32[]{:S(2)}, u32[]{:S(2)}) collective-permute-start(bf16[3,2,104,1024]{3,2,1,0:T(8,128)(2,1)S(1)} %collective-permute-done.10.refs_8_), channel_id=1, source_target_pairs={{0,16},{16,0},{1,17},{17,1},{2,18},{18,2},{3,19},{19,3},{4,20},{20... | collective-permute-start | bytes 3833864 | tf_op jit(solution)/shard_map/ppermute | solution.py:340
  57.1 27.7 %collective-permute-start.5 = (bf16[528,1024]{1,0:T(8,128)(2,1)}, bf16[528,1024]{1,0:T(8,128)(2,1)}, u32[]{:S(2)}, u32[]{:S(2)}) collective-permute-start(bf16[528,1024]{1,0:T(8,128)(2,1)} %collective-permute-done.3.refs_4_.refs_1_), channel_id=1, source_target_pairs={{4,0},{5,1},{6,2},{7,3},{20,16},{21,17},{22,18},{23,19}} | collective-permute-start | bytes 3244040 | tf_op jit(solution)/shard_map/ppermute | solution.py:303
  59.1 27.6 %collective-permute-start.4 = (bf16[528,1024]{1,0:T(8,128)(2,1)S(1)}, bf16[528,1024]{1,0:T(8,128)(2,1)S(1)}, u32[]{:S(2)}, u32[]{:S(2)}) collective-permute-start(bf16[528,1024]{1,0:T(8,128)(2,1)S(1)} %collective-permute-done.1.refs_3_.refs_0_), channel_id=1, source_target_pairs={{8,12},{9,13},{10,14},{11,15},{24,28},{25,29},{26,30},{27,31}} | collective-permute-start | bytes 3244040 | tf_op jit(solution)/shard_map/ppermute | solution.py:303
  62.2 21.4 %collective-permute-start.8 = (bf16[1,2,104,1024]{3,2,1,0:T(8,128)(2,1)S(1)}, bf16[1,2,104,1024]{3,2,1,0:T(8,128)(2,1)S(1)}, u32[]{:S(2)}, u32[]{:S(2)}) collective-permute-start(bf16[1,2,104,1024]{3,2,1,0:T(8,128)(2,1)S(1)} %shard_map.68), channel_id=1, source_target_pairs={{0,2},{1,3},{2,0},{3,1},{4,6},{5,7},{6,4},{7,5},{8,10},{9,11},{10,... | collective-permute-start | bytes 1277960 | tf_op jit(solution)/shard_map/ppermute | solution.py:339
  63.9 22.9 %collective-permute-start.13 = (bf16[2,2,104,512]{3,2,1,0:T(8,128)(2,1)S(1)}, bf16[2,2,104,512]{3,2,1,0:T(8,128)(2,1)S(1)}, u32[]{:S(2)}, u32[]{:S(2)}) collective-permute-start(bf16[2,2,104,512]{3,2,1,0:T(8,128)(2,1)S(1)} %get-tuple-element.18.refs_0_), channel_id=1, source_target_pairs={{16,0},{0,16},{17,1},{1,17},{18,2},{2,18},{19,3},{3,19},{20,4},{4,... | collective-permute-start | bytes 1277960 | tf_op jit(solution)/shard_map/ppermute | solution.py:363
  73.7 31.9 %collective-permute-start.15 = (bf16[2,2,104,512]{3,2,1,0:T(8,128)(2,1)S(1)}, bf16[2,2,104,512]{3,2,1,0:T(8,128)(2,1)S(1)}, u32[]{:S(2)}, u32[]{:S(2)}) collective-permute-start(bf16[2,2,104,512]{3,2,1,0:T(8,128)(2,1)S(1)} %get-tuple-element.21), channel_id=1, source_target_pairs={{0,12},{1,13},{2,14},{3,15},{4,0},{5,1},{6,2},{7,3},{8,4},{9,5},{1... | collective-permute-start | bytes 1277960 | tf_op jit(solution)/shard_map/ppermute | solution.py:360
  83.6 20.9 %collective-permute-start.16 = (bf16[2,2,104,512]{3,2,1,0:T(8,128)(2,1)S(1)}, bf16[2,2,104,512]{3,2,1,0:T(8,128)(2,1)S(1)}, u32[]{:S(2)}, u32[]{:S(2)}) collective-permute-start(bf16[2,2,104,512]{3,2,1,0:T(8,128)(2,1)S(1)} %get-tuple-element.22), channel_id=1, source_target_pairs={{0,8},{1,9},{2,10},{3,11},{4,12},{5,13},{6,14},{7,15},{8,0},{9,1},... | collective-permute-start | bytes 1277960 | tf_op jit(solution)/shard_map/ppermute | solution.py:360
  101.9 21.0 %collective-permute-start.25 = (bf16[2,2,104,512]{3,2,1,0:T(8,128)(2,1)S(1)}, bf16[2,2,104,512]{3,2,1,0:T(8,128)(2,1)S(1)}, u32[]{:S(2)}, u32[]{:S(2)}) collective-permute-start(bf16[2,2,104,512]{3,2,1,0:T(8,128)(2,1)S(1)} %get-tuple-element.26), channel_id=1, source_target_pairs={{0,4},{1,5},{2,6},{3,7},{4,8},{5,9},{6,10},{7,11},{8,12},{9,13},{1... | collective-permute-start | bytes 1277960 | tf_op jit(solution)/shard_map/ppermute | solution.py:360
  104.5 22.3 %collective-permute-start.26 = (bf16[2,2,104,512]{3,2,1,0:T(8,128)(2,1)S(1)}, bf16[2,2,104,512]{3,2,1,0:T(8,128)(2,1)S(1)}, u32[]{:S(2)}, u32[]{:S(2)}) collective-permute-start(bf16[2,2,104,512]{3,2,1,0:T(8,128)(2,1)S(1)} %collective-permute-done.16.refs_4_.refs_2_), channel_id=1, source_target_pairs={{16,0},{0,16},{17,1},{1,17},{18,2},{2,18},{19,3},{3,19},{20,4},{4,... | collective-permute-start | bytes 1277960 | tf_op jit(solution)/shard_map/ppermute | solution.py:363
  105.6 21.2 %collective-permute-start.27 = (bf16[2,2,104,512]{3,2,1,0:T(8,128)(2,1)S(1)}, bf16[2,2,104,512]{3,2,1,0:T(8,128)(2,1)S(1)}, u32[]{:S(2)}, u32[]{:S(2)}) collective-permute-start(bf16[2,2,104,512]{3,2,1,0:T(8,128)(2,1)S(1)} %collective-permute-done.15.refs_3_.refs_1_), channel_id=1, source_target_pairs={{16,0},{0,16},{17,1},{1,17},{18,2},{2,18},{19,3},{3,19},{20,4},{4,... | collective-permute-start | bytes 1277960 | tf_op jit(solution)/shard_map/ppermute | solution.py:363
  106.0 18.0 %collective-permute-start.17 = (bf16[224,512]{1,0:T(8,128)(2,1)S(1)}, bf16[224,512]{1,0:T(8,128)(2,1)S(1)}, u32[]{:S(2)}, u32[]{:S(2)}) collective-permute-start(bf16[224,512]{1,0:T(8,128)(2,1)S(1)} %get-tuple-element.25), channel_id=1, source_target_pairs={{0,2},{1,3},{2,0},{3,1},{4,6},{5,7},{6,4},{7,5},{8,10},{9,11},{10,... | collective-permute-start | bytes 688136 | tf_op jit(solution)/shard_map/ppermute | solution.py:375
  122.9 26.8 %collective-permute-start.29 = (bf16[2,2,104,512]{3,2,1,0:T(8,128)(2,1)S(1)}, bf16[2,2,104,512]{3,2,1,0:T(8,128)(2,1)S(1)}, u32[]{:S(2)}, u32[]{:S(2)}) collective-permute-start(bf16[2,2,104,512]{3,2,1,0:T(8,128)(2,1)S(1)} %collective-permute-done.25.refs_8_.refs_3_), channel_id=1, source_target_pairs={{16,0},{0,16},{17,1},{1,17},{18,2},{2,18},{19,3},{3,19},{20,4},{4,... | collective-permute-start | bytes 1277960 | tf_op jit(solution)/shard_map/ppermute | solution.py:363
  126.8 10.1 %collective-permute-start.21 = (bf16[104,512]{1,0:T(8,128)(2,1)S(1)}, bf16[104,512]{1,0:T(8,128)(2,1)S(1)}, u32[]{:S(2)}, u32[]{:S(2)}) collective-permute-start(bf16[104,512]{1,0:T(8,128)(2,1)S(1)} %shard_map.73.refs_0_), channel_id=1, source_target_pairs={{0,8},{1,9},{2,10},{3,11},{4,12},{5,13},{6,14},{7,15},{8,0},{9,1},... | collective-permute-start | bytes 319496 | tf_op jit(solution)/shard_map/ppermute | solution.py:377
  133.2 14.8 %collective-permute-start.22 = (bf16[104,512]{1,0:T(8,128)(2,1)S(1)}, bf16[104,512]{1,0:T(8,128)(2,1)S(1)}, u32[]{:S(2)}, u32[]{:S(2)}) collective-permute-start(bf16[104,512]{1,0:T(8,128)(2,1)S(1)} %shard_map.73.refs_0_), channel_id=1, source_target_pairs={{0,10},{1,11},{2,8},{3,9},{4,14},{5,15},{6,12},{7,13},{8,2},{9,3},... | collective-permute-start | bytes 319496 | tf_op jit(solution)/shard_map/ppermute | solution.py:377
  134.2 13.9 %collective-permute-start.23 = (bf16[104,512]{1,0:T(8,128)(2,1)S(1)}, bf16[104,512]{1,0:T(8,128)(2,1)S(1)}, u32[]{:S(2)}, u32[]{:S(2)}) collective-permute-start(bf16[104,512]{1,0:T(8,128)(2,1)S(1)} %shard_map.73.refs_0_), channel_id=1, source_target_pairs={{0,4},{1,5},{2,6},{3,7},{4,8},{5,9},{6,10},{7,11},{8,12},{9,13},{1... | collective-permute-start | bytes 319496 | tf_op jit(solution)/shard_map/ppermute | solution.py:377
  134.6 13.4 %collective-permute-start.24 = (bf16[104,512]{1,0:T(8,128)(2,1)S(1)}, bf16[104,512]{1,0:T(8,128)(2,1)S(1)}, u32[]{:S(2)}, u32[]{:S(2)}) collective-permute-start(bf16[104,512]{1,0:T(8,128)(2,1)S(1)} %shard_map.73.refs_0_), channel_id=1, source_target_pairs={{0,6},{1,7},{2,4},{3,5},{4,10},{5,11},{6,8},{7,9},{8,14},{9,15},{1... | collective-permute-start | bytes 319496 | tf_op jit(solution)/shard_map/ppermute | solution.py:377
  (9 other events, 88.4 us)

commit v5 on v4

--- a/solution.py
+++ b/solution.py
@@ -212,7 +212,7 @@
             ),
             out_shape=outs,
             compiler_params=PARAMS,
-            cost_estimate=cost(16 * hid * width * count, 16 * hid * rows * width * count, 1 if last else 1),
+            cost_estimate=cost(16 * hid * width * count, 16 * hid * rows * width * count, 1),
         )(spot, *[blocks[m] for m in arrays], *own, near, *far, *given, *after)
 
     def cut(spot, gate_t, up_t, width, ds, first, count, after=()):
@@ -365,7 +365,7 @@
         crossed = pieces[planes:] if share > 1 else held
         one, two, three = held[1], held[2 % planes], held[-1]
         x0, x1, x2, x3 = crossed[0], crossed[1], crossed[2 % planes], crossed[-1]
-        later = [(one, two), (), (three, x2, x1)]
+        later = [(two,), (one,), (three, x2, x1)]
         keep, send = product(spot, rows, blocks, own, near, far[1], cuts[1], sums, total, after=(x0,))
         came = lax.ppermute(send, "gx", flip(1))
         mine, total, send = stage(
@@ -374,7 +374,12 @@
         )
         came = lax.ppermute(send, "gx", flip(2))
         hidden = stage(activate, [shape(hid, rows)], mine, total, came, after=later[1])[0]
-        beside = [lax.ppermute(hidden, "gx", shift(-k, d)) if k or d else hidden for k in range(planes) for d in (0, 2)]
+        column = {0: hidden}
+        for k in sorted(range(1, planes), key=lambda k: -min(k, planes - k)):
+            column[k] = lax.ppermute(hidden, "gx", shift(-k))
+        beside = []
+        for k in range(planes):
+            beside += [column[k], lax.ppermute(column[k], "gx", flip(2))]
         beside = move(
             lambda given, outs: [(a, ..., outs[0], (i // 2, i % 2)) for i, a in enumerate(given)],
             [shape(planes, 2, hid, rows)],

time: 157 us -> 151 us (0.962)
  starting transfers between devices: 53.1 us -> 45.3 us
  waiting for transfers between devices: 67.1 us -> 68.8 us
    ppermute x7, starting transfers between devices: 12.6 us -> 5.62 us  [the longest x4 3.94 us: body(): beside += [column[k], lax.ppermute(column[k], 'gx', flip(2))]]
    ppermute x2, starting transfers between devices: 6.59 us -> 4.75 us  [body(): came = lax.ppermute(send, 'gx', flip(1))]
    ppermute x2, waiting for transfers between devices: 11.5 us -> 13.2 us  [body(): lax.ppermute(brought, 'groups', [(i, i ^ 1) for i in range(groups)])]
  transfers between devices with their start and end apart: 30 -> 30, of which waited for: 9 -> 11; matrix products, arithmetic and copies ran while one was open for 2% -> 2% of each run, Pallas kernels for 16% -> 17%
where the time goes in v5:
time: 151 us; the launch traced here: 150 us
  waiting for transfers between devices  68.8 us (46%)
  starting transfers between devices  45.3 us (30%)
  Pallas kernels  29.3 us (19%)
  other arithmetic  5.86 us (4%)
    ppermute x6, waiting for transfers between devices, body(): lax.ppermute(blocks[0] if s == 1 else blocks[-2], 'gx', line(s, way))  23.4 us
    ppermute x3, waiting for transfers between devices, body(): lax.ppermute(h, 'gx', shift(-k))  16.6 us
    ppermute x2, waiting for transfers between devices, body(): lax.ppermute(brought, 'groups', [(i, i ^ 1) for i in range(groups)])  13.2 us
    pallas_call x2, Pallas kernels, product(): pl.pallas_call(kernel, grid_spec=pltpu.PrefetchScalarGridSpec(num_scalar_...  12.9 us
    ppermute x6, starting transfers between devices, body(): lax.ppermute(blocks[0] if s == 1 else blocks[-2], 'gx', line(s, way))  11 us
    ppermute x4, starting transfers between devices, body(): pieces += [lax.ppermute(h, 'groups', swap(r)) for h in held]  7.58 us
    ppermute x3, waiting for transfers between devices, body(): column[k] = lax.ppermute(hidden, 'gx', shift(-k))  7.34 us
    pallas_call x3, Pallas kernels, cut(): pl.pallas_call(kernel, grid_spec=pltpu.PrefetchScalarGridSpec(num_scalar_...  7.21 us
  transfers between devices with their start and end apart: 30, of which 11 were waited for; matrix products, arithmetic and copies ran while one was open for 2% of the time, Pallas kernels for 17%

profile of v5, /device:TPU:1, one launch (start us, length us, event | category | flops | bytes accessed | tf_op | source)
XLA Modules:
  0.0 150.1 jit_solution(2939276614791482446)
XLA Ops:
  0.0 1.8 %fusion.1 = (bf16[512,1024]{1,0:T(8,128)(2,1)S(1)}, f32[512]{0:T(512)S(1)}) fusion(bf16[512,1024]{1,0:T(8,128)(2,1)} %param.6, f32[1024]{0:T(1024)} %param.7), kind=kLoop, calls=%fused_computation.4 | loop fusion | flops 2620928 | bytes 2103296 | tf_op jit(solution)/shard_map/convert_element_type | solution.py:299
  4.2 5.7 %collective-permute-start = (bf16[528,1024]{1,0:T(8,128)(2,1)}, bf16[528,1024]{1,0:T(8,128)(2,1)}, u32[]{:S(2)}, u32[]{:S(2)}) collective-permute-start(bf16[528,1024]{1,0:T(8,128)(2,1)} %fusion.3.refs_2_.refs_0_), channel_id=1, source_target_pairs={{0,4},{1,5},{2,6},{3,7},{4,8},{5,9},{6,10},{7,11},{8,12},{9,13},{1... | collective-permute-start | bytes 3244040 | tf_op jit(solution)/shard_map/ppermute | solution.py:303
  10.7 2.6 %shard_map.64.refs_2_.refs_1_ = bf16[3,2,104,1024]{3,2,1,0:T(8,128)(2,1)S(1)} custom-call(s32[11]{0:T(128)S(1)} %pad_add_fusion.spot, bf16[104,16384]{1,0:T(8,128)(2,1)S(1)} %bitcast.12, bf16[104,16384]{1,0:T(8,128)(2,1)} %bitcast.13, bf16[528,1024]{1,0:T(8,128)(2,1)} %fusion.3.refs_2_.refs_0_), custom_call_target="tpu_custom_call" | custom-call | bytes 2555904 | tf_op jit(solution)/shard_map/pallas_call | solution.py:234
  14.7 2.1 %shard_map.66 = (bf16[2,4,104,512]{3,2,1,0:T(8,128)(2,1)S(1)}, bf16[2,4,104,512]{3,2,1,0:T(8,128)(2,1)S(1)}) custom-call(bf16[104,16384]{1,0:T(8,128)(2,1)} %refs_0_.1, bf16[3,2,104,1024]{3,2,1,0:T(8,128)(2,1)S(1)} %shard_map.64.refs_2_.refs_1_), custom_call_target="tpu_custom_call" | custom-call | bytes 3407872 | tf_op jit(solution)/shard_map/pallas_call | solution.py:33
  18.4 12.4 %collective-permute-done.2.refs_2_ = bf16[528,1024]{1,0:T(8,128)(2,1)} collective-permute-done((bf16[528,1024]{1,0:T(8,128)(2,1)}, bf16[528,1024]{1,0:T(8,128)(2,1)}, u32[]{:S(2)}, u32[]{:S(2)}) %collective-permute-start.2) | collective-permute-done | bytes 1081376 | tf_op jit(solution)/shard_map/ppermute | solution.py:303
  32.8 3.0 %shard_map.65 = bf16[4,2,104,1024]{3,2,1,0:T(8,128)(2,1)S(1)} custom-call(s32[11]{0:T(128)S(1)} %pad_add_fusion.spot, bf16[104,16384]{1,0:T(8,128)(2,1)} %bitcast.8, bf16[104,16384]{1,0:T(8,128)(2,1)} %bitcast.14, bf16[3,2,104,1024]{3,2,1,0:T(8,128)(2,1)S(1)} %shard_map.64.refs_2_.refs_1_), custom_call_target="tpu_custom_call" | custom-call | bytes 3407872 | tf_op jit(solution)/shard_map/pallas_call | solution.py:234
  38.7 3.4 %collective-permute-done.10.refs_8_ = bf16[3,2,104,1024]{3,2,1,0:T(8,128)(2,1)S(1)} collective-permute-done((bf16[3,2,104,1024]{3,2,1,0:T(8,128)(2,1)S(1)}, bf16[3,2,104,1024]{3,2,1,0:T(8,128)(2,1)S(1)}, u32[]{:S(2)}, u32[]{:S(2)}) %collective-permute-start.10) | collective-permute-done | bytes 1277984 | tf_op jit(solution)/shard_map/ppermute | solution.py:339
  42.1 4.0 %collective-permute-start.11 = (bf16[3,2,104,1024]{3,2,1,0:T(8,128)(2,1)S(1)}, bf16[3,2,104,1024]{3,2,1,0:T(8,128)(2,1)}, u32[]{:S(2)}, u32[]{:S(2)}) collective-permute-start(bf16[3,2,104,1024]{3,2,1,0:T(8,128)(2,1)S(1)} %collective-permute-done.10.refs_8_), channel_id=1, source_target_pairs={{0,16},{16,0},{1,17},{17,1},{2,18},{18,2},{3,19},{19,3},{4,20},{20... | collective-permute-start | bytes 3833864 | tf_op jit(solution)/shard_map/ppermute | solution.py:340
  46.1 11.0 %collective-permute-done.3.refs_4_.refs_1_ = bf16[528,1024]{1,0:T(8,128)(2,1)} collective-permute-done((bf16[528,1024]{1,0:T(8,128)(2,1)}, bf16[528,1024]{1,0:T(8,128)(2,1)}, u32[]{:S(2)}, u32[]{:S(2)}) %collective-permute-start.3) | collective-permute-done | bytes 1081376 | tf_op jit(solution)/shard_map/ppermute | solution.py:303
  60.6 1.6 %shard_map.68 = bf16[1,2,104,1024]{3,2,1,0:T(8,128)(2,1)S(1)} custom-call(s32[11]{0:T(128)S(1)} %pad_add_fusion.spot, bf16[104,16384]{1,0:T(8,128)(2,1)} %bitcast.9, bf16[104,16384]{1,0:T(8,128)(2,1)} %bitcast.15, bf16[2,4,104,512]{3,2,1,0:T(8,128)(2,1)S(1)} %shard_map.67.refs_2_, bf16[528,1024]{1,0:T(8,128)(2,1)S(1)} %collective-permute-done.1.refs_3_.refs_0_, ...), custom_call_target="tpu_custom_call" | custom-call | bytes 851968 | tf_op jit(solution)/shard_map/pallas_call | solution.py:234
  63.9 3.6 %collective-permute-start.13 = (bf16[2,2,104,512]{3,2,1,0:T(8,128)(2,1)S(1)}, bf16[2,2,104,512]{3,2,1,0:T(8,128)(2,1)S(1)}, u32[]{:S(2)}, u32[]{:S(2)}) collective-permute-start(bf16[2,2,104,512]{3,2,1,0:T(8,128)(2,1)S(1)} %get-tuple-element.18.refs_0_), channel_id=1, source_target_pairs={{16,0},{0,16},{17,1},{1,17},{18,2},{2,18},{19,3},{3,19},{20,4},{4,... | collective-permute-start | bytes 1277960 | tf_op jit(solution)/shard_map/ppermute | solution.py:363
  67.5 6.2 %collective-permute-done.11.refs_9_ = bf16[3,2,104,1024]{3,2,1,0:T(8,128)(2,1)} collective-permute-done((bf16[3,2,104,1024]{3,2,1,0:T(8,128)(2,1)S(1)}, bf16[3,2,104,1024]{3,2,1,0:T(8,128)(2,1)}, u32[]{:S(2)}, u32[]{:S(2)}) %collective-permute-start.11) | collective-permute-done | bytes 1277984 | tf_op jit(solution)/shard_map/ppermute | solution.py:340
  73.7 2.9 %collective-permute-start.15 = (bf16[2,2,104,512]{3,2,1,0:T(8,128)(2,1)S(1)}, bf16[2,2,104,512]{3,2,1,0:T(8,128)(2,1)S(1)}, u32[]{:S(2)}, u32[]{:S(2)}) collective-permute-start(bf16[2,2,104,512]{3,2,1,0:T(8,128)(2,1)S(1)} %get-tuple-element.21), channel_id=1, source_target_pairs={{0,8},{1,9},{2,10},{3,11},{4,12},{5,13},{6,14},{7,15},{8,0},{9,1},... | collective-permute-start | bytes 1277960 | tf_op jit(solution)/shard_map/ppermute | solution.py:360
  76.6 8.2 %shard_map.69.refs_9_ = f32[832,512]{1,0:T(8,128)} custom-call(s32[11]{0:T(128)S(1)} %pad_add_fusion.spot, bf16[528,1024]{1,0:T(8,128)(2,1)} %fusion.3.refs_2_.refs_0_, bf16[528,1024]{1,0:T(8,128)(2,1)} %collective-permute-done.refs_1_, bf16[528,1024]{1,0:T(8,128)(2,1)} %collective-permute-done.2.refs_2_, ...), custom_call_target="tpu_custom_call" | custom-call | flops 2617245696 | bytes 5111808 | tf_op jit(solution)/shard_map/pallas_call | solution.py:201
  87.0 7.1 %collective-permute-done.9.refs_8_ = bf16[1,2,104,1024]{3,2,1,0:T(8,128)(2,1)S(1)} collective-permute-done((bf16[1,2,104,1024]{3,2,1,0:T(8,128)(2,1)S(1)}, bf16[1,2,104,1024]{3,2,1,0:T(8,128)(2,1)S(1)}, u32[]{:S(2)}, u32[]{:S(2)}) %collective-permute-start.9) | collective-permute-done | bytes 426016 | tf_op jit(solution)/shard_map/ppermute | solution.py:340
  94.0 4.8 %shard_map.71 = (f32[416,512]{1,0:T(8,128)S(1)}, bf16[432,512]{1,0:T(8,128)(2,1)S(1)}) custom-call(s32[11]{0:T(128)S(1)} %pad_add_fusion.spot, bf16[528,1024]{1,0:T(8,128)(2,1)S(1)} %collective-permute-done.1.refs_3_.refs_0_, bf16[528,1024]{1,0:T(8,128)(2,1)} %collective-permute-done.3.refs_4_.refs_1_, bf16[528,1024]{1,0:T(8,128)(2,1)S(1)} %collective-permute-done.4.refs_2_, ...), custom_call_target="tpu_custom_call" | custom-call | flops 872415232 | bytes 1703936 | tf_op jit(solution)/shard_map/pallas_call | solution.py:201
  98.8 3.2 %collective-permute-start.14 = (bf16[432,512]{1,0:T(8,128)(2,1)S(1)}, bf16[432,512]{1,0:T(8,128)(2,1)S(1)}, u32[]{:S(2)}, u32[]{:S(2)}) collective-permute-start(bf16[432,512]{1,0:T(8,128)(2,1)S(1)} %get-tuple-element.20), channel_id=1, source_target_pairs={{0,1},{1,0},{2,3},{3,2},{4,5},{5,4},{6,7},{7,6},{8,9},{9,8},{10,11... | collective-permute-start | bytes 1327112 | tf_op jit(solution)/shard_map/ppermute | solution.py:370
  104.9 1.6 %collective-permute-start.27 = (bf16[2,2,104,512]{3,2,1,0:T(8,128)(2,1)S(1)}, bf16[2,2,104,512]{3,2,1,0:T(8,128)(2,1)S(1)}, u32[]{:S(2)}, u32[]{:S(2)}) collective-permute-start(bf16[2,2,104,512]{3,2,1,0:T(8,128)(2,1)S(1)} %collective-permute-done.17.refs_3_.refs_1_), channel_id=1, source_target_pairs={{16,0},{0,16},{17,1},{1,17},{18,2},{2,18},{19,3},{3,19},{20,4},{4,... | collective-permute-start | bytes 1277960 | tf_op jit(solution)/shard_map/ppermute | solution.py:363
  106.7 16.2 %collective-permute-done.25.refs_8_.refs_3_ = bf16[2,2,104,512]{3,2,1,0:T(8,128)(2,1)S(1)} collective-permute-done((bf16[2,2,104,512]{3,2,1,0:T(8,128)(2,1)S(1)}, bf16[2,2,104,512]{3,2,1,0:T(8,128)(2,1)S(1)}, u32[]{:S(2)}, u32[]{:S(2)}) %collective-permute-start.25) | collective-permute-done | bytes 426016 | tf_op jit(solution)/shard_map/ppermute | solution.py:360
  129.3 6.4 %collective-permute-done.21.refs_4_ = bf16[104,512]{1,0:T(8,128)(2,1)S(1)} collective-permute-done((bf16[104,512]{1,0:T(8,128)(2,1)S(1)}, bf16[104,512]{1,0:T(8,128)(2,1)S(1)}, u32[]{:S(2)}, u32[]{:S(2)}) %collective-permute-start.21) | collective-permute-done | bytes 106528 | tf_op jit(solution)/shard_map/ppermute | solution.py:379
  137.2 2.4 %collective-permute-done.22.refs_5_ = bf16[104,512]{1,0:T(8,128)(2,1)S(1)} collective-permute-done((bf16[104,512]{1,0:T(8,128)(2,1)S(1)}, bf16[104,512]{1,0:T(8,128)(2,1)S(1)}, u32[]{:S(2)}, u32[]{:S(2)}) %collective-permute-start.22) | collective-permute-done | bytes 106528 | tf_op jit(solution)/shard_map/ppermute | solution.py:382
  139.6 2.3 %collective-permute-done.24.refs_7_ = bf16[104,512]{1,0:T(8,128)(2,1)S(1)} collective-permute-done((bf16[104,512]{1,0:T(8,128)(2,1)S(1)}, bf16[104,512]{1,0:T(8,128)(2,1)S(1)}, u32[]{:S(2)}, u32[]{:S(2)}) %collective-permute-start.24) | collective-permute-done | bytes 106528 | tf_op jit(solution)/shard_map/ppermute | solution.py:382
  143.5 2.6 %shard_map.75.refs_8_ = f32[2,512,512]{2,1,0:T(8,128)} custom-call(bf16[4,2,104,512]{3,2,1,0:T(8,128)(2,1)S(1)} %shard_map.74.side, bf16[2,2,104,512]{3,2,1,0:T(8,128)(2,1)S(1)} %get-tuple-element.18.refs_0_, bf16[2,2,104,512]{3,2,1,0:T(8,128)(2,1)S(1)} %collective-permute-done.17.refs_3_.refs_1_, ...), custom_call_target="tpu_custom_call" | custom-call | flops 17448304640 | bytes 51118080 | tf_op jit(solution)/shard_map/pallas_call | solution.py:273
  146.1 3.9 %shard_map.76 = bf16[512,1024]{1,0:T(8,128)(2,1)} custom-call(bf16[4,2,104,512]{3,2,1,0:T(8,128)(2,1)S(1)} %collective-permute-done.28.side, bf16[2,2,104,512]{3,2,1,0:T(8,128)(2,1)S(1)} %get-tuple-element.18.refs_0_, bf16[2,2,104,512]{3,2,1,0:T(8,128)(2,1)S(1)} %collective-permute-done.17.refs_3_.refs_1_, ...), custom_call_target="tpu_custom_call" | custom-call | flops 17448304640 | bytes 51118080 | tf_op jit(solution)/shard_map/pallas_call | solution.py:273
  (68 shorter events, 30.9 us)
Async XLA Ops:
  2.9 27.9 %collective-permute-start.2 = (bf16[528,1024]{1,0:T(8,128)(2,1)}, bf16[528,1024]{1,0:T(8,128)(2,1)}, u32[]{:S(2)}, u32[]{:S(2)}) collective-permute-start(bf16[528,1024]{1,0:T(8,128)(2,1)} %fusion.3.refs_2_.refs_0_), channel_id=1, source_target_pairs={{4,0},{5,1},{6,2},{7,3},{8,4},{9,5},{10,6},{11,7},{12,8},{13,9},{1... | collective-permute-start | bytes 3244040 | tf_op jit(solution)/shard_map/ppermute | solution.py:303
  4.2 27.9 %collective-permute-start = (bf16[528,1024]{1,0:T(8,128)(2,1)}, bf16[528,1024]{1,0:T(8,128)(2,1)}, u32[]{:S(2)}, u32[]{:S(2)}) collective-permute-start(bf16[528,1024]{1,0:T(8,128)(2,1)} %fusion.3.refs_2_.refs_0_), channel_id=1, source_target_pairs={{0,4},{1,5},{2,6},{3,7},{4,8},{5,9},{6,10},{7,11},{8,12},{9,13},{1... | collective-permute-start | bytes 3244040 | tf_op jit(solution)/shard_map/ppermute | solution.py:303
  13.3 28.8 %collective-permute-start.10 = (bf16[3,2,104,1024]{3,2,1,0:T(8,128)(2,1)S(1)}, bf16[3,2,104,1024]{3,2,1,0:T(8,128)(2,1)S(1)}, u32[]{:S(2)}, u32[]{:S(2)}) collective-permute-start(bf16[3,2,104,1024]{3,2,1,0:T(8,128)(2,1)S(1)} %shard_map.64.refs_2_.refs_1_), channel_id=1, source_target_pairs={{0,2},{1,3},{2,0},{3,1},{4,6},{5,7},{6,4},{7,5},{8,10},{9,11},{10,... | collective-permute-start | bytes 3833864 | tf_op jit(solution)/shard_map/ppermute | solution.py:339
  16.8 20.3 %collective-permute-start.7 = (bf16[2,4,104,512]{3,2,1,0:T(8,128)(2,1)S(1)}, bf16[2,4,104,512]{3,2,1,0:T(8,128)(2,1)S(1)}, u32[]{:S(2)}, u32[]{:S(2)}) collective-permute-start(bf16[2,4,104,512]{3,2,1,0:T(8,128)(2,1)S(1)} %get-tuple-element.17), channel_id=1, source_target_pairs={{0,1},{1,0},{2,3},{3,2},{4,5},{5,4},{6,7},{7,6},{8,9},{9,8},{10,11... | collective-permute-start | bytes 2555912 | tf_op jit(solution)/shard_map/ppermute | solution.py:326
  30.8 26.3 %collective-permute-start.3 = (bf16[528,1024]{1,0:T(8,128)(2,1)}, bf16[528,1024]{1,0:T(8,128)(2,1)}, u32[]{:S(2)}, u32[]{:S(2)}) collective-permute-start(bf16[528,1024]{1,0:T(8,128)(2,1)} %collective-permute-done.2.refs_2_), channel_id=1, source_target_pairs={{4,0},{5,1},{6,2},{7,3},{8,4},{9,5},{10,6},{11,7},{20,16},{21,17},... | collective-permute-start | bytes 3244040 | tf_op jit(solution)/shard_map/ppermute | solution.py:303
  32.1 27.0 %collective-permute-start.1 = (bf16[528,1024]{1,0:T(8,128)(2,1)}, bf16[528,1024]{1,0:T(8,128)(2,1)S(1)}, u32[]{:S(2)}, u32[]{:S(2)}) collective-permute-start(bf16[528,1024]{1,0:T(8,128)(2,1)} %collective-permute-done.refs_1_), channel_id=1, source_target_pairs={{4,8},{5,9},{6,10},{7,11},{8,12},{9,13},{10,14},{11,15},{20,24},{2... | collective-permute-start | bytes 3244040 | tf_op jit(solution)/shard_map/ppermute | solution.py:303
  35.8 28.0 %collective-permute-start.6 = (bf16[4,2,104,1024]{3,2,1,0:T(8,128)(2,1)S(1)}, bf16[4,2,104,1024]{3,2,1,0:T(8,128)(2,1)S(1)}, u32[]{:S(2)}, u32[]{:S(2)}) collective-permute-start(bf16[4,2,104,1024]{3,2,1,0:T(8,128)(2,1)S(1)} %shard_map.65), channel_id=1, source_target_pairs={{0,1},{1,0},{2,3},{3,2},{4,5},{5,4},{6,7},{7,6},{8,9},{9,8},{10,11... | collective-permute-start | bytes 5111816 | tf_op jit(solution)/shard_map/ppermute | solution.py:343
  37.2 25.0 %collective-permute-start.12 = (bf16[2,4,104,512]{3,2,1,0:T(8,128)(2,1)S(1)}, bf16[2,4,104,512]{3,2,1,0:T(8,128)(2,1)S(1)}, u32[]{:S(2)}, u32[]{:S(2)}) collective-permute-start(bf16[2,4,104,512]{3,2,1,0:T(8,128)(2,1)S(1)} %shard_map.67.refs_2_), channel_id=1, source_target_pairs={{0,2},{1,3},{2,0},{3,1},{4,6},{5,7},{6,4},{7,5},{8,10},{9,11},{10,... | collective-permute-start | bytes 2555912 | tf_op jit(solution)/shard_map/ppermute | solution.py:333
  42.1 31.6 %collective-permute-start.11 = (bf16[3,2,104,1024]{3,2,1,0:T(8,128)(2,1)S(1)}, bf16[3,2,104,1024]{3,2,1,0:T(8,128)(2,1)}, u32[]{:S(2)}, u32[]{:S(2)}) collective-permute-start(bf16[3,2,104,1024]{3,2,1,0:T(8,128)(2,1)S(1)} %collective-permute-done.10.refs_8_), channel_id=1, source_target_pairs={{0,16},{16,0},{1,17},{17,1},{2,18},{18,2},{3,19},{19,3},{4,20},{20... | collective-permute-start | bytes 3833864 | tf_op jit(solution)/shard_map/ppermute | solution.py:340
  57.1 27.7 %collective-permute-start.5 = (bf16[528,1024]{1,0:T(8,128)(2,1)}, bf16[528,1024]{1,0:T(8,128)(2,1)}, u32[]{:S(2)}, u32[]{:S(2)}) collective-permute-start(bf16[528,1024]{1,0:T(8,128)(2,1)} %collective-permute-done.3.refs_4_.refs_1_), channel_id=1, source_target_pairs={{4,0},{5,1},{6,2},{7,3},{20,16},{21,17},{22,18},{23,19}} | collective-permute-start | bytes 3244040 | tf_op jit(solution)/shard_map/ppermute | solution.py:303
  59.1 27.8 %collective-permute-start.4 = (bf16[528,1024]{1,0:T(8,128)(2,1)S(1)}, bf16[528,1024]{1,0:T(8,128)(2,1)S(1)}, u32[]{:S(2)}, u32[]{:S(2)}) collective-permute-start(bf16[528,1024]{1,0:T(8,128)(2,1)S(1)} %collective-permute-done.1.refs_3_.refs_0_), channel_id=1, source_target_pairs={{8,12},{9,13},{10,14},{11,15},{24,28},{25,29},{26,30},{27,31}} | collective-permute-start | bytes 3244040 | tf_op jit(solution)/shard_map/ppermute | solution.py:303
  62.2 22.5 %collective-permute-start.8 = (bf16[1,2,104,1024]{3,2,1,0:T(8,128)(2,1)S(1)}, bf16[1,2,104,1024]{3,2,1,0:T(8,128)(2,1)S(1)}, u32[]{:S(2)}, u32[]{:S(2)}) collective-permute-start(bf16[1,2,104,1024]{3,2,1,0:T(8,128)(2,1)S(1)} %shard_map.68), channel_id=1, source_target_pairs={{0,2},{1,3},{2,0},{3,1},{4,6},{5,7},{6,4},{7,5},{8,10},{9,11},{10,... | collective-permute-start | bytes 1277960 | tf_op jit(solution)/shard_map/ppermute | solution.py:339
  63.9 23.1 %collective-permute-start.13 = (bf16[2,2,104,512]{3,2,1,0:T(8,128)(2,1)S(1)}, bf16[2,2,104,512]{3,2,1,0:T(8,128)(2,1)S(1)}, u32[]{:S(2)}, u32[]{:S(2)}) collective-permute-start(bf16[2,2,104,512]{3,2,1,0:T(8,128)(2,1)S(1)} %get-tuple-element.18.refs_0_), channel_id=1, source_target_pairs={{16,0},{0,16},{17,1},{1,17},{18,2},{2,18},{19,3},{3,19},{20,4},{4,... | collective-permute-start | bytes 1277960 | tf_op jit(solution)/shard_map/ppermute | solution.py:363
  73.7 29.7 %collective-permute-start.15 = (bf16[2,2,104,512]{3,2,1,0:T(8,128)(2,1)S(1)}, bf16[2,2,104,512]{3,2,1,0:T(8,128)(2,1)S(1)}, u32[]{:S(2)}, u32[]{:S(2)}) collective-permute-start(bf16[2,2,104,512]{3,2,1,0:T(8,128)(2,1)S(1)} %get-tuple-element.21), channel_id=1, source_target_pairs={{0,8},{1,9},{2,10},{3,11},{4,12},{5,13},{6,14},{7,15},{8,0},{9,1},... | collective-permute-start | bytes 1277960 | tf_op jit(solution)/shard_map/ppermute | solution.py:360
  84.8 20.1 %collective-permute-start.17 = (bf16[2,2,104,512]{3,2,1,0:T(8,128)(2,1)S(1)}, bf16[2,2,104,512]{3,2,1,0:T(8,128)(2,1)S(1)}, u32[]{:S(2)}, u32[]{:S(2)}) collective-permute-start(bf16[2,2,104,512]{3,2,1,0:T(8,128)(2,1)S(1)} %get-tuple-element.25), channel_id=1, source_target_pairs={{0,12},{1,13},{2,14},{3,15},{4,0},{5,1},{6,2},{7,3},{8,4},{9,5},{1... | collective-permute-start | bytes 1277960 | tf_op jit(solution)/shard_map/ppermute | solution.py:360
  84.8 9.2 %collective-permute-start.9 = (bf16[1,2,104,1024]{3,2,1,0:T(8,128)(2,1)S(1)}, bf16[1,2,104,1024]{3,2,1,0:T(8,128)(2,1)S(1)}, u32[]{:S(2)}, u32[]{:S(2)}) collective-permute-start(bf16[1,2,104,1024]{3,2,1,0:T(8,128)(2,1)S(1)} %collective-permute-done.8.refs_7_), channel_id=1, source_target_pairs={{0,16},{16,0},{1,17},{17,1},{2,18},{18,2},{3,19},{19,3},{4,20},{20... | collective-permute-start | bytes 1277960 | tf_op jit(solution)/shard_map/ppermute | solution.py:340
  102.0 20.9 %collective-permute-start.25 = (bf16[2,2,104,512]{3,2,1,0:T(8,128)(2,1)S(1)}, bf16[2,2,104,512]{3,2,1,0:T(8,128)(2,1)S(1)}, u32[]{:S(2)}, u32[]{:S(2)}) collective-permute-start(bf16[2,2,104,512]{3,2,1,0:T(8,128)(2,1)S(1)} %get-tuple-element.26), channel_id=1, source_target_pairs={{0,4},{1,5},{2,6},{3,7},{4,8},{5,9},{6,10},{7,11},{8,12},{9,13},{1... | collective-permute-start | bytes 1277960 | tf_op jit(solution)/shard_map/ppermute | solution.py:360
  103.4 22.2 %collective-permute-start.26 = (bf16[2,2,104,512]{3,2,1,0:T(8,128)(2,1)S(1)}, bf16[2,2,104,512]{3,2,1,0:T(8,128)(2,1)S(1)}, u32[]{:S(2)}, u32[]{:S(2)}) collective-permute-start(bf16[2,2,104,512]{3,2,1,0:T(8,128)(2,1)S(1)} %collective-permute-done.15.refs_3_.refs_2_), channel_id=1, source_target_pairs={{16,0},{0,16},{17,1},{1,17},{18,2},{2,18},{19,3},{3,19},{20,4},{4,... | collective-permute-start | bytes 1277960 | tf_op jit(solution)/shard_map/ppermute | solution.py:363
  104.9 21.0 %collective-permute-start.27 = (bf16[2,2,104,512]{3,2,1,0:T(8,128)(2,1)S(1)}, bf16[2,2,104,512]{3,2,1,0:T(8,128)(2,1)S(1)}, u32[]{:S(2)}, u32[]{:S(2)}) collective-permute-start(bf16[2,2,104,512]{3,2,1,0:T(8,128)(2,1)S(1)} %collective-permute-done.17.refs_3_.refs_1_), channel_id=1, source_target_pairs={{16,0},{0,16},{17,1},{1,17},{18,2},{2,18},{19,3},{3,19},{20,4},{4,... | collective-permute-start | bytes 1277960 | tf_op jit(solution)/shard_map/ppermute | solution.py:363
  106.6 17.5 %collective-permute-start.16 = (bf16[224,512]{1,0:T(8,128)(2,1)S(1)}, bf16[224,512]{1,0:T(8,128)(2,1)S(1)}, u32[]{:S(2)}, u32[]{:S(2)}) collective-permute-start(bf16[224,512]{1,0:T(8,128)(2,1)S(1)} %get-tuple-element.24), channel_id=1, source_target_pairs={{0,2},{1,3},{2,0},{3,1},{4,6},{5,7},{6,4},{7,5},{8,10},{9,11},{10,... | collective-permute-start | bytes 688136 | tf_op jit(solution)/shard_map/ppermute | solution.py:375
  122.9 20.6 %collective-permute-start.29 = (bf16[2,2,104,512]{3,2,1,0:T(8,128)(2,1)S(1)}, bf16[2,2,104,512]{3,2,1,0:T(8,128)(2,1)S(1)}, u32[]{:S(2)}, u32[]{:S(2)}) collective-permute-start(bf16[2,2,104,512]{3,2,1,0:T(8,128)(2,1)S(1)} %collective-permute-done.25.refs_8_.refs_3_), channel_id=1, source_target_pairs={{16,0},{0,16},{17,1},{1,17},{18,2},{2,18},{19,3},{3,19},{20,4},{4,... | collective-permute-start | bytes 1277960 | tf_op jit(solution)/shard_map/ppermute | solution.py:363
  125.5 10.2 %collective-permute-start.21 = (bf16[104,512]{1,0:T(8,128)(2,1)S(1)}, bf16[104,512]{1,0:T(8,128)(2,1)S(1)}, u32[]{:S(2)}, u32[]{:S(2)}) collective-permute-start(bf16[104,512]{1,0:T(8,128)(2,1)S(1)} %shard_map.73.refs_0_), channel_id=1, source_target_pairs={{0,8},{1,9},{2,10},{3,11},{4,12},{5,13},{6,14},{7,15},{8,0},{9,1},... | collective-permute-start | bytes 319496 | tf_op jit(solution)/shard_map/ppermute | solution.py:379
  125.5 11.4 %collective-permute-start.23 = (bf16[104,512]{1,0:T(8,128)(2,1)S(1)}, bf16[104,512]{1,0:T(8,128)(2,1)S(1)}, u32[]{:S(2)}, u32[]{:S(2)}) collective-permute-start(bf16[104,512]{1,0:T(8,128)(2,1)S(1)} %shard_map.73.refs_0_), channel_id=1, source_target_pairs={{0,4},{1,5},{2,6},{3,7},{4,8},{5,9},{6,10},{7,11},{8,12},{9,13},{1... | collective-permute-start | bytes 319496 | tf_op jit(solution)/shard_map/ppermute | solution.py:379
  125.9 11.3 %collective-permute-start.18 = (bf16[104,512]{1,0:T(8,128)(2,1)S(1)}, bf16[104,512]{1,0:T(8,128)(2,1)S(1)}, u32[]{:S(2)}, u32[]{:S(2)}) collective-permute-start(bf16[104,512]{1,0:T(8,128)(2,1)S(1)} %shard_map.73.refs_0_), channel_id=1, source_target_pairs={{0,2},{1,3},{2,0},{3,1},{4,6},{5,7},{6,4},{7,5},{8,10},{9,11},{10,... | collective-permute-start | bytes 319496 | tf_op jit(solution)/shard_map/ppermute | solution.py:382
  (9 other events, 77.2 us)

commit v6 on v5

--- a/solution.py
+++ b/solution.py
@@ -36,7 +36,7 @@
         in_specs=[VMEM] * len(operands) + [ANY] * len(after),
         out_specs=[VMEM] * len(outs),
         compiler_params=PARAMS,
-        cost_estimate=cost(4 * sum(o.size for o in outs), 0, 1),
+        cost_estimate=cost(4 * sum(o.size for o in outs), 0, 20),
     )(*operands, *after)
 
 
@@ -63,7 +63,7 @@
         in_specs=[VMEM] * len(operands) + [ANY] * len(after),
         out_specs=[VMEM] * len(outs),
         compiler_params=PARAMS,
-        cost_estimate=cost(4 * sum(o.size for o in outs), 0, 1),
+        cost_estimate=cost(4 * sum(o.size for o in outs), 0, 2),
     )(*operands, *after)
 
 
@@ -212,7 +212,7 @@
             ),
             out_shape=outs,
             compiler_params=PARAMS,
-            cost_estimate=cost(16 * hid * width * count, 16 * hid * rows * width * count, 1),
+            cost_estimate=cost(16 * hid * width * count, 16 * hid * rows * width * count, 5 if last else 1),
         )(spot, *[blocks[m] for m in arrays], *own, near, *far, *given, *after)
 
     def cut(spot, gate_t, up_t, width, ds, first, count, after=()):
@@ -241,7 +241,7 @@
             ),
             out_shape=[shape(count, 2, hid, width)] * len(ds),
             compiler_params=PARAMS,
-            cost_estimate=cost(8 * len(ds) * count * hid * width, 0, 1),
+            cost_estimate=cost(8 * len(ds) * count * hid * width, 0, 5),
         )(spot, *[gate_t, up_t] * len(ds), *after)
 
     def mix(side, pieces, share, dc, total=None):
@@ -340,7 +340,7 @@
                 far.append((brought, lax.ppermute(brought, "groups", [(i, i ^ 1) for i in range(groups)])))
             else:
                 far.append(tuple(lax.ppermute(w, "gx", flip(d)) for d, w in zip((2, 3), sends)))
-        near = lax.ppermute(cut(spot, *own, width, (1,), 0, planes, after=first_sends)[0], "gx", flip(1))
+        near = lax.ppermute(cut(spot, *own, width, (1,), 0, planes, after=(send,))[0], "gx", flip(1))
 
 
         def third_moves(ks, given, outs):
@@ -354,9 +354,9 @@
             return moves
 
         ready = move(
-            functools.partial(third_moves, range(planes)), [shape(2, 2, hid, part)] * planes, keep, came, across, after=blocks[-4:-2]
+            functools.partial(third_moves, range(planes)), [shape(2, 2, hid, part)] * planes, keep, came, across, after=()
         )
-        sums = product(spot, rows, blocks, own, near, far[0], cuts[0], after=(across,))
+        sums = product(spot, rows, blocks, own, near, far[0], cuts[0], after=(ready[0],))
         held = [lax.ppermute(h, "gx", shift(-k)) if k else h for k, h in enumerate(ready)]
         pieces = list(held)
         for r in range(1, share):
@@ -365,7 +365,7 @@
         crossed = pieces[planes:] if share > 1 else held
         one, two, three = held[1], held[2 % planes], held[-1]
         x0, x1, x2, x3 = crossed[0], crossed[1], crossed[2 % planes], crossed[-1]
-        later = [(two,), (one,), (three, x2, x1)]
+        later = [(), (), (three, x2, x1)]
         keep, send = product(spot, rows, blocks, own, near, far[1], cuts[1], sums, total, after=(x0,))
         came = lax.ppermute(send, "gx", flip(1))
         mine, total, send = stage(

time: 151 us -> 146 us (0.967)
  starting transfers between devices: 45.3 us -> 42 us
    ppermute x3, waiting for transfers between devices: 16.6 us -> 7.71 us  [body(): lax.ppermute(h, 'gx', shift(-k))]
    ppermute x3, waiting for transfers between devices: 7.34 us -> 2.22 us  [body(): column[k] = lax.ppermute(hidden, 'gx', shift(-k))]
    ppermute x2, waiting for transfers between devices: 3.39 us -> 8.01 us  [body(): brought = lax.ppermute(sends[0], ('groups', 'gx'), far_flip())]
    ppermute x1, waiting for transfers between devices: 0.01 us -> 4.25 us  [body(): across = lax.ppermute(send, 'gx', flip(2))]
    ppermute x4, waiting for transfers between devices: 0.01 us -> 4.24 us  [body(): pieces += [lax.ppermute(h, 'groups', swap(r)) for h in held]]
    ppermute x6, waiting for transfers between devices: 23.4 us -> 21.1 us  [body(): lax.ppermute(blocks[0] if s == 1 else blocks[-2], 'gx', line(s, way))]
    ppermute x3, starting transfers between devices: 4.31 us -> 2.53 us  [body(): lax.ppermute(h, 'gx', shift(-k))]
  transfers between devices with their start and end apart: 30 -> 30, of which waited for: 11 -> 12; matrix products, arithmetic and copies ran while one was open for 2% -> 2% of each run, Pallas kernels for 17% -> 17%
where the time goes in v6:
time: 146 us; the launch traced here: 145 us
  waiting for transfers between devices  67.8 us (46%)
  starting transfers between devices  42 us (29%)
  Pallas kernels  29 us (20%)
  other arithmetic  5.14 us (4%)
    ppermute x6, waiting for transfers between devices, body(): lax.ppermute(blocks[0] if s == 1 else blocks[-2], 'gx', line(s, way))  21.1 us
    ppermute x2, waiting for transfers between devices, body(): lax.ppermute(brought, 'groups', [(i, i ^ 1) for i in range(groups)])  14.7 us
    pallas_call x2, Pallas kernels, product(): pl.pallas_call(kernel, grid_spec=pltpu.PrefetchScalarGridSpec(num_scalar_...  13 us
    ppermute x6, starting transfers between devices, body(): lax.ppermute(blocks[0] if s == 1 else blocks[-2], 'gx', line(s, way))  11 us
    ppermute x2, waiting for transfers between devices, body(): brought = lax.ppermute(sends[0], ('groups', 'gx'), far_flip())  8.01 us
    ppermute x3, waiting for transfers between devices, body(): lax.ppermute(h, 'gx', shift(-k))  7.71 us
    ppermute x4, starting transfers between devices, body(): pieces += [lax.ppermute(h, 'groups', swap(r)) for h in held]  6.99 us
    pallas_call x3, Pallas kernels, cut(): pl.pallas_call(kernel, grid_spec=pltpu.PrefetchScalarGridSpec(num_scalar_...  6.91 us
  transfers between devices with their start and end apart: 30, of which 12 were waited for; matrix products, arithmetic and copies ran while one was open for 2% of the time, Pallas kernels for 17%

profile of v6, /device:TPU:1, one launch (start us, length us, event | category | flops | bytes accessed | tf_op | source)
XLA Modules:
  0.0 144.8 jit_solution(10752720722887878538)
XLA Ops:
  4.1 5.7 %collective-permute-start = (bf16[528,1024]{1,0:T(8,128)(2,1)}, bf16[528,1024]{1,0:T(8,128)(2,1)}, u32[]{:S(2)}, u32[]{:S(2)}) collective-permute-start(bf16[528,1024]{1,0:T(8,128)(2,1)} %fusion.3.refs_2_.refs_0_), channel_id=1, source_target_pairs={{0,4},{1,5},{2,6},{3,7},{4,8},{5,9},{6,10},{7,11},{8,12},{9,13},{1... | collective-permute-start | bytes 3244040 | tf_op jit(solution)/shard_map/ppermute | solution.py:303
  10.6 2.6 %shard_map.64.refs_1_ = bf16[3,2,104,1024]{3,2,1,0:T(8,128)(2,1)S(1)} custom-call(s32[11]{0:T(128)S(1)} %pad_add_fusion.spot, bf16[104,16384]{1,0:T(8,128)(2,1)S(1)} %bitcast.11, bf16[104,16384]{1,0:T(8,128)(2,1)} %bitcast.13, bf16[528,1024]{1,0:T(8,128)(2,1)} %fusion.3.refs_2_.refs_0_), custom_call_target="tpu_custom_call" | custom-call | bytes 12779520 | tf_op jit(solution)/shard_map/pallas_call | solution.py:234
  13.2 2.1 %shard_map.65 = (bf16[2,4,104,512]{3,2,1,0:T(8,128)(2,1)S(1)}, bf16[2,4,104,512]{3,2,1,0:T(8,128)(2,1)S(1)}) custom-call(bf16[104,16384]{1,0:T(8,128)(2,1)} %refs_0_.1, bf16[3,2,104,1024]{3,2,1,0:T(8,128)(2,1)S(1)} %shard_map.64.refs_1_), custom_call_target="tpu_custom_call" | custom-call | bytes 68157440 | tf_op jit(solution)/shard_map/pallas_call | solution.py:33
  18.1 12.7 %collective-permute-done.2.refs_2_ = bf16[528,1024]{1,0:T(8,128)(2,1)} collective-permute-done((bf16[528,1024]{1,0:T(8,128)(2,1)}, bf16[528,1024]{1,0:T(8,128)(2,1)}, u32[]{:S(2)}, u32[]{:S(2)}) %collective-permute-start.2) | collective-permute-done | bytes 1081376 | tf_op jit(solution)/shard_map/ppermute | solution.py:303
  32.9 2.7 %shard_map.67 = bf16[4,2,104,1024]{3,2,1,0:T(8,128)(2,1)S(1)} custom-call(s32[11]{0:T(128)S(1)} %pad_add_fusion.spot, bf16[104,16384]{1,0:T(8,128)(2,1)S(1)} %bitcast.12, bf16[104,16384]{1,0:T(8,128)(2,1)} %bitcast.14, bf16[2,4,104,512]{3,2,1,0:T(8,128)(2,1)S(1)} %shard_map.66.refs_2_), custom_call_target="tpu_custom_call" | custom-call | bytes 17039360 | tf_op jit(solution)/shard_map/pallas_call | solution.py:234
  38.3 8.0 %collective-permute-done.10.refs_8_ = bf16[3,2,104,1024]{3,2,1,0:T(8,128)(2,1)S(1)} collective-permute-done((bf16[3,2,104,1024]{3,2,1,0:T(8,128)(2,1)S(1)}, bf16[3,2,104,1024]{3,2,1,0:T(8,128)(2,1)S(1)}, u32[]{:S(2)}, u32[]{:S(2)}) %collective-permute-start.10) | collective-permute-done | bytes 1277984 | tf_op jit(solution)/shard_map/ppermute | solution.py:339
  46.3 2.3 %collective-permute-start.11 = (bf16[3,2,104,1024]{3,2,1,0:T(8,128)(2,1)S(1)}, bf16[3,2,104,1024]{3,2,1,0:T(8,128)(2,1)S(1)}, u32[]{:S(2)}, u32[]{:S(2)}) collective-permute-start(bf16[3,2,104,1024]{3,2,1,0:T(8,128)(2,1)S(1)} %collective-permute-done.10.refs_8_), channel_id=1, source_target_pairs={{0,16},{16,0},{1,17},{17,1},{2,18},{18,2},{3,19},{19,3},{4,20},{20... | collective-permute-start | bytes 3833864 | tf_op jit(solution)/shard_map/ppermute | solution.py:340
  48.6 8.3 %collective-permute-done.3.refs_4_.refs_1_ = bf16[528,1024]{1,0:T(8,128)(2,1)S(1)} collective-permute-done((bf16[528,1024]{1,0:T(8,128)(2,1)}, bf16[528,1024]{1,0:T(8,128)(2,1)S(1)}, u32[]{:S(2)}, u32[]{:S(2)}) %collective-permute-start.3) | collective-permute-done | bytes 1081376 | tf_op jit(solution)/shard_map/ppermute | solution.py:303
  60.5 4.2 %collective-permute-done.12.refs_2_ = bf16[2,4,104,512]{3,2,1,0:T(8,128)(2,1)S(1)} collective-permute-done((bf16[2,4,104,512]{3,2,1,0:T(8,128)(2,1)S(1)}, bf16[2,4,104,512]{3,2,1,0:T(8,128)(2,1)S(1)}, u32[]{:S(2)}, u32[]{:S(2)}) %collective-permute-start.12) | collective-permute-done | bytes 852000 | tf_op jit(solution)/shard_map/ppermute | solution.py:333
  69.8 7.0 %collective-permute-done.11.refs_9_ = bf16[3,2,104,1024]{3,2,1,0:T(8,128)(2,1)S(1)} collective-permute-done((bf16[3,2,104,1024]{3,2,1,0:T(8,128)(2,1)S(1)}, bf16[3,2,104,1024]{3,2,1,0:T(8,128)(2,1)S(1)}, u32[]{:S(2)}, u32[]{:S(2)}) %collective-permute-start.11) | collective-permute-done | bytes 1277984 | tf_op jit(solution)/shard_map/ppermute | solution.py:340
  76.8 2.1 %collective-permute-start.24 = (bf16[2,2,104,512]{3,2,1,0:T(8,128)(2,1)S(1)}, bf16[2,2,104,512]{3,2,1,0:T(8,128)(2,1)S(1)}, u32[]{:S(2)}, u32[]{:S(2)}) collective-permute-start(bf16[2,2,104,512]{3,2,1,0:T(8,128)(2,1)S(1)} %get-tuple-element.25), channel_id=1, source_target_pairs={{0,8},{1,9},{2,10},{3,11},{4,12},{5,13},{6,14},{7,15},{8,0},{9,1},... | collective-permute-start | bytes 1277960 | tf_op jit(solution)/shard_map/ppermute | solution.py:360
  78.9 8.2 %shard_map.70.refs_9_ = f32[832,512]{1,0:T(8,128)} custom-call(s32[11]{0:T(128)S(1)} %pad_add_fusion.spot, bf16[528,1024]{1,0:T(8,128)(2,1)} %fusion.3.refs_2_.refs_0_, bf16[528,1024]{1,0:T(8,128)(2,1)} %collective-permute-done.refs_1_, bf16[528,1024]{1,0:T(8,128)(2,1)} %collective-permute-done.2.refs_2_, ...), custom_call_target="tpu_custom_call" | custom-call | flops 2617245696 | bytes 5111808 | tf_op jit(solution)/shard_map/pallas_call | solution.py:201
  87.2 2.3 %collective-permute-start.9 = (bf16[1,2,104,1024]{3,2,1,0:T(8,128)(2,1)S(1)}, bf16[1,2,104,1024]{3,2,1,0:T(8,128)(2,1)S(1)}, u32[]{:S(2)}, u32[]{:S(2)}) collective-permute-start(bf16[1,2,104,1024]{3,2,1,0:T(8,128)(2,1)S(1)} %collective-permute-done.8.refs_7_), channel_id=1, source_target_pairs={{0,16},{16,0},{1,17},{17,1},{2,18},{18,2},{3,19},{19,3},{4,20},{20... | collective-permute-start | bytes 1277960 | tf_op jit(solution)/shard_map/ppermute | solution.py:340
  90.2 7.7 %collective-permute-done.9.refs_8_ = bf16[1,2,104,1024]{3,2,1,0:T(8,128)(2,1)S(1)} collective-permute-done((bf16[1,2,104,1024]{3,2,1,0:T(8,128)(2,1)S(1)}, bf16[1,2,104,1024]{3,2,1,0:T(8,128)(2,1)S(1)}, u32[]{:S(2)}, u32[]{:S(2)}) %collective-permute-start.9) | collective-permute-done | bytes 426016 | tf_op jit(solution)/shard_map/ppermute | solution.py:340
  97.9 4.8 %shard_map.71 = (f32[416,512]{1,0:T(8,128)S(1)}, bf16[432,512]{1,0:T(8,128)(2,1)S(1)}) custom-call(s32[11]{0:T(128)S(1)} %pad_add_fusion.spot, bf16[528,1024]{1,0:T(8,128)(2,1)S(1)} %collective-permute-done.1.refs_3_.refs_0_, bf16[528,1024]{1,0:T(8,128)(2,1)S(1)} %collective-permute-done.3.refs_4_.refs_1_, ...), custom_call_target="tpu_custom_call" | custom-call | flops 4362076160 | bytes 8519680 | tf_op jit(solution)/shard_map/pallas_call | solution.py:201
  102.7 2.4 %collective-permute-start.14 = (bf16[432,512]{1,0:T(8,128)(2,1)S(1)}, bf16[432,512]{1,0:T(8,128)(2,1)S(1)}, u32[]{:S(2)}, u32[]{:S(2)}) collective-permute-start(bf16[432,512]{1,0:T(8,128)(2,1)S(1)} %get-tuple-element.20), channel_id=1, source_target_pairs={{0,1},{1,0},{2,3},{3,2},{4,5},{5,4},{6,7},{7,6},{8,9},{9,8},{10,11... | collective-permute-start | bytes 1327112 | tf_op jit(solution)/shard_map/ppermute | solution.py:370
  107.4 2.2 %collective-permute-start.27 = (bf16[2,2,104,512]{3,2,1,0:T(8,128)(2,1)S(1)}, bf16[2,2,104,512]{3,2,1,0:T(8,128)(2,1)S(1)}, u32[]{:S(2)}, u32[]{:S(2)}) collective-permute-start(bf16[2,2,104,512]{3,2,1,0:T(8,128)(2,1)S(1)} %collective-permute-done.26.refs_1_), channel_id=1, source_target_pairs={{16,0},{0,16},{17,1},{1,17},{18,2},{2,18},{19,3},{3,19},{20,4},{4,... | collective-permute-start | bytes 1277960 | tf_op jit(solution)/shard_map/ppermute | solution.py:363
  111.1 7.1 %collective-permute-done.23.refs_8_.refs_3_ = bf16[2,2,104,512]{3,2,1,0:T(8,128)(2,1)S(1)} collective-permute-done((bf16[2,2,104,512]{3,2,1,0:T(8,128)(2,1)S(1)}, bf16[2,2,104,512]{3,2,1,0:T(8,128)(2,1)S(1)}, u32[]{:S(2)}, u32[]{:S(2)}) %collective-permute-start.23) | collective-permute-done | bytes 426016 | tf_op jit(solution)/shard_map/ppermute | solution.py:360
  121.3 4.2 %collective-permute-done.27.refs_10_.refs_5_ = bf16[2,2,104,512]{3,2,1,0:T(8,128)(2,1)S(1)} collective-permute-done((bf16[2,2,104,512]{3,2,1,0:T(8,128)(2,1)S(1)}, bf16[2,2,104,512]{3,2,1,0:T(8,128)(2,1)S(1)}, u32[]{:S(2)}, u32[]{:S(2)}) %collective-permute-start.27) | collective-permute-done | bytes 426016 | tf_op jit(solution)/shard_map/ppermute | solution.py:363
  127.1 2.2 %collective-permute-done.19.refs_4_ = bf16[104,512]{1,0:T(8,128)(2,1)S(1)} collective-permute-done((bf16[104,512]{1,0:T(8,128)(2,1)S(1)}, bf16[104,512]{1,0:T(8,128)(2,1)S(1)}, u32[]{:S(2)}, u32[]{:S(2)}) %collective-permute-start.19) | collective-permute-done | bytes 106528 | tf_op jit(solution)/shard_map/ppermute | solution.py:379
  130.8 3.2 %collective-permute-done.20.refs_5_ = bf16[104,512]{1,0:T(8,128)(2,1)S(1)} collective-permute-done((bf16[104,512]{1,0:T(8,128)(2,1)S(1)}, bf16[104,512]{1,0:T(8,128)(2,1)S(1)}, u32[]{:S(2)}, u32[]{:S(2)}) %collective-permute-start.20) | collective-permute-done | bytes 106528 | tf_op jit(solution)/shard_map/ppermute | solution.py:382
  134.0 2.3 %collective-permute-done.22.refs_7_ = bf16[104,512]{1,0:T(8,128)(2,1)S(1)} collective-permute-done((bf16[104,512]{1,0:T(8,128)(2,1)S(1)}, bf16[104,512]{1,0:T(8,128)(2,1)S(1)}, u32[]{:S(2)}, u32[]{:S(2)}) %collective-permute-start.22) | collective-permute-done | bytes 106528 | tf_op jit(solution)/shard_map/ppermute | solution.py:382
  138.2 2.7 %shard_map.75.refs_8_ = f32[2,512,512]{2,1,0:T(8,128)} custom-call(bf16[4,2,104,512]{3,2,1,0:T(8,128)(2,1)S(1)} %shard_map.74.side, bf16[2,2,104,512]{3,2,1,0:T(8,128)(2,1)S(1)} %get-tuple-element.18.refs_10_.refs_0_, bf16[2,2,104,512]{3,2,1,0:T(8,128)(2,1)S(1)} %collective-permute-done.26.refs_1_, ...), custom_call_target="tpu_custom_call" | custom-call | flops 17448304640 | bytes 51118080 | tf_op jit(solution)/shard_map/pallas_call | solution.py:273
  140.9 3.9 %shard_map.76 = bf16[512,1024]{1,0:T(8,128)(2,1)} custom-call(bf16[4,2,104,512]{3,2,1,0:T(8,128)(2,1)S(1)} %collective-permute-done.28.side, bf16[2,2,104,512]{3,2,1,0:T(8,128)(2,1)S(1)} %get-tuple-element.18.refs_10_.refs_0_, bf16[2,2,104,512]{3,2,1,0:T(8,128)(2,1)S(1)} %collective-permute-done.26.refs_1_, ...), custom_call_target="tpu_custom_call" | custom-call | flops 17448304640 | bytes 51118080 | tf_op jit(solution)/shard_map/pallas_call | solution.py:273
  (70 shorter events, 33.5 us)
Async XLA Ops:
  2.9 27.9 %collective-permute-start.2 = (bf16[528,1024]{1,0:T(8,128)(2,1)}, bf16[528,1024]{1,0:T(8,128)(2,1)}, u32[]{:S(2)}, u32[]{:S(2)}) collective-permute-start(bf16[528,1024]{1,0:T(8,128)(2,1)} %fusion.3.refs_2_.refs_0_), channel_id=1, source_target_pairs={{4,0},{5,1},{6,2},{7,3},{8,4},{9,5},{10,6},{11,7},{12,8},{13,9},{1... | collective-permute-start | bytes 3244040 | tf_op jit(solution)/shard_map/ppermute | solution.py:303
  4.1 27.9 %collective-permute-start = (bf16[528,1024]{1,0:T(8,128)(2,1)}, bf16[528,1024]{1,0:T(8,128)(2,1)}, u32[]{:S(2)}, u32[]{:S(2)}) collective-permute-start(bf16[528,1024]{1,0:T(8,128)(2,1)} %fusion.3.refs_2_.refs_0_), channel_id=1, source_target_pairs={{0,4},{1,5},{2,6},{3,7},{4,8},{5,9},{6,10},{7,11},{8,12},{9,13},{1... | collective-permute-start | bytes 3244040 | tf_op jit(solution)/shard_map/ppermute | solution.py:303
  15.3 17.5 %collective-permute-start.6 = (bf16[2,4,104,512]{3,2,1,0:T(8,128)(2,1)S(1)}, bf16[2,4,104,512]{3,2,1,0:T(8,128)(2,1)S(1)}, u32[]{:S(2)}, u32[]{:S(2)}) collective-permute-start(bf16[2,4,104,512]{3,2,1,0:T(8,128)(2,1)S(1)} %get-tuple-element.17), channel_id=1, source_target_pairs={{0,1},{1,0},{2,3},{3,2},{4,5},{5,4},{6,7},{7,6},{8,9},{9,8},{10,11... | collective-permute-start | bytes 2555912 | tf_op jit(solution)/shard_map/ppermute | solution.py:326
  16.4 30.0 %collective-permute-start.10 = (bf16[3,2,104,1024]{3,2,1,0:T(8,128)(2,1)S(1)}, bf16[3,2,104,1024]{3,2,1,0:T(8,128)(2,1)S(1)}, u32[]{:S(2)}, u32[]{:S(2)}) collective-permute-start(bf16[3,2,104,1024]{3,2,1,0:T(8,128)(2,1)S(1)} %shard_map.64.refs_1_), channel_id=1, source_target_pairs={{0,2},{1,3},{2,0},{3,1},{4,6},{5,7},{6,4},{7,5},{8,10},{9,11},{10,... | collective-permute-start | bytes 3833864 | tf_op jit(solution)/shard_map/ppermute | solution.py:339
  30.8 26.2 %collective-permute-start.3 = (bf16[528,1024]{1,0:T(8,128)(2,1)}, bf16[528,1024]{1,0:T(8,128)(2,1)S(1)}, u32[]{:S(2)}, u32[]{:S(2)}) collective-permute-start(bf16[528,1024]{1,0:T(8,128)(2,1)} %collective-permute-done.2.refs_2_), channel_id=1, source_target_pairs={{4,0},{5,1},{6,2},{7,3},{8,4},{9,5},{10,6},{11,7},{20,16},{21,17},... | collective-permute-start | bytes 3244040 | tf_op jit(solution)/shard_map/ppermute | solution.py:303
  32.1 26.9 %collective-permute-start.1 = (bf16[528,1024]{1,0:T(8,128)(2,1)}, bf16[528,1024]{1,0:T(8,128)(2,1)S(1)}, u32[]{:S(2)}, u32[]{:S(2)}) collective-permute-start(bf16[528,1024]{1,0:T(8,128)(2,1)} %collective-permute-done.refs_1_), channel_id=1, source_target_pairs={{4,8},{5,9},{6,10},{7,11},{8,12},{9,13},{10,14},{11,15},{20,24},{2... | collective-permute-start | bytes 3244040 | tf_op jit(solution)/shard_map/ppermute | solution.py:303
  35.6 32.3 %collective-permute-start.7 = (bf16[4,2,104,1024]{3,2,1,0:T(8,128)(2,1)S(1)}, bf16[4,2,104,1024]{3,2,1,0:T(8,128)(2,1)S(1)}, u32[]{:S(2)}, u32[]{:S(2)}) collective-permute-start(bf16[4,2,104,1024]{3,2,1,0:T(8,128)(2,1)S(1)} %shard_map.67), channel_id=1, source_target_pairs={{0,1},{1,0},{2,3},{3,2},{4,5},{5,4},{6,7},{7,6},{8,9},{9,8},{10,11... | collective-permute-start | bytes 5111816 | tf_op jit(solution)/shard_map/ppermute | solution.py:343
  36.9 27.8 %collective-permute-start.12 = (bf16[2,4,104,512]{3,2,1,0:T(8,128)(2,1)S(1)}, bf16[2,4,104,512]{3,2,1,0:T(8,128)(2,1)S(1)}, u32[]{:S(2)}, u32[]{:S(2)}) collective-permute-start(bf16[2,4,104,512]{3,2,1,0:T(8,128)(2,1)S(1)} %shard_map.66.refs_2_), channel_id=1, source_target_pairs={{0,2},{1,3},{2,0},{3,1},{4,6},{5,7},{6,4},{7,5},{8,10},{9,11},{10,... | collective-permute-start | bytes 2555912 | tf_op jit(solution)/shard_map/ppermute | solution.py:333
  46.3 30.4 %collective-permute-start.11 = (bf16[3,2,104,1024]{3,2,1,0:T(8,128)(2,1)S(1)}, bf16[3,2,104,1024]{3,2,1,0:T(8,128)(2,1)S(1)}, u32[]{:S(2)}, u32[]{:S(2)}) collective-permute-start(bf16[3,2,104,1024]{3,2,1,0:T(8,128)(2,1)S(1)} %collective-permute-done.10.refs_8_), channel_id=1, source_target_pairs={{0,16},{16,0},{1,17},{17,1},{2,18},{18,2},{3,19},{19,3},{4,20},{20... | collective-permute-start | bytes 3833864 | tf_op jit(solution)/shard_map/ppermute | solution.py:340
  57.0 30.2 %collective-permute-start.5 = (bf16[528,1024]{1,0:T(8,128)(2,1)S(1)}, bf16[528,1024]{1,0:T(8,128)(2,1)}, u32[]{:S(2)}, u32[]{:S(2)}) collective-permute-start(bf16[528,1024]{1,0:T(8,128)(2,1)S(1)} %collective-permute-done.3.refs_4_.refs_1_), channel_id=1, source_target_pairs={{4,0},{5,1},{6,2},{7,3},{20,16},{21,17},{22,18},{23,19}} | collective-permute-start | bytes 3244040 | tf_op jit(solution)/shard_map/ppermute | solution.py:303
  59.0 31.1 %collective-permute-start.4 = (bf16[528,1024]{1,0:T(8,128)(2,1)S(1)}, bf16[528,1024]{1,0:T(8,128)(2,1)S(1)}, u32[]{:S(2)}, u32[]{:S(2)}) collective-permute-start(bf16[528,1024]{1,0:T(8,128)(2,1)S(1)} %collective-permute-done.1.refs_3_.refs_0_), channel_id=1, source_target_pairs={{8,12},{9,13},{10,14},{11,15},{24,28},{25,29},{26,30},{27,31}} | collective-permute-start | bytes 3244040 | tf_op jit(solution)/shard_map/ppermute | solution.py:303
  66.4 20.6 %collective-permute-start.8 = (bf16[1,2,104,1024]{3,2,1,0:T(8,128)(2,1)S(1)}, bf16[1,2,104,1024]{3,2,1,0:T(8,128)(2,1)S(1)}, u32[]{:S(2)}, u32[]{:S(2)}) collective-permute-start(bf16[1,2,104,1024]{3,2,1,0:T(8,128)(2,1)S(1)} %shard_map.68), channel_id=1, source_target_pairs={{0,2},{1,3},{2,0},{3,1},{4,6},{5,7},{6,4},{7,5},{8,10},{9,11},{10,... | collective-permute-start | bytes 1277960 | tf_op jit(solution)/shard_map/ppermute | solution.py:339
  67.9 22.3 %collective-permute-start.13 = (bf16[2,2,104,512]{3,2,1,0:T(8,128)(2,1)S(1)}, bf16[2,2,104,512]{3,2,1,0:T(8,128)(2,1)S(1)}, u32[]{:S(2)}, u32[]{:S(2)}) collective-permute-start(bf16[2,2,104,512]{3,2,1,0:T(8,128)(2,1)S(1)} %get-tuple-element.18.refs_10_.refs_0_), channel_id=1, source_target_pairs={{16,0},{0,16},{17,1},{1,17},{18,2},{2,18},{19,3},{3,19},{20,4},{4,... | collective-permute-start | bytes 1277960 | tf_op jit(solution)/shard_map/ppermute | solution.py:363
  76.8 28.6 %collective-permute-start.24 = (bf16[2,2,104,512]{3,2,1,0:T(8,128)(2,1)S(1)}, bf16[2,2,104,512]{3,2,1,0:T(8,128)(2,1)S(1)}, u32[]{:S(2)}, u32[]{:S(2)}) collective-permute-start(bf16[2,2,104,512]{3,2,1,0:T(8,128)(2,1)S(1)} %get-tuple-element.25), channel_id=1, source_target_pairs={{0,8},{1,9},{2,10},{3,11},{4,12},{5,13},{6,14},{7,15},{8,0},{9,1},... | collective-permute-start | bytes 1277960 | tf_op jit(solution)/shard_map/ppermute | solution.py:360
  87.1 20.3 %collective-permute-start.26 = (bf16[2,2,104,512]{3,2,1,0:T(8,128)(2,1)S(1)}, bf16[2,2,104,512]{3,2,1,0:T(8,128)(2,1)S(1)}, u32[]{:S(2)}, u32[]{:S(2)}) collective-permute-start(bf16[2,2,104,512]{3,2,1,0:T(8,128)(2,1)S(1)} %get-tuple-element.26), channel_id=1, source_target_pairs={{0,12},{1,13},{2,14},{3,15},{4,0},{5,1},{6,2},{7,3},{8,4},{9,5},{1... | collective-permute-start | bytes 1277960 | tf_op jit(solution)/shard_map/ppermute | solution.py:360
  87.2 10.7 %collective-permute-start.9 = (bf16[1,2,104,1024]{3,2,1,0:T(8,128)(2,1)S(1)}, bf16[1,2,104,1024]{3,2,1,0:T(8,128)(2,1)S(1)}, u32[]{:S(2)}, u32[]{:S(2)}) collective-permute-start(bf16[1,2,104,1024]{3,2,1,0:T(8,128)(2,1)S(1)} %collective-permute-done.8.refs_7_), channel_id=1, source_target_pairs={{0,16},{16,0},{1,17},{17,1},{2,18},{18,2},{3,19},{19,3},{4,20},{20... | collective-permute-start | bytes 1277960 | tf_op jit(solution)/shard_map/ppermute | solution.py:340
  105.1 13.2 %collective-permute-start.23 = (bf16[2,2,104,512]{3,2,1,0:T(8,128)(2,1)S(1)}, bf16[2,2,104,512]{3,2,1,0:T(8,128)(2,1)S(1)}, u32[]{:S(2)}, u32[]{:S(2)}) collective-permute-start(bf16[2,2,104,512]{3,2,1,0:T(8,128)(2,1)S(1)} %get-tuple-element.24), channel_id=1, source_target_pairs={{0,4},{1,5},{2,6},{3,7},{4,8},{5,9},{6,10},{7,11},{8,12},{9,13},{1... | collective-permute-start | bytes 1277960 | tf_op jit(solution)/shard_map/ppermute | solution.py:360
  105.4 14.6 %collective-permute-start.25 = (bf16[2,2,104,512]{3,2,1,0:T(8,128)(2,1)S(1)}, bf16[2,2,104,512]{3,2,1,0:T(8,128)(2,1)S(1)}, u32[]{:S(2)}, u32[]{:S(2)}) collective-permute-start(bf16[2,2,104,512]{3,2,1,0:T(8,128)(2,1)S(1)} %collective-permute-done.24.refs_2_), channel_id=1, source_target_pairs={{16,0},{0,16},{17,1},{1,17},{18,2},{2,18},{19,3},{3,19},{20,4},{4,... | collective-permute-start | bytes 1277960 | tf_op jit(solution)/shard_map/ppermute | solution.py:363
  107.4 18.1 %collective-permute-start.27 = (bf16[2,2,104,512]{3,2,1,0:T(8,128)(2,1)S(1)}, bf16[2,2,104,512]{3,2,1,0:T(8,128)(2,1)S(1)}, u32[]{:S(2)}, u32[]{:S(2)}) collective-permute-start(bf16[2,2,104,512]{3,2,1,0:T(8,128)(2,1)S(1)} %collective-permute-done.26.refs_1_), channel_id=1, source_target_pairs={{16,0},{0,16},{17,1},{1,17},{18,2},{2,18},{19,3},{3,19},{20,4},{4,... | collective-permute-start | bytes 1277960 | tf_op jit(solution)/shard_map/ppermute | solution.py:363
  109.8 9.9 %collective-permute-start.15 = (bf16[224,512]{1,0:T(8,128)(2,1)S(1)}, bf16[224,512]{1,0:T(8,128)(2,1)S(1)}, u32[]{:S(2)}, u32[]{:S(2)}) collective-permute-start(bf16[224,512]{1,0:T(8,128)(2,1)S(1)} %get-tuple-element.23), channel_id=1, source_target_pairs={{0,2},{1,3},{2,0},{3,1},{4,6},{5,7},{6,4},{7,5},{8,10},{9,11},{10,... | collective-permute-start | bytes 688136 | tf_op jit(solution)/shard_map/ppermute | solution.py:375
  118.2 20.0 %collective-permute-start.29 = (bf16[2,2,104,512]{3,2,1,0:T(8,128)(2,1)S(1)}, bf16[2,2,104,512]{3,2,1,0:T(8,128)(2,1)S(1)}, u32[]{:S(2)}, u32[]{:S(2)}) collective-permute-start(bf16[2,2,104,512]{3,2,1,0:T(8,128)(2,1)S(1)} %collective-permute-done.23.refs_8_.refs_3_), channel_id=1, source_target_pairs={{16,0},{0,16},{17,1},{1,17},{18,2},{2,18},{19,3},{3,19},{20,4},{4,... | collective-permute-start | bytes 1277960 | tf_op jit(solution)/shard_map/ppermute | solution.py:363
  119.8 7.0 %collective-permute-start.17 = (bf16[104,512]{1,0:T(8,128)(2,1)S(1)}, bf16[104,512]{1,0:T(8,128)(2,1)S(1)}, u32[]{:S(2)}, u32[]{:S(2)}) collective-permute-start(bf16[104,512]{1,0:T(8,128)(2,1)S(1)} %shard_map.73.refs_0_), channel_id=1, source_target_pairs={{0,12},{1,13},{2,14},{3,15},{4,0},{5,1},{6,2},{7,3},{8,4},{9,5},{1... | collective-permute-start | bytes 319496 | tf_op jit(solution)/shard_map/ppermute | solution.py:379
  120.0 9.3 %collective-permute-start.19 = (bf16[104,512]{1,0:T(8,128)(2,1)S(1)}, bf16[104,512]{1,0:T(8,128)(2,1)S(1)}, u32[]{:S(2)}, u32[]{:S(2)}) collective-permute-start(bf16[104,512]{1,0:T(8,128)(2,1)S(1)} %shard_map.73.refs_0_), channel_id=1, source_target_pairs={{0,8},{1,9},{2,10},{3,11},{4,12},{5,13},{6,14},{7,15},{8,0},{9,1},... | collective-permute-start | bytes 319496 | tf_op jit(solution)/shard_map/ppermute | solution.py:379
  120.0 10.7 %collective-permute-start.21 = (bf16[104,512]{1,0:T(8,128)(2,1)S(1)}, bf16[104,512]{1,0:T(8,128)(2,1)S(1)}, u32[]{:S(2)}, u32[]{:S(2)}) collective-permute-start(bf16[104,512]{1,0:T(8,128)(2,1)S(1)} %shard_map.73.refs_0_), channel_id=1, source_target_pairs={{0,4},{1,5},{2,6},{3,7},{4,8},{5,9},{6,10},{7,11},{8,12},{9,13},{1... | collective-permute-start | bytes 319496 | tf_op jit(solution)/shard_map/ppermute | solution.py:379
  (10 other events, 73.1 us)

commit v7 on v6

--- a/solution.py
+++ b/solution.py
@@ -356,7 +356,7 @@
         ready = move(
             functools.partial(third_moves, range(planes)), [shape(2, 2, hid, part)] * planes, keep, came, across, after=()
         )
-        sums = product(spot, rows, blocks, own, near, far[0], cuts[0], after=(ready[0],))
+        sums = product(spot, rows, blocks, own, near, far[0], cuts[0], after=(across,))
         held = [lax.ppermute(h, "gx", shift(-k)) if k else h for k, h in enumerate(ready)]
         pieces = list(held)
         for r in range(1, share):
@@ -365,7 +365,7 @@
         crossed = pieces[planes:] if share > 1 else held
         one, two, three = held[1], held[2 % planes], held[-1]
         x0, x1, x2, x3 = crossed[0], crossed[1], crossed[2 % planes], crossed[-1]
-        later = [(), (), (three, x2, x1)]
+        later = [(two,), (x2,), (x1,)]
         keep, send = product(spot, rows, blocks, own, near, far[1], cuts[1], sums, total, after=(x0,))
         came = lax.ppermute(send, "gx", flip(1))
         mine, total, send = stage(

time: 146 us -> 145 us (level)
  transfers between devices with their start and end apart: 30 -> 30, of which waited for: 12 -> 13; matrix products, arithmetic and copies ran while one was open for 2% -> 2% of each run, Pallas kernels for 17% -> 17%
where the time goes in v7:
time: 145 us
  waiting for transfers between devices  66.5 us (46%)
  starting transfers between devices  43.1 us (30%)
  Pallas kernels  29 us (20%)
  other arithmetic  5.14 us (4%)
    ppermute x6, waiting for transfers between devices, body(): lax.ppermute(blocks[0] if s == 1 else blocks[-2], 'gx', line(s, way))  21.2 us
    ppermute x2, waiting for transfers between devices, body(): lax.ppermute(brought, 'groups', [(i, i ^ 1) for i in range(groups)])  14.6 us
    pallas_call x2, Pallas kernels, product(): pl.pallas_call(kernel, grid_spec=pltpu.PrefetchScalarGridSpec(num_scalar_...  13 us
    ppermute x6, starting transfers between devices, body(): lax.ppermute(blocks[0] if s == 1 else blocks[-2], 'gx', line(s, way))  11 us
    ppermute x2, waiting for transfers between devices, body(): brought = lax.ppermute(sends[0], ('groups', 'gx'), far_flip())  8.03 us
    ppermute x3, waiting for transfers between devices, body(): lax.ppermute(h, 'gx', shift(-k))  7.73 us
    ppermute x4, starting transfers between devices, body(): pieces += [lax.ppermute(h, 'groups', swap(r)) for h in held]  6.98 us
    pallas_call x3, Pallas kernels, cut(): pl.pallas_call(kernel, grid_spec=pltpu.PrefetchScalarGridSpec(num_scalar_...  6.91 us
  transfers between devices with their start and end apart: 30, of which 13 were waited for; matrix products, arithmetic and copies ran while one was open for 2% of the time, Pallas kernels for 17%

profile of v7, /device:TPU:1, one launch (start us, length us, event | category | flops | bytes accessed | tf_op | source)
XLA Modules:
  0.0 144.7 jit_solution(14208941225084835411)
XLA Ops:
  4.2 5.7 %collective-permute-start = (bf16[528,1024]{1,0:T(8,128)(2,1)}, bf16[528,1024]{1,0:T(8,128)(2,1)}, u32[]{:S(2)}, u32[]{:S(2)}) collective-permute-start(bf16[528,1024]{1,0:T(8,128)(2,1)} %fusion.3.refs_2_.refs_0_), channel_id=1, source_target_pairs={{0,4},{1,5},{2,6},{3,7},{4,8},{5,9},{6,10},{7,11},{8,12},{9,13},{1... | collective-permute-start | bytes 3244040 | tf_op jit(solution)/shard_map/ppermute | solution.py:303
  10.7 2.6 %shard_map.64.refs_1_ = bf16[3,2,104,1024]{3,2,1,0:T(8,128)(2,1)S(1)} custom-call(s32[11]{0:T(128)S(1)} %pad_add_fusion.spot, bf16[104,16384]{1,0:T(8,128)(2,1)S(1)} %bitcast.11, bf16[104,16384]{1,0:T(8,128)(2,1)} %bitcast.13, bf16[528,1024]{1,0:T(8,128)(2,1)} %fusion.3.refs_2_.refs_0_), custom_call_target="tpu_custom_call" | custom-call | bytes 12779520 | tf_op jit(solution)/shard_map/pallas_call | solution.py:234
  13.3 2.1 %shard_map.65 = (bf16[2,4,104,512]{3,2,1,0:T(8,128)(2,1)S(1)}, bf16[2,4,104,512]{3,2,1,0:T(8,128)(2,1)S(1)}) custom-call(bf16[104,16384]{1,0:T(8,128)(2,1)} %refs_0_.1, bf16[3,2,104,1024]{3,2,1,0:T(8,128)(2,1)S(1)} %shard_map.64.refs_1_), custom_call_target="tpu_custom_call" | custom-call | bytes 68157440 | tf_op jit(solution)/shard_map/pallas_call | solution.py:33
  18.1 12.7 %collective-permute-done.2.refs_2_ = bf16[528,1024]{1,0:T(8,128)(2,1)} collective-permute-done((bf16[528,1024]{1,0:T(8,128)(2,1)}, bf16[528,1024]{1,0:T(8,128)(2,1)}, u32[]{:S(2)}, u32[]{:S(2)}) %collective-permute-start.2) | collective-permute-done | bytes 1081376 | tf_op jit(solution)/shard_map/ppermute | solution.py:303
  32.9 2.7 %shard_map.67 = bf16[4,2,104,1024]{3,2,1,0:T(8,128)(2,1)S(1)} custom-call(s32[11]{0:T(128)S(1)} %pad_add_fusion.spot, bf16[104,16384]{1,0:T(8,128)(2,1)S(1)} %bitcast.12, bf16[104,16384]{1,0:T(8,128)(2,1)} %bitcast.14, bf16[2,4,104,512]{3,2,1,0:T(8,128)(2,1)S(1)} %shard_map.66.refs_2_), custom_call_target="tpu_custom_call" | custom-call | bytes 17039360 | tf_op jit(solution)/shard_map/pallas_call | solution.py:234
  38.3 8.0 %collective-permute-done.10.refs_8_ = bf16[3,2,104,1024]{3,2,1,0:T(8,128)(2,1)S(1)} collective-permute-done((bf16[3,2,104,1024]{3,2,1,0:T(8,128)(2,1)S(1)}, bf16[3,2,104,1024]{3,2,1,0:T(8,128)(2,1)S(1)}, u32[]{:S(2)}, u32[]{:S(2)}) %collective-permute-start.10) | collective-permute-done | bytes 1277984 | tf_op jit(solution)/shard_map/ppermute | solution.py:339
  46.4 2.3 %collective-permute-start.11 = (bf16[3,2,104,1024]{3,2,1,0:T(8,128)(2,1)S(1)}, bf16[3,2,104,1024]{3,2,1,0:T(8,128)(2,1)}, u32[]{:S(2)}, u32[]{:S(2)}) collective-permute-start(bf16[3,2,104,1024]{3,2,1,0:T(8,128)(2,1)S(1)} %collective-permute-done.10.refs_8_), channel_id=1, source_target_pairs={{0,16},{16,0},{1,17},{17,1},{2,18},{18,2},{3,19},{19,3},{4,20},{20... | collective-permute-start | bytes 3833864 | tf_op jit(solution)/shard_map/ppermute | solution.py:340
  48.7 8.4 %collective-permute-done.3.refs_4_.refs_1_ = bf16[528,1024]{1,0:T(8,128)(2,1)S(1)} collective-permute-done((bf16[528,1024]{1,0:T(8,128)(2,1)}, bf16[528,1024]{1,0:T(8,128)(2,1)S(1)}, u32[]{:S(2)}, u32[]{:S(2)}) %collective-permute-start.3) | collective-permute-done | bytes 1081376 | tf_op jit(solution)/shard_map/ppermute | solution.py:303
  60.6 4.2 %collective-permute-done.12.refs_10_.refs_2_ = bf16[2,4,104,512]{3,2,1,0:T(8,128)(2,1)S(1)} collective-permute-done((bf16[2,4,104,512]{3,2,1,0:T(8,128)(2,1)S(1)}, bf16[2,4,104,512]{3,2,1,0:T(8,128)(2,1)S(1)}, u32[]{:S(2)}, u32[]{:S(2)}) %collective-permute-start.12) | collective-permute-done | bytes 852000 | tf_op jit(solution)/shard_map/ppermute | solution.py:333
  69.8 7.0 %collective-permute-done.11.refs_9_ = bf16[3,2,104,1024]{3,2,1,0:T(8,128)(2,1)} collective-permute-done((bf16[3,2,104,1024]{3,2,1,0:T(8,128)(2,1)S(1)}, bf16[3,2,104,1024]{3,2,1,0:T(8,128)(2,1)}, u32[]{:S(2)}, u32[]{:S(2)}) %collective-permute-start.11) | collective-permute-done | bytes 1277984 | tf_op jit(solution)/shard_map/ppermute | solution.py:340
  76.8 2.1 %collective-permute-start.15 = (bf16[2,2,104,512]{3,2,1,0:T(8,128)(2,1)S(1)}, bf16[2,2,104,512]{3,2,1,0:T(8,128)(2,1)S(1)}, u32[]{:S(2)}, u32[]{:S(2)}) collective-permute-start(bf16[2,2,104,512]{3,2,1,0:T(8,128)(2,1)S(1)} %get-tuple-element.21), channel_id=1, source_target_pairs={{0,8},{1,9},{2,10},{3,11},{4,12},{5,13},{6,14},{7,15},{8,0},{9,1},... | collective-permute-start | bytes 1277960 | tf_op jit(solution)/shard_map/ppermute | solution.py:360
  78.9 8.2 %shard_map.69.refs_9_ = f32[832,512]{1,0:T(8,128)} custom-call(s32[11]{0:T(128)S(1)} %pad_add_fusion.spot, bf16[528,1024]{1,0:T(8,128)(2,1)} %fusion.3.refs_2_.refs_0_, bf16[528,1024]{1,0:T(8,128)(2,1)} %collective-permute-done.refs_1_, bf16[528,1024]{1,0:T(8,128)(2,1)} %collective-permute-done.2.refs_2_, ...), custom_call_target="tpu_custom_call" | custom-call | flops 2617245696 | bytes 5111808 | tf_op jit(solution)/shard_map/pallas_call | solution.py:201
  87.2 2.3 %collective-permute-start.9 = (bf16[1,2,104,1024]{3,2,1,0:T(8,128)(2,1)S(1)}, bf16[1,2,104,1024]{3,2,1,0:T(8,128)(2,1)S(1)}, u32[]{:S(2)}, u32[]{:S(2)}) collective-permute-start(bf16[1,2,104,1024]{3,2,1,0:T(8,128)(2,1)S(1)} %collective-permute-done.8.refs_7_), channel_id=1, source_target_pairs={{0,16},{16,0},{1,17},{17,1},{2,18},{18,2},{3,19},{19,3},{4,20},{20... | collective-permute-start | bytes 1277960 | tf_op jit(solution)/shard_map/ppermute | solution.py:340
  90.2 7.6 %collective-permute-done.9.refs_8_ = bf16[1,2,104,1024]{3,2,1,0:T(8,128)(2,1)S(1)} collective-permute-done((bf16[1,2,104,1024]{3,2,1,0:T(8,128)(2,1)S(1)}, bf16[1,2,104,1024]{3,2,1,0:T(8,128)(2,1)S(1)}, u32[]{:S(2)}, u32[]{:S(2)}) %collective-permute-start.9) | collective-permute-done | bytes 426016 | tf_op jit(solution)/shard_map/ppermute | solution.py:340
  97.9 4.8 %shard_map.71 = (f32[416,512]{1,0:T(8,128)S(1)}, bf16[432,512]{1,0:T(8,128)(2,1)S(1)}) custom-call(s32[11]{0:T(128)S(1)} %pad_add_fusion.spot, bf16[528,1024]{1,0:T(8,128)(2,1)S(1)} %collective-permute-done.1.refs_3_.refs_0_, bf16[528,1024]{1,0:T(8,128)(2,1)S(1)} %copy-done.2, bf16[528,1024]{1,0:T(8,128)(2,1)S(1)} %collective-permute-done.4.refs_2_, ...), custom_call_target="tpu_custom_call" | custom-call | flops 4362076160 | bytes 8519680 | tf_op jit(solution)/shard_map/pallas_call | solution.py:201
  102.6 2.4 %collective-permute-start.14 = (bf16[432,512]{1,0:T(8,128)(2,1)S(1)}, bf16[432,512]{1,0:T(8,128)(2,1)S(1)}, u32[]{:S(2)}, u32[]{:S(2)}) collective-permute-start(bf16[432,512]{1,0:T(8,128)(2,1)S(1)} %get-tuple-element.20), channel_id=1, source_target_pairs={{0,1},{1,0},{2,3},{3,2},{4,5},{5,4},{6,7},{7,6},{8,9},{9,8},{10,11... | collective-permute-start | bytes 1327112 | tf_op jit(solution)/shard_map/ppermute | solution.py:370
  107.4 2.2 %collective-permute-start.26 = (bf16[2,2,104,512]{3,2,1,0:T(8,128)(2,1)S(1)}, bf16[2,2,104,512]{3,2,1,0:T(8,128)(2,1)S(1)}, u32[]{:S(2)}, u32[]{:S(2)}) collective-permute-start(bf16[2,2,104,512]{3,2,1,0:T(8,128)(2,1)S(1)} %collective-permute-done.25.refs_1_), channel_id=1, source_target_pairs={{16,0},{0,16},{17,1},{1,17},{18,2},{2,18},{19,3},{3,19},{20,4},{4,... | collective-permute-start | bytes 1277960 | tf_op jit(solution)/shard_map/ppermute | solution.py:363
  111.1 7.2 %collective-permute-done.28.refs_3_ = bf16[2,2,104,512]{3,2,1,0:T(8,128)(2,1)S(1)} collective-permute-done((bf16[2,2,104,512]{3,2,1,0:T(8,128)(2,1)S(1)}, bf16[2,2,104,512]{3,2,1,0:T(8,128)(2,1)S(1)}, u32[]{:S(2)}, u32[]{:S(2)}) %collective-permute-start.28) | collective-permute-done | bytes 426016 | tf_op jit(solution)/shard_map/ppermute | solution.py:360
  121.4 4.2 %collective-permute-done.26.refs_8_.refs_5_ = bf16[2,2,104,512]{3,2,1,0:T(8,128)(2,1)S(1)} collective-permute-done((bf16[2,2,104,512]{3,2,1,0:T(8,128)(2,1)S(1)}, bf16[2,2,104,512]{3,2,1,0:T(8,128)(2,1)S(1)}, u32[]{:S(2)}, u32[]{:S(2)}) %collective-permute-start.26) | collective-permute-done | bytes 426016 | tf_op jit(solution)/shard_map/ppermute | solution.py:363
  130.7 2.2 %collective-permute-done.22.refs_5_ = bf16[104,512]{1,0:T(8,128)(2,1)S(1)} collective-permute-done((bf16[104,512]{1,0:T(8,128)(2,1)S(1)}, bf16[104,512]{1,0:T(8,128)(2,1)S(1)}, u32[]{:S(2)}, u32[]{:S(2)}) %collective-permute-start.22) | collective-permute-done | bytes 106528 | tf_op jit(solution)/shard_map/ppermute | solution.py:382
  132.9 2.3 %collective-permute-done.24.refs_7_ = bf16[104,512]{1,0:T(8,128)(2,1)S(1)} collective-permute-done((bf16[104,512]{1,0:T(8,128)(2,1)S(1)}, bf16[104,512]{1,0:T(8,128)(2,1)S(1)}, u32[]{:S(2)}, u32[]{:S(2)}) %collective-permute-start.24) | collective-permute-done | bytes 106528 | tf_op jit(solution)/shard_map/ppermute | solution.py:382
  135.3 2.8 %collective-permute-start.27 = (bf16[4,2,104,512]{3,2,1,0:T(8,128)(2,1)S(1)}, bf16[4,2,104,512]{3,2,1,0:T(8,128)(2,1)S(1)}, u32[]{:S(2)}, u32[]{:S(2)}) collective-permute-start(bf16[4,2,104,512]{3,2,1,0:T(8,128)(2,1)S(1)} %shard_map.74.side), channel_id=1, source_target_pairs={{0,1},{1,0},{2,3},{3,2},{4,5},{5,4},{6,7},{7,6},{8,9},{9,8},{10,11... | collective-permute-start | bytes 2555912 | tf_op jit(solution)/shard_map/ppermute | solution.py:389
  138.1 2.6 %shard_map.75.refs_8_ = f32[2,512,512]{2,1,0:T(8,128)} custom-call(bf16[4,2,104,512]{3,2,1,0:T(8,128)(2,1)S(1)} %shard_map.74.side, bf16[2,2,104,512]{3,2,1,0:T(8,128)(2,1)S(1)} %get-tuple-element.18.refs_0_, bf16[2,2,104,512]{3,2,1,0:T(8,128)(2,1)S(1)} %collective-permute-done.25.refs_1_, ...), custom_call_target="tpu_custom_call" | custom-call | flops 17448304640 | bytes 51118080 | tf_op jit(solution)/shard_map/pallas_call | solution.py:273
  140.7 3.9 %shard_map.76 = bf16[512,1024]{1,0:T(8,128)(2,1)} custom-call(bf16[4,2,104,512]{3,2,1,0:T(8,128)(2,1)S(1)} %collective-permute-done.27.side, bf16[2,2,104,512]{3,2,1,0:T(8,128)(2,1)S(1)} %get-tuple-element.18.refs_0_, bf16[2,2,104,512]{3,2,1,0:T(8,128)(2,1)S(1)} %collective-permute-done.25.refs_1_, ...), custom_call_target="tpu_custom_call" | custom-call | flops 17448304640 | bytes 51118080 | tf_op jit(solution)/shard_map/pallas_call | solution.py:273
  (72 shorter events, 33.7 us)
Async XLA Ops:
  2.9 27.9 %collective-permute-start.2 = (bf16[528,1024]{1,0:T(8,128)(2,1)}, bf16[528,1024]{1,0:T(8,128)(2,1)}, u32[]{:S(2)}, u32[]{:S(2)}) collective-permute-start(bf16[528,1024]{1,0:T(8,128)(2,1)} %fusion.3.refs_2_.refs_0_), channel_id=1, source_target_pairs={{4,0},{5,1},{6,2},{7,3},{8,4},{9,5},{10,6},{11,7},{12,8},{13,9},{1... | collective-permute-start | bytes 3244040 | tf_op jit(solution)/shard_map/ppermute | solution.py:303
  4.2 27.9 %collective-permute-start = (bf16[528,1024]{1,0:T(8,128)(2,1)}, bf16[528,1024]{1,0:T(8,128)(2,1)}, u32[]{:S(2)}, u32[]{:S(2)}) collective-permute-start(bf16[528,1024]{1,0:T(8,128)(2,1)} %fusion.3.refs_2_.refs_0_), channel_id=1, source_target_pairs={{0,4},{1,5},{2,6},{3,7},{4,8},{5,9},{6,10},{7,11},{8,12},{9,13},{1... | collective-permute-start | bytes 3244040 | tf_op jit(solution)/shard_map/ppermute | solution.py:303
  15.4 17.5 %collective-permute-start.6 = (bf16[2,4,104,512]{3,2,1,0:T(8,128)(2,1)S(1)}, bf16[2,4,104,512]{3,2,1,0:T(8,128)(2,1)S(1)}, u32[]{:S(2)}, u32[]{:S(2)}) collective-permute-start(bf16[2,4,104,512]{3,2,1,0:T(8,128)(2,1)S(1)} %get-tuple-element.17), channel_id=1, source_target_pairs={{0,1},{1,0},{2,3},{3,2},{4,5},{5,4},{6,7},{7,6},{8,9},{9,8},{10,11... | collective-permute-start | bytes 2555912 | tf_op jit(solution)/shard_map/ppermute | solution.py:326
  16.4 30.0 %collective-permute-start.10 = (bf16[3,2,104,1024]{3,2,1,0:T(8,128)(2,1)S(1)}, bf16[3,2,104,1024]{3,2,1,0:T(8,128)(2,1)S(1)}, u32[]{:S(2)}, u32[]{:S(2)}) collective-permute-start(bf16[3,2,104,1024]{3,2,1,0:T(8,128)(2,1)S(1)} %shard_map.64.refs_1_), channel_id=1, source_target_pairs={{0,2},{1,3},{2,0},{3,1},{4,6},{5,7},{6,4},{7,5},{8,10},{9,11},{10,... | collective-permute-start | bytes 3833864 | tf_op jit(solution)/shard_map/ppermute | solution.py:339
  30.8 26.3 %collective-permute-start.3 = (bf16[528,1024]{1,0:T(8,128)(2,1)}, bf16[528,1024]{1,0:T(8,128)(2,1)S(1)}, u32[]{:S(2)}, u32[]{:S(2)}) collective-permute-start(bf16[528,1024]{1,0:T(8,128)(2,1)} %collective-permute-done.2.refs_2_), channel_id=1, source_target_pairs={{4,0},{5,1},{6,2},{7,3},{8,4},{9,5},{10,6},{11,7},{20,16},{21,17},... | collective-permute-start | bytes 3244040 | tf_op jit(solution)/shard_map/ppermute | solution.py:303
  32.1 27.0 %collective-permute-start.1 = (bf16[528,1024]{1,0:T(8,128)(2,1)}, bf16[528,1024]{1,0:T(8,128)(2,1)S(1)}, u32[]{:S(2)}, u32[]{:S(2)}) collective-permute-start(bf16[528,1024]{1,0:T(8,128)(2,1)} %collective-permute-done.refs_1_), channel_id=1, source_target_pairs={{4,8},{5,9},{6,10},{7,11},{8,12},{9,13},{10,14},{11,15},{20,24},{2... | collective-permute-start | bytes 3244040 | tf_op jit(solution)/shard_map/ppermute | solution.py:303
  35.6 32.3 %collective-permute-start.7 = (bf16[4,2,104,1024]{3,2,1,0:T(8,128)(2,1)S(1)}, bf16[4,2,104,1024]{3,2,1,0:T(8,128)(2,1)S(1)}, u32[]{:S(2)}, u32[]{:S(2)}) collective-permute-start(bf16[4,2,104,1024]{3,2,1,0:T(8,128)(2,1)S(1)} %shard_map.67), channel_id=1, source_target_pairs={{0,1},{1,0},{2,3},{3,2},{4,5},{5,4},{6,7},{7,6},{8,9},{9,8},{10,11... | collective-permute-start | bytes 5111816 | tf_op jit(solution)/shard_map/ppermute | solution.py:343
  36.9 27.8 %collective-permute-start.12 = (bf16[2,4,104,512]{3,2,1,0:T(8,128)(2,1)S(1)}, bf16[2,4,104,512]{3,2,1,0:T(8,128)(2,1)S(1)}, u32[]{:S(2)}, u32[]{:S(2)}) collective-permute-start(bf16[2,4,104,512]{3,2,1,0:T(8,128)(2,1)S(1)} %shard_map.66.refs_2_), channel_id=1, source_target_pairs={{0,2},{1,3},{2,0},{3,1},{4,6},{5,7},{6,4},{7,5},{8,10},{9,11},{10,... | collective-permute-start | bytes 2555912 | tf_op jit(solution)/shard_map/ppermute | solution.py:333
  46.4 30.4 %collective-permute-start.11 = (bf16[3,2,104,1024]{3,2,1,0:T(8,128)(2,1)S(1)}, bf16[3,2,104,1024]{3,2,1,0:T(8,128)(2,1)}, u32[]{:S(2)}, u32[]{:S(2)}) collective-permute-start(bf16[3,2,104,1024]{3,2,1,0:T(8,128)(2,1)S(1)} %collective-permute-done.10.refs_8_), channel_id=1, source_target_pairs={{0,16},{16,0},{1,17},{17,1},{2,18},{18,2},{3,19},{19,3},{4,20},{20... | collective-permute-start | bytes 3833864 | tf_op jit(solution)/shard_map/ppermute | solution.py:340
  57.1 30.1 %collective-permute-start.5 = (bf16[528,1024]{1,0:T(8,128)(2,1)S(1)}, bf16[528,1024]{1,0:T(8,128)(2,1)}, u32[]{:S(2)}, u32[]{:S(2)}) collective-permute-start(bf16[528,1024]{1,0:T(8,128)(2,1)S(1)} %collective-permute-done.3.refs_4_.refs_1_), channel_id=1, source_target_pairs={{4,0},{5,1},{6,2},{7,3},{20,16},{21,17},{22,18},{23,19}} | collective-permute-start | bytes 3244040 | tf_op jit(solution)/shard_map/ppermute | solution.py:303
  59.1 31.1 %collective-permute-start.4 = (bf16[528,1024]{1,0:T(8,128)(2,1)S(1)}, bf16[528,1024]{1,0:T(8,128)(2,1)S(1)}, u32[]{:S(2)}, u32[]{:S(2)}) collective-permute-start(bf16[528,1024]{1,0:T(8,128)(2,1)S(1)} %collective-permute-done.1.refs_3_.refs_0_), channel_id=1, source_target_pairs={{8,12},{9,13},{10,14},{11,15},{24,28},{25,29},{26,30},{27,31}} | collective-permute-start | bytes 3244040 | tf_op jit(solution)/shard_map/ppermute | solution.py:303
  66.5 20.6 %collective-permute-start.8 = (bf16[1,2,104,1024]{3,2,1,0:T(8,128)(2,1)S(1)}, bf16[1,2,104,1024]{3,2,1,0:T(8,128)(2,1)S(1)}, u32[]{:S(2)}, u32[]{:S(2)}) collective-permute-start(bf16[1,2,104,1024]{3,2,1,0:T(8,128)(2,1)S(1)} %shard_map.68), channel_id=1, source_target_pairs={{0,2},{1,3},{2,0},{3,1},{4,6},{5,7},{6,4},{7,5},{8,10},{9,11},{10,... | collective-permute-start | bytes 1277960 | tf_op jit(solution)/shard_map/ppermute | solution.py:339
  67.9 22.3 %collective-permute-start.13 = (bf16[2,2,104,512]{3,2,1,0:T(8,128)(2,1)S(1)}, bf16[2,2,104,512]{3,2,1,0:T(8,128)(2,1)S(1)}, u32[]{:S(2)}, u32[]{:S(2)}) collective-permute-start(bf16[2,2,104,512]{3,2,1,0:T(8,128)(2,1)S(1)} %get-tuple-element.18.refs_0_), channel_id=1, source_target_pairs={{16,0},{0,16},{17,1},{1,17},{18,2},{2,18},{19,3},{3,19},{20,4},{4,... | collective-permute-start | bytes 1277960 | tf_op jit(solution)/shard_map/ppermute | solution.py:363
  76.8 28.7 %collective-permute-start.15 = (bf16[2,2,104,512]{3,2,1,0:T(8,128)(2,1)S(1)}, bf16[2,2,104,512]{3,2,1,0:T(8,128)(2,1)S(1)}, u32[]{:S(2)}, u32[]{:S(2)}) collective-permute-start(bf16[2,2,104,512]{3,2,1,0:T(8,128)(2,1)S(1)} %get-tuple-element.21), channel_id=1, source_target_pairs={{0,8},{1,9},{2,10},{3,11},{4,12},{5,13},{6,14},{7,15},{8,0},{9,1},... | collective-permute-start | bytes 1277960 | tf_op jit(solution)/shard_map/ppermute | solution.py:360
  87.1 20.3 %collective-permute-start.25 = (bf16[2,2,104,512]{3,2,1,0:T(8,128)(2,1)S(1)}, bf16[2,2,104,512]{3,2,1,0:T(8,128)(2,1)S(1)}, u32[]{:S(2)}, u32[]{:S(2)}) collective-permute-start(bf16[2,2,104,512]{3,2,1,0:T(8,128)(2,1)S(1)} %get-tuple-element.25), channel_id=1, source_target_pairs={{0,12},{1,13},{2,14},{3,15},{4,0},{5,1},{6,2},{7,3},{8,4},{9,5},{1... | collective-permute-start | bytes 1277960 | tf_op jit(solution)/shard_map/ppermute | solution.py:360
  87.2 10.7 %collective-permute-start.9 = (bf16[1,2,104,1024]{3,2,1,0:T(8,128)(2,1)S(1)}, bf16[1,2,104,1024]{3,2,1,0:T(8,128)(2,1)S(1)}, u32[]{:S(2)}, u32[]{:S(2)}) collective-permute-start(bf16[1,2,104,1024]{3,2,1,0:T(8,128)(2,1)S(1)} %collective-permute-done.8.refs_7_), channel_id=1, source_target_pairs={{0,16},{16,0},{1,17},{17,1},{2,18},{18,2},{3,19},{19,3},{4,20},{20... | collective-permute-start | bytes 1277960 | tf_op jit(solution)/shard_map/ppermute | solution.py:340
  102.6 7.0 %collective-permute-start.14 = (bf16[432,512]{1,0:T(8,128)(2,1)S(1)}, bf16[432,512]{1,0:T(8,128)(2,1)S(1)}, u32[]{:S(2)}, u32[]{:S(2)}) collective-permute-start(bf16[432,512]{1,0:T(8,128)(2,1)S(1)} %get-tuple-element.20), channel_id=1, source_target_pairs={{0,1},{1,0},{2,3},{3,2},{4,5},{5,4},{6,7},{7,6},{8,9},{9,8},{10,11... | collective-permute-start | bytes 1327112 | tf_op jit(solution)/shard_map/ppermute | solution.py:370
  105.1 13.2 %collective-permute-start.28 = (bf16[2,2,104,512]{3,2,1,0:T(8,128)(2,1)S(1)}, bf16[2,2,104,512]{3,2,1,0:T(8,128)(2,1)S(1)}, u32[]{:S(2)}, u32[]{:S(2)}) collective-permute-start(bf16[2,2,104,512]{3,2,1,0:T(8,128)(2,1)S(1)} %get-tuple-element.26), channel_id=1, source_target_pairs={{0,4},{1,5},{2,6},{3,7},{4,8},{5,9},{6,10},{7,11},{8,12},{9,13},{1... | collective-permute-start | bytes 1277960 | tf_op jit(solution)/shard_map/ppermute | solution.py:360
  105.4 14.3 %collective-permute-start.17 = (bf16[2,2,104,512]{3,2,1,0:T(8,128)(2,1)S(1)}, bf16[2,2,104,512]{3,2,1,0:T(8,128)(2,1)S(1)}, u32[]{:S(2)}, u32[]{:S(2)}) collective-permute-start(bf16[2,2,104,512]{3,2,1,0:T(8,128)(2,1)S(1)} %collective-permute-done.15.refs_3_.refs_2_), channel_id=1, source_target_pairs={{16,0},{0,16},{17,1},{1,17},{18,2},{2,18},{19,3},{3,19},{20,4},{4,... | collective-permute-start | bytes 1277960 | tf_op jit(solution)/shard_map/ppermute | solution.py:363
  107.4 18.2 %collective-permute-start.26 = (bf16[2,2,104,512]{3,2,1,0:T(8,128)(2,1)S(1)}, bf16[2,2,104,512]{3,2,1,0:T(8,128)(2,1)S(1)}, u32[]{:S(2)}, u32[]{:S(2)}) collective-permute-start(bf16[2,2,104,512]{3,2,1,0:T(8,128)(2,1)S(1)} %collective-permute-done.25.refs_1_), channel_id=1, source_target_pairs={{16,0},{0,16},{17,1},{1,17},{18,2},{2,18},{19,3},{3,19},{20,4},{4,... | collective-permute-start | bytes 1277960 | tf_op jit(solution)/shard_map/ppermute | solution.py:363
  109.7 10.0 %collective-permute-start.16 = (bf16[224,512]{1,0:T(8,128)(2,1)S(1)}, bf16[224,512]{1,0:T(8,128)(2,1)S(1)}, u32[]{:S(2)}, u32[]{:S(2)}) collective-permute-start(bf16[224,512]{1,0:T(8,128)(2,1)S(1)} %get-tuple-element.24), channel_id=1, source_target_pairs={{0,2},{1,3},{2,0},{3,1},{4,6},{5,7},{6,4},{7,5},{8,10},{9,11},{10,... | collective-permute-start | bytes 688136 | tf_op jit(solution)/shard_map/ppermute | solution.py:375
  118.3 19.8 %collective-permute-start.29 = (bf16[2,2,104,512]{3,2,1,0:T(8,128)(2,1)S(1)}, bf16[2,2,104,512]{3,2,1,0:T(8,128)(2,1)S(1)}, u32[]{:S(2)}, u32[]{:S(2)}) collective-permute-start(bf16[2,2,104,512]{3,2,1,0:T(8,128)(2,1)S(1)} %collective-permute-done.28.refs_3_), channel_id=1, source_target_pairs={{16,0},{0,16},{17,1},{1,17},{18,2},{2,18},{19,3},{3,19},{20,4},{4,... | collective-permute-start | bytes 1277960 | tf_op jit(solution)/shard_map/ppermute | solution.py:363
  119.9 7.0 %collective-permute-start.19 = (bf16[104,512]{1,0:T(8,128)(2,1)S(1)}, bf16[104,512]{1,0:T(8,128)(2,1)S(1)}, u32[]{:S(2)}, u32[]{:S(2)}) collective-permute-start(bf16[104,512]{1,0:T(8,128)(2,1)S(1)} %shard_map.73.refs_0_), channel_id=1, source_target_pairs={{0,12},{1,13},{2,14},{3,15},{4,0},{5,1},{6,2},{7,3},{8,4},{9,5},{1... | collective-permute-start | bytes 319496 | tf_op jit(solution)/shard_map/ppermute | solution.py:379
  120.2 9.0 %collective-permute-start.23 = (bf16[104,512]{1,0:T(8,128)(2,1)S(1)}, bf16[104,512]{1,0:T(8,128)(2,1)S(1)}, u32[]{:S(2)}, u32[]{:S(2)}) collective-permute-start(bf16[104,512]{1,0:T(8,128)(2,1)S(1)} %shard_map.73.refs_0_), channel_id=1, source_target_pairs={{0,4},{1,5},{2,6},{3,7},{4,8},{5,9},{6,10},{7,11},{8,12},{9,13},{1... | collective-permute-start | bytes 319496 | tf_op jit(solution)/shard_map/ppermute | solution.py:379
  (11 other events, 103.9 us)
